TPU v7x, 32 devices: a whole 2x2x4 slice. The times are simulated.
32 devices in a mesh: gx: 8 (over z, y), gy: 4 (over x, core).
Axes of the slice: x: 2, y: 2, z: 4, core: 2. Of those that a mesh axis runs over, the one named last changes fastest.
Arguments:
- ocean_fields: bfloat16 [2048, 8, 512], P(('gx', 'gy')), may hold values from -6 to 6
- dest_device: int32 [2048, 2], P(('gx', 'gy')), may hold values from 0 to 31, all different within a row; in each aligned block of 64 rows (0 to 63, 64 to 127, ...) at most 8 rows name the same one
- dest_tile: int32 [2048, 2], P(('gx', 'gy')), may hold values from 0 to 7
- cell_target: int32 [2048, 2, 512], P(('gx', 'gy')), may hold values from 0 to 1023
- cell_weight: bfloat16 [2048, 2, 512], P(('gx', 'gy')), may hold values from 0.049804688 to 1
- sea_mask: int32 [2048, 512], P(('gx', 'gy')), may hold values 0 or 1
- land_flux: float32 [8, 256, 1024], P(None, 'gy', 'gx'), may hold values from -6 to 6
- land_area: float32 [256, 1024], P('gy', 'gx'), may hold values from 0.5 to 8
- kappa: float32 [256, 1024], P('gy', 'gx'), may hold values from 0.02 to 0.24
Outputs:
- smoothed: float32 [8, 256, 1024], P(None, 'gy', 'gx')
Inputs may be any that keep to these rules, and one draw needn't show every extreme that they name: `dest_device`: the 2 devices named by one ocean tile differ; among the 64 ocean tiles of one device at most 8 name the same device.
All inputs are finite; a program needn't handle non-finite values. No bound on the sum of `sea_mask` on one device may be relied on, other than what follows from the above.
Results may differ from a plain program's by a relative error of at most 0.0003.
Values may be sent and summed in bfloat16 or wider, within the bound.
No kernel may reach another device: no remote copies, remote signals or barrier semaphores. Data moves between devices by JAX's collectives and lax.ppermute only.
A program may use at most 64 MiB of HBM per device.

v0:
```python
import jax
import jax.numpy as jnp
from jax import lax
from jax.sharding import PartitionSpec as P

TILE_ROWS = 8
ATM_COLS = 128
SWEEPS = 3


def with_halo(cells, sides, width):
    for axis, dim in sides:
        count = lax.axis_size(axis)
        ends = count - 1
        head = lax.slice_in_dim(cells, 0, width, axis=dim)
        tail = lax.slice_in_dim(cells, cells.shape[dim] - width, cells.shape[dim], axis=dim)
        cells = jnp.concatenate(
            [
                lax.ppermute(tail, axis, [(i, (i + 1) % count) for i in range(ends)]),
                cells,
                lax.ppermute(head, axis, [((i + 1) % count, i) for i in range(ends)]),
            ],
            axis=dim,
        )
    return cells


def sweep_valid(padded, kpad):
    center = padded[:, 1:-1, 1:-1]
    kcenter = kpad[1:-1, 1:-1]
    result = center
    for near, knear in (
        (padded[:, 2:, 1:-1], kpad[2:, 1:-1]),
        (padded[:, :-2, 1:-1], kpad[:-2, 1:-1]),
        (padded[:, 1:-1, 2:], kpad[1:-1, 2:]),
        (padded[:, 1:-1, :-2], kpad[1:-1, :-2]),
    ):
        result = result + 0.5 * (kcenter + knear)[None] * (near - center)
    return result


def shards(
    ocean_fields,
    dest_device,
    dest_tile,
    cell_target,
    cell_weight,
    sea_mask,
    land_flux,
    land_area,
    kappa,
):
    tiles_here, field_count, tile_cells = ocean_fields.shape
    crossing_count = dest_device.shape[1]
    width_x = lax.axis_size("gx")
    width_y = lax.axis_size("gy")
    device_count = width_x * width_y
    pair_count = tiles_here * crossing_count
    capacity = max(2, pair_count * 2 // device_count)
    slot_count = device_count * capacity
    rows_here, cols_here = land_area.shape
    tiles_atm = rows_here // TILE_ROWS
    dest_flat = dest_device.reshape(pair_count)
    peer_hot = (dest_flat[:, None] == jnp.arange(device_count, dtype=jnp.int32)[None, :]).astype(
        jnp.int32
    )
    within = jnp.sum((jnp.cumsum(peer_hot, axis=0) - 1) * peer_hot, axis=1)
    position = dest_flat * capacity + within
    pair_fields = jnp.broadcast_to(
        ocean_fields[:, None], (tiles_here, crossing_count, field_count, tile_cells)
    ).reshape(pair_count, field_count, tile_cells)
    weighted = (cell_weight * sea_mask[:, None, :].astype(jnp.bfloat16)).reshape(
        pair_count, tile_cells
    )
    targets = cell_target.reshape(pair_count, tile_cells)
    tile_ids = dest_tile.reshape(pair_count)
    send_fields = (
        jnp.zeros((slot_count, field_count, tile_cells), jnp.bfloat16).at[position].set(pair_fields)
    )
    send_weights = jnp.zeros((slot_count, tile_cells), jnp.bfloat16).at[position].set(weighted)
    send_targets = jnp.zeros((slot_count, tile_cells), jnp.int32).at[position].set(targets)
    send_tiles = jnp.zeros((slot_count,), jnp.int32).at[position].set(tile_ids)
    got_fields, got_weights, got_targets, got_tiles = (
        lax.all_to_all(
            send_fields.reshape(device_count, capacity, field_count, tile_cells),
            ("gx", "gy"),
            split_axis=0,
            concat_axis=0,
            tiled=True,
        ),
        lax.all_to_all(
            send_weights.reshape(device_count, capacity, tile_cells),
            ("gx", "gy"),
            split_axis=0,
            concat_axis=0,
            tiled=True,
        ),
        lax.all_to_all(
            send_targets.reshape(device_count, capacity, tile_cells),
            ("gx", "gy"),
            split_axis=0,
            concat_axis=0,
            tiled=True,
        ),
        lax.all_to_all(
            send_tiles.reshape(device_count, capacity),
            ("gx", "gy"),
            split_axis=0,
            concat_axis=0,
            tiled=True,
        ),
    )
    group = min(32, slot_count)
    turns = slot_count // group
    batched = (
        got_fields.reshape(turns, group, field_count, tile_cells),
        got_weights.reshape(turns, group, tile_cells),
        got_targets.reshape(turns, group, tile_cells),
        got_tiles.reshape(turns, group),
    )
    row_iota = jnp.arange(TILE_ROWS, dtype=jnp.int32)
    col_iota = jnp.arange(ATM_COLS, dtype=jnp.int32)
    tile_iota = jnp.arange(tiles_atm, dtype=jnp.int32)

    def accumulate(total, items):
        fields_in, weights_in, targets_in, tiles_in = items
        ones_row = jnp.ones((group, 1, tile_cells), jnp.bfloat16)
        stacked = jnp.concatenate([fields_in, ones_row], axis=1)
        row_hot = (targets_in[:, None, :] // ATM_COLS == row_iota[None, :, None]).astype(
            jnp.bfloat16
        )
        left_side = (stacked[:, :, None, :] * row_hot[:, None, :, :]).reshape(
            group, (field_count + 1) * TILE_ROWS, tile_cells
        )
        right_side = jnp.where(
            targets_in[:, :, None] % ATM_COLS == col_iota[None, None, :],
            weights_in[:, :, None],
            jnp.zeros((), jnp.bfloat16),
        )
        contrib = jnp.einsum(
            "gmc,gcx->gmx", left_side, right_side, preferred_element_type=jnp.float32
        )
        tile_hot = (tiles_in[:, None] == tile_iota[None, :]).astype(jnp.float32)
        added = jnp.einsum("gt,gmx->tmx", tile_hot, contrib, precision=lax.Precision.HIGHEST)
        return (total + added, None)

    start_total = jnp.zeros((tiles_atm, (field_count + 1) * TILE_ROWS, cols_here), jnp.float32)
    totals, unused = lax.scan(accumulate, start_total, batched)
    totals = jnp.transpose(
        totals.reshape(tiles_atm, field_count + 1, TILE_ROWS, cols_here), (1, 0, 2, 3)
    ).reshape(field_count + 1, rows_here, cols_here)
    numer = totals[:field_count]
    denom = totals[field_count]
    field = (numer + land_area[None] * land_flux) / (denom + land_area)[None]
    kpad = with_halo(kappa, (("gx", 1), ("gy", 0)), 1)
    for sweep_index in range(SWEEPS):
        padded = with_halo(field, (("gx", 2), ("gy", 1)), 1)
        field = sweep_valid(padded, kpad)
    return field


def solution(mesh):
    return jax.shard_map(
        shards,
        mesh=mesh,
        in_specs=(
            P(("gx", "gy"), None, None),
            P(("gx", "gy"), None),
            P(("gx", "gy"), None),
            P(("gx", "gy"), None, None),
            P(("gx", "gy"), None, None),
            P(("gx", "gy"), None),
            P(None, "gy", "gx"),
            P("gy", "gx"),
            P("gy", "gx"),
        ),
        out_specs=P(None, "gy", "gx"),
        check_vma=False,
    )
```

profile of v0, /device:TPU:21, one launch (start us, length us, event | category | flops | bytes accessed | tf_op | source)
XLA Modules:
  0.0 276.7 jit_solution(16760887192060477348)
XLA Ops:
  5.0 6.2 %all-to-all-start = ((s32[32,1,8]{2,1,0:T(1,128)}), s32[32,1,8]{2,1,0:T(1,128)S(1)}, u32[]{:S(2)}, u32[]{:S(2)}) async-start(s32[32,1,8]{2,1,0:T(1,128)} %bitcast.2), calls=%async_computation | async-start | bytes 32768 | tf_op jit(solution)/shard_map/all_to_all | solution.py:105
  15.0 5.9 %all-to-all-start.3 = ((bf16[32,8,512]{2,1,0:T(8,128)(2,1)}), bf16[32,8,512]{2,1,0:T(8,128)(2,1)S(1)}, u32[]{:S(2)}, u32[]{:S(2)}) async-start(bf16[32,8,512]{2,1,0:T(8,128)(2,1)} %bitcast.8), calls=%async_computation.3 | async-start | bytes 524288 | tf_op jit(solution)/shard_map/all_to_all | solution.py:91
  22.9 5.0 %all-to-all-done.3 = bf16[32,8,512]{2,1,0:T(8,128)(2,1)S(1)} async-done(((bf16[32,8,512]{2,1,0:T(8,128)(2,1)}), bf16[32,8,512]{2,1,0:T(8,128)(2,1)S(1)}, u32[]{:S(2)}, u32[]{:S(2)}) %all-to-all-start.3) | async-done | bytes 262176 | tf_op jit(solution)/shard_map/all_to_all | solution.py:91
  27.9 6.2 %all-to-all-start.2 = ((s32[32,8,512]{2,1,0:T(8,128)}), s32[32,8,512]{2,1,0:T(8,128)S(1)}, u32[]{:S(2)}, u32[]{:S(2)}) async-start(s32[32,8,512]{2,1,0:T(8,128)} %bitcast.6), calls=%async_computation.2 | async-start | bytes 1048576 | tf_op jit(solution)/shard_map/all_to_all | solution.py:98
  35.6 13.7 %scatter_fusion = bf16[256,8,512]{2,1,0:T(8,128)(2,1)} fusion(bf16[256,8,512]{2,1,0:T(8,128)(2,1)} %broadcast_in_dim.90, s32[128]{0:T(128)S(1)} %fusion.80, bf16[128,8,512]{2,1,0:T(8,128)(2,1)S(1)} %bitcast.78), kind=kCustom, calls=%fused_computation.1 | custom fusion | bytes 3146240 | tf_op jit(solution)/shard_map/scatter | solution.py:78
  49.3 5.9 %all-to-all-start.1 = ((bf16[32,8,8,512]{3,2,1,0:T(8,128)(2,1)}), bf16[32,8,8,512]{3,2,1,0:T(8,128)(2,1)}, u32[]{:S(2)}, u32[]{:S(2)}) async-start(bf16[32,8,8,512]{3,2,1,0:T(8,128)(2,1)} %bitcast.4), calls=%async_computation.1 | async-start | bytes 4194304 | tf_op jit(solution)/shard_map/all_to_all | solution.py:84
  55.3 3.1 %collective-permute-start = (f32[64,1]{1,0:T(8,128)S(1)}, f32[64,1]{1,0:T(8,128)S(1)}, u32[]{:S(2)}, u32[]{:S(2)}) collective-permute-start(f32[64,1]{1,0:T(8,128)S(1)} %get-tuple-element.213), channel_id=1, source_target_pairs={{0,4},{4,8},{8,12},{12,16},{16,20},{20,24},{24,28},{1,5},{5,9},{9,... | collective-permute-start | bytes 776 | tf_op jit(solution)/shard_map/ppermute | solution.py:19
  61.8 38.5 %all-to-all-done.1 = bf16[32,8,8,512]{3,2,1,0:T(8,128)(2,1)} async-done(((bf16[32,8,8,512]{3,2,1,0:T(8,128)(2,1)}), bf16[32,8,8,512]{3,2,1,0:T(8,128)(2,1)}, u32[]{:S(2)}, u32[]{:S(2)}) %all-to-all-start.1) | async-done | bytes 2097184 | tf_op jit(solution)/shard_map/all_to_all | solution.py:84
  100.4 104.9 %while.15 = (s32[]{:T(128)}, f32[8,72,128]{2,0,1:T(8,128)S(1)}, s32[8,32]{1,0:T(8,128)S(1)}, bf16[8,32,8,512]{3,2,1,0:T(8,128)(2,1)}, s32[8,32,512]{2,1,0:T(8,12...) while((s32[]{:T(128)}, f32[8,72,128]{2,0,1:T(8,128)S(1)}, ...), condition=%wide.region_7.8_spmd.clone.clone, body=%wide.region_6.7_spmd.clone.clone.sunk | while | flops 336494848 | bytes 5374461 | solution.py:148
  101.6 11.2 %fusion.100 = f32[32,72,128]{2,1,0:T(8,128)S(1)} fusion(s32[32,512]{1,0:T(8,128)S(1)} %add_select_fusion.5, bf16[32,512]{1,0:T(8,128)(2,1)S(1)} %dynamic-slice_bitcast_fusion.4, bf16[32,8,512]{2,1,0:T(8,128)(2,1)S(1)} %fusion.99, bf16[32,9,512]{2,1,0:T(8,128)(2,1)S(1)} %concatenate.91), kind=kOutput, calls=%fused_computation.8.clone.1 | convolution fusion | flops 307363840 | bytes 1835008 | tf_op jit(solution)/shard_map/while/body/eval_jaxpr/gmc,gcx->gmx/dot_general | solution.py:140
  114.7 11.2 %fusion.100 = f32[32,72,128]{2,1,0:T(8,128)S(1)} fusion(s32[32,512]{1,0:T(8,128)S(1)} %add_select_fusion.5, bf16[32,512]{1,0:T(8,128)(2,1)S(1)} %dynamic-slice_bitcast_fusion.4, bf16[32,8,512]{2,1,0:T(8,128)(2,1)S(1)} %fusion.99, bf16[32,9,512]{2,1,0:T(8,128)(2,1)S(1)} %concatenate.91), kind=kOutput, calls=%fused_computation.8.clone.1 | convolution fusion | flops 307363840 | bytes 1835008 | tf_op jit(solution)/shard_map/while/body/eval_jaxpr/gmc,gcx->gmx/dot_general | solution.py:140
  127.8 11.2 %fusion.100 = f32[32,72,128]{2,1,0:T(8,128)S(1)} fusion(s32[32,512]{1,0:T(8,128)S(1)} %add_select_fusion.5, bf16[32,512]{1,0:T(8,128)(2,1)S(1)} %dynamic-slice_bitcast_fusion.4, bf16[32,8,512]{2,1,0:T(8,128)(2,1)S(1)} %fusion.99, bf16[32,9,512]{2,1,0:T(8,128)(2,1)S(1)} %concatenate.91), kind=kOutput, calls=%fused_computation.8.clone.1 | convolution fusion | flops 307363840 | bytes 1835008 | tf_op jit(solution)/shard_map/while/body/eval_jaxpr/gmc,gcx->gmx/dot_general | solution.py:140
  140.9 11.2 %fusion.100 = f32[32,72,128]{2,1,0:T(8,128)S(1)} fusion(s32[32,512]{1,0:T(8,128)S(1)} %add_select_fusion.5, bf16[32,512]{1,0:T(8,128)(2,1)S(1)} %dynamic-slice_bitcast_fusion.4, bf16[32,8,512]{2,1,0:T(8,128)(2,1)S(1)} %fusion.99, bf16[32,9,512]{2,1,0:T(8,128)(2,1)S(1)} %concatenate.91), kind=kOutput, calls=%fused_computation.8.clone.1 | convolution fusion | flops 307363840 | bytes 1835008 | tf_op jit(solution)/shard_map/while/body/eval_jaxpr/gmc,gcx->gmx/dot_general | solution.py:140
  154.0 11.2 %fusion.100 = f32[32,72,128]{2,1,0:T(8,128)S(1)} fusion(s32[32,512]{1,0:T(8,128)S(1)} %add_select_fusion.5, bf16[32,512]{1,0:T(8,128)(2,1)S(1)} %dynamic-slice_bitcast_fusion.4, bf16[32,8,512]{2,1,0:T(8,128)(2,1)S(1)} %fusion.99, bf16[32,9,512]{2,1,0:T(8,128)(2,1)S(1)} %concatenate.91), kind=kOutput, calls=%fused_computation.8.clone.1 | convolution fusion | flops 307363840 | bytes 1835008 | tf_op jit(solution)/shard_map/while/body/eval_jaxpr/gmc,gcx->gmx/dot_general | solution.py:140
  167.1 11.2 %fusion.100 = f32[32,72,128]{2,1,0:T(8,128)S(1)} fusion(s32[32,512]{1,0:T(8,128)S(1)} %add_select_fusion.5, bf16[32,512]{1,0:T(8,128)(2,1)S(1)} %dynamic-slice_bitcast_fusion.4, bf16[32,8,512]{2,1,0:T(8,128)(2,1)S(1)} %fusion.99, bf16[32,9,512]{2,1,0:T(8,128)(2,1)S(1)} %concatenate.91), kind=kOutput, calls=%fused_computation.8.clone.1 | convolution fusion | flops 307363840 | bytes 1835008 | tf_op jit(solution)/shard_map/while/body/eval_jaxpr/gmc,gcx->gmx/dot_general | solution.py:140
  180.3 11.2 %fusion.100 = f32[32,72,128]{2,1,0:T(8,128)S(1)} fusion(s32[32,512]{1,0:T(8,128)S(1)} %add_select_fusion.5, bf16[32,512]{1,0:T(8,128)(2,1)S(1)} %dynamic-slice_bitcast_fusion.4, bf16[32,8,512]{2,1,0:T(8,128)(2,1)S(1)} %fusion.99, bf16[32,9,512]{2,1,0:T(8,128)(2,1)S(1)} %concatenate.91), kind=kOutput, calls=%fused_computation.8.clone.1 | convolution fusion | flops 307363840 | bytes 1835008 | tf_op jit(solution)/shard_map/while/body/eval_jaxpr/gmc,gcx->gmx/dot_general | solution.py:140
  193.4 11.2 %fusion.100 = f32[32,72,128]{2,1,0:T(8,128)S(1)} fusion(s32[32,512]{1,0:T(8,128)S(1)} %add_select_fusion.5, bf16[32,512]{1,0:T(8,128)(2,1)S(1)} %dynamic-slice_bitcast_fusion.4, bf16[32,8,512]{2,1,0:T(8,128)(2,1)S(1)} %fusion.99, bf16[32,9,512]{2,1,0:T(8,128)(2,1)S(1)} %concatenate.91), kind=kOutput, calls=%fused_computation.8.clone.1 | convolution fusion | flops 307363840 | bytes 1835008 | tf_op jit(solution)/shard_map/while/body/eval_jaxpr/gmc,gcx->gmx/dot_general | solution.py:140
  205.6 5.0 %collective-permute-start.3 = (f32[8,64,1]{2,1,0:T(8,128)S(1)}, f32[8,64,1]{2,1,0:T(8,128)S(1)}, u32[]{:S(2)}, u32[]{:S(2)}) collective-permute-start(f32[8,64,1]{2,1,0:T(8,128)S(1)} %get-tuple-element.205), channel_id=1, source_target_pairs={{0,4},{4,8},{8,12},{12,16},{16,20},{20,24},{24,28},{1,5},{5,9},{9,... | collective-permute-start | bytes 6152 | tf_op jit(solution)/shard_map/ppermute | solution.py:19
  212.6 2.6 collective-permute-start.2
  215.2 2.9 %collective-permute-start.6 = (f32[1,130]{1,0:T(1,128)S(1)}, f32[1,130]{1,0:T(1,128)S(1)}, u32[]{:S(2)}, u32[]{:S(2)}) collective-permute-start(f32[1,130]{1,0:T(1,128)S(1)} %get-tuple-element.209), channel_id=1, source_target_pairs={{0,1},{1,2},{2,3},{4,5},{5,6},{6,7},{8,9},{9,10},{10,11},{12,13},{... | collective-permute-start | bytes 1568 | tf_op jit(solution)/shard_map/ppermute | solution.py:19
  218.2 4.0 %collective-permute-done.3 = f32[8,64,1]{2,1,0:T(8,128)S(1)} collective-permute-done((f32[8,64,1]{2,1,0:T(8,128)S(1)}, f32[8,64,1]{2,1,0:T(8,128)S(1)}, u32[]{:S(2)}, u32[]{:S(2)}) %collective-permute-start.3) | collective-permute-done | bytes 2080 | tf_op jit(solution)/shard_map/ppermute | solution.py:19
  222.3 2.6 collective-permute-start.5
  224.9 3.0 %collective-permute-start.7 = (f32[8,1,130]{2,1,0:T(1,128)S(1)}, f32[8,1,130]{2,1,0:T(1,128)S(1)}, u32[]{:S(2)}, u32[]{:S(2)}) collective-permute-start(f32[8,1,130]{2,1,0:T(1,128)S(1)} %get-tuple-element.199), channel_id=1, source_target_pairs={{0,1},{1,2},{2,3},{4,5},{5,6},{6,7},{8,9},{9,10},{10,11},{12,13},{... | collective-permute-start | bytes 12488 | tf_op jit(solution)/shard_map/ppermute | solution.py:19
  229.2 5.0 %collective-permute-start.8 = (f32[8,64,1]{2,1,0:T(8,128)S(1)}, f32[8,64,1]{2,1,0:T(8,128)S(1)}, u32[]{:S(2)}, u32[]{:S(2)}) collective-permute-start(f32[8,64,1]{2,1,0:T(8,128)S(1)} %get-tuple-element.203), channel_id=1, source_target_pairs={{0,4},{4,8},{8,12},{12,16},{16,20},{20,24},{24,28},{1,5},{5,9},{9,... | collective-permute-start | bytes 6152 | tf_op jit(solution)/shard_map/ppermute | solution.py:19
  236.2 4.0 %collective-permute-done.8 = f32[8,64,1]{2,1,0:T(8,128)S(1)} collective-permute-done((f32[8,64,1]{2,1,0:T(8,128)S(1)}, f32[8,64,1]{2,1,0:T(8,128)S(1)}, u32[]{:S(2)}, u32[]{:S(2)}) %collective-permute-start.8) | collective-permute-done | bytes 2080 | tf_op jit(solution)/shard_map/ppermute | solution.py:19
  240.2 5.5 %collective-permute-done.9 = f32[8,64,1]{2,1,0:T(8,128)S(1)} collective-permute-done((f32[8,64,1]{2,1,0:T(8,128)S(1)}, f32[8,64,1]{2,1,0:T(8,128)S(1)}, u32[]{:S(2)}, u32[]{:S(2)}) %collective-permute-start.9) | collective-permute-done | bytes 2080 | tf_op jit(solution)/shard_map/ppermute | solution.py:21
  245.8 2.3 collective-permute-start.10
  248.1 3.3 %collective-permute-start.11 = (f32[8,1,130]{2,1,0:T(1,128)S(1)}, f32[8,1,130]{2,1,0:T(1,128)S(1)}, u32[]{:S(2)}, u32[]{:S(2)}) collective-permute-start(f32[8,1,130]{2,1,0:T(1,128)S(1)} %get-tuple-element.197), channel_id=1, source_target_pairs={{0,1},{1,2},{2,3},{4,5},{5,6},{6,7},{8,9},{9,10},{10,11},{12,13},{... | collective-permute-start | bytes 12488 | tf_op jit(solution)/shard_map/ppermute | solution.py:19
  252.7 5.0 %collective-permute-start.12 = (f32[8,64,1]{2,1,0:T(8,128)S(1)}, f32[8,64,1]{2,1,0:T(8,128)S(1)}, u32[]{:S(2)}, u32[]{:S(2)}) collective-permute-start(f32[8,64,1]{2,1,0:T(8,128)S(1)} %get-tuple-element.201), channel_id=1, source_target_pairs={{0,4},{4,8},{8,12},{12,16},{16,20},{20,24},{24,28},{1,5},{5,9},{9,... | collective-permute-start | bytes 6152 | tf_op jit(solution)/shard_map/ppermute | solution.py:19
  259.7 3.9 %collective-permute-done.12 = f32[8,64,1]{2,1,0:T(8,128)S(1)} collective-permute-done((f32[8,64,1]{2,1,0:T(8,128)S(1)}, f32[8,64,1]{2,1,0:T(8,128)S(1)}, u32[]{:S(2)}, u32[]{:S(2)}) %collective-permute-start.12) | collective-permute-done | bytes 2080 | tf_op jit(solution)/shard_map/ppermute | solution.py:19
  263.6 5.5 %collective-permute-done.13 = f32[8,64,1]{2,1,0:T(8,128)S(1)} collective-permute-done((f32[8,64,1]{2,1,0:T(8,128)S(1)}, f32[8,64,1]{2,1,0:T(8,128)S(1)}, u32[]{:S(2)}, u32[]{:S(2)}) %collective-permute-start.13) | collective-permute-done | bytes 2080 | tf_op jit(solution)/shard_map/ppermute | solution.py:21
  271.5 3.3 %collective-permute-start.15 = (f32[8,1,130]{2,1,0:T(1,128)S(1)}, f32[8,1,130]{2,1,0:T(1,128)S(1)}, u32[]{:S(2)}, u32[]{:S(2)}) collective-permute-start(f32[8,1,130]{2,1,0:T(1,128)S(1)} %get-tuple-element.195), channel_id=1, source_target_pairs={{0,1},{1,2},{2,3},{4,5},{5,6},{6,7},{8,9},{9,10},{10,11},{12,13},{... | collective-permute-start | bytes 12488 | tf_op jit(solution)/shard_map/ppermute | solution.py:19
  (132 shorter events, 43.3 us)
Async XLA Ops:
  0.0 20.9 %copy-start.2 = (s32[64,2,512]{2,1,0:T(2,128)S(1)}, s32[64,2,512]{2,1,0:T(2,128)}, u32[]{:S(2)}) copy-start(s32[64,2,512]{2,1,0:T(2,128)} %param.14) | copy-start | bytes 786436
  0.0 34.1 %copy-start = (bf16[64,8,512]{2,1,0:T(8,128)(2,1)S(1)}, bf16[64,8,512]{2,1,0:T(8,128)(2,1)}, u32[]{:S(2)}) copy-start(bf16[64,8,512]{2,1,0:T(8,128)(2,1)} %param.11) | copy-start | bytes 1572868
  5.0 10.0 %all-to-all-start = ((s32[32,1,8]{2,1,0:T(1,128)}), s32[32,1,8]{2,1,0:T(1,128)S(1)}, u32[]{:S(2)}, u32[]{:S(2)}) async-start(s32[32,1,8]{2,1,0:T(1,128)} %bitcast.2), calls=%async_computation | async-start | bytes 32768 | tf_op jit(solution)/shard_map/all_to_all | solution.py:105
  15.0 12.9 %all-to-all-start.3 = ((bf16[32,8,512]{2,1,0:T(8,128)(2,1)}), bf16[32,8,512]{2,1,0:T(8,128)(2,1)S(1)}, u32[]{:S(2)}, u32[]{:S(2)}) async-start(bf16[32,8,512]{2,1,0:T(8,128)(2,1)} %bitcast.8), calls=%async_computation.3 | async-start | bytes 524288 | tf_op jit(solution)/shard_map/all_to_all | solution.py:91
  27.9 21.5 %all-to-all-start.2 = ((s32[32,8,512]{2,1,0:T(8,128)}), s32[32,8,512]{2,1,0:T(8,128)S(1)}, u32[]{:S(2)}, u32[]{:S(2)}) async-start(s32[32,8,512]{2,1,0:T(8,128)} %bitcast.6), calls=%async_computation.2 | async-start | bytes 1048576 | tf_op jit(solution)/shard_map/all_to_all | solution.py:98
  49.3 5.9 %copy-start.1 = (f32[64,128]{1,0:T(8,128)S(1)}, f32[64,128]{1,0:T(8,128)}, u32[]{:S(2)}) copy-start(f32[64,128]{1,0:T(8,128)} %param.19) | copy-start | bytes 98308
  49.3 51.0 %all-to-all-start.1 = ((bf16[32,8,8,512]{3,2,1,0:T(8,128)(2,1)}), bf16[32,8,8,512]{3,2,1,0:T(8,128)(2,1)}, u32[]{:S(2)}, u32[]{:S(2)}) async-start(bf16[32,8,8,512]{3,2,1,0:T(8,128)(2,1)} %bitcast.4), calls=%async_computation.1 | async-start | bytes 4194304 | tf_op jit(solution)/shard_map/all_to_all | solution.py:84
  55.3 157.2 %collective-permute-start = (f32[64,1]{1,0:T(8,128)S(1)}, f32[64,1]{1,0:T(8,128)S(1)}, u32[]{:S(2)}, u32[]{:S(2)}) collective-permute-start(f32[64,1]{1,0:T(8,128)S(1)} %get-tuple-element.213), channel_id=1, source_target_pairs={{0,4},{4,8},{8,12},{12,16},{16,20},{20,24},{24,28},{1,5},{5,9},{9,... | collective-permute-start | bytes 776 | tf_op jit(solution)/shard_map/ppermute | solution.py:19
  58.5 154.1 %collective-permute-start.1 = (f32[64,1]{1,0:T(8,128)S(1)}, f32[64,1]{1,0:T(8,128)S(1)}, u32[]{:S(2)}, u32[]{:S(2)}) collective-permute-start(f32[64,1]{1,0:T(8,128)S(1)} %get-tuple-element.212), channel_id=1, source_target_pairs={{4,0},{8,4},{12,8},{16,12},{20,16},{24,20},{28,24},{5,1},{9,5},{13... | collective-permute-start | bytes 776 | tf_op jit(solution)/shard_map/ppermute | solution.py:21
  100.4 105.0 %copy-start.4 = (f32[64,128]{1,0:T(8,128)S(1)}, f32[64,128]{1,0:T(8,128)}, u32[]{:S(2)}) copy-start(f32[64,128]{1,0:T(8,128)} %param.18) | copy-start | bytes 98308
  100.4 105.0 %copy-start.3 = (f32[8,64,128]{2,1,0:T(8,128)S(1)}, f32[8,64,128]{2,1,0:T(8,128)}, u32[]{:S(2)}) copy-start(f32[8,64,128]{2,1,0:T(8,128)} %param.17) | copy-start | bytes 786436
  205.6 16.6 %collective-permute-start.3 = (f32[8,64,1]{2,1,0:T(8,128)S(1)}, f32[8,64,1]{2,1,0:T(8,128)S(1)}, u32[]{:S(2)}, u32[]{:S(2)}) collective-permute-start(f32[8,64,1]{2,1,0:T(8,128)S(1)} %get-tuple-element.205), channel_id=1, source_target_pairs={{0,4},{4,8},{8,12},{12,16},{16,20},{20,24},{24,28},{1,5},{5,9},{9,... | collective-permute-start | bytes 6152 | tf_op jit(solution)/shard_map/ppermute | solution.py:19
  210.6 11.6 %collective-permute-start.4 = (f32[8,64,1]{2,1,0:T(8,128)S(1)}, f32[8,64,1]{2,1,0:T(8,128)S(1)}, u32[]{:S(2)}, u32[]{:S(2)}) collective-permute-start(f32[8,64,1]{2,1,0:T(8,128)S(1)} %get-tuple-element.204), channel_id=1, source_target_pairs={{4,0},{8,4},{12,8},{16,12},{20,16},{24,20},{28,24},{5,1},{9,5},{13... | collective-permute-start | bytes 6152 | tf_op jit(solution)/shard_map/ppermute | solution.py:21
  212.6 15.3 %collective-permute-start.2 = (f32[1,130]{1,0:T(1,128)S(1)}, f32[1,130]{1,0:T(1,128)S(1)}, u32[]{:S(2)}, u32[]{:S(2)}) collective-permute-start(f32[1,130]{1,0:T(1,128)S(1)} %get-tuple-element.208), channel_id=1, source_target_pairs={{1,0},{2,1},{3,2},{5,4},{6,5},{7,6},{9,8},{10,9},{11,10},{13,12},{... | collective-permute-start | bytes 1568 | tf_op jit(solution)/shard_map/ppermute | solution.py:21
  215.2 12.7 %collective-permute-start.6 = (f32[1,130]{1,0:T(1,128)S(1)}, f32[1,130]{1,0:T(1,128)S(1)}, u32[]{:S(2)}, u32[]{:S(2)}) collective-permute-start(f32[1,130]{1,0:T(1,128)S(1)} %get-tuple-element.209), channel_id=1, source_target_pairs={{0,1},{1,2},{2,3},{4,5},{5,6},{6,7},{8,9},{9,10},{10,11},{12,13},{... | collective-permute-start | bytes 1568 | tf_op jit(solution)/shard_map/ppermute | solution.py:19
  222.3 5.7 %collective-permute-start.5 = (f32[8,1,130]{2,1,0:T(1,128)S(1)}, f32[8,1,130]{2,1,0:T(1,128)S(1)}, u32[]{:S(2)}, u32[]{:S(2)}) collective-permute-start(f32[8,1,130]{2,1,0:T(1,128)S(1)} %get-tuple-element.198), channel_id=1, source_target_pairs={{1,0},{2,1},{3,2},{5,4},{6,5},{7,6},{9,8},{10,9},{11,10},{13,12},{... | collective-permute-start | bytes 12488 | tf_op jit(solution)/shard_map/ppermute | solution.py:21
  224.9 3.8 %collective-permute-start.7 = (f32[8,1,130]{2,1,0:T(1,128)S(1)}, f32[8,1,130]{2,1,0:T(1,128)S(1)}, u32[]{:S(2)}, u32[]{:S(2)}) collective-permute-start(f32[8,1,130]{2,1,0:T(1,128)S(1)} %get-tuple-element.199), channel_id=1, source_target_pairs={{0,1},{1,2},{2,3},{4,5},{5,6},{6,7},{8,9},{9,10},{10,11},{12,13},{... | collective-permute-start | bytes 12488 | tf_op jit(solution)/shard_map/ppermute | solution.py:19
  229.2 10.9 %collective-permute-start.8 = (f32[8,64,1]{2,1,0:T(8,128)S(1)}, f32[8,64,1]{2,1,0:T(8,128)S(1)}, u32[]{:S(2)}, u32[]{:S(2)}) collective-permute-start(f32[8,64,1]{2,1,0:T(8,128)S(1)} %get-tuple-element.203), channel_id=1, source_target_pairs={{0,4},{4,8},{8,12},{12,16},{16,20},{20,24},{24,28},{1,5},{5,9},{9,... | collective-permute-start | bytes 6152 | tf_op jit(solution)/shard_map/ppermute | solution.py:19
  234.3 11.4 %collective-permute-start.9 = (f32[8,64,1]{2,1,0:T(8,128)S(1)}, f32[8,64,1]{2,1,0:T(8,128)S(1)}, u32[]{:S(2)}, u32[]{:S(2)}) collective-permute-start(f32[8,64,1]{2,1,0:T(8,128)S(1)} %get-tuple-element.202), channel_id=1, source_target_pairs={{4,0},{8,4},{12,8},{16,12},{20,16},{24,20},{28,24},{5,1},{9,5},{13... | collective-permute-start | bytes 6152 | tf_op jit(solution)/shard_map/ppermute | solution.py:21
  245.8 5.6 %collective-permute-start.10 = (f32[8,1,130]{2,1,0:T(1,128)S(1)}, f32[8,1,130]{2,1,0:T(1,128)S(1)}, u32[]{:S(2)}, u32[]{:S(2)}) collective-permute-start(f32[8,1,130]{2,1,0:T(1,128)S(1)} %get-tuple-element.196), channel_id=1, source_target_pairs={{1,0},{2,1},{3,2},{5,4},{6,5},{7,6},{9,8},{10,9},{11,10},{13,12},{... | collective-permute-start | bytes 12488 | tf_op jit(solution)/shard_map/ppermute | solution.py:21
  248.1 4.1 %collective-permute-start.11 = (f32[8,1,130]{2,1,0:T(1,128)S(1)}, f32[8,1,130]{2,1,0:T(1,128)S(1)}, u32[]{:S(2)}, u32[]{:S(2)}) collective-permute-start(f32[8,1,130]{2,1,0:T(1,128)S(1)} %get-tuple-element.197), channel_id=1, source_target_pairs={{0,1},{1,2},{2,3},{4,5},{5,6},{6,7},{8,9},{9,10},{10,11},{12,13},{... | collective-permute-start | bytes 12488 | tf_op jit(solution)/shard_map/ppermute | solution.py:19
  252.7 10.8 %collective-permute-start.12 = (f32[8,64,1]{2,1,0:T(8,128)S(1)}, f32[8,64,1]{2,1,0:T(8,128)S(1)}, u32[]{:S(2)}, u32[]{:S(2)}) collective-permute-start(f32[8,64,1]{2,1,0:T(8,128)S(1)} %get-tuple-element.201), channel_id=1, source_target_pairs={{0,4},{4,8},{8,12},{12,16},{16,20},{20,24},{24,28},{1,5},{5,9},{9,... | collective-permute-start | bytes 6152 | tf_op jit(solution)/shard_map/ppermute | solution.py:19
  257.8 11.3 %collective-permute-start.13 = (f32[8,64,1]{2,1,0:T(8,128)S(1)}, f32[8,64,1]{2,1,0:T(8,128)S(1)}, u32[]{:S(2)}, u32[]{:S(2)}) collective-permute-start(f32[8,64,1]{2,1,0:T(8,128)S(1)} %get-tuple-element.200), channel_id=1, source_target_pairs={{4,0},{8,4},{12,8},{16,12},{20,16},{24,20},{28,24},{5,1},{9,5},{13... | collective-permute-start | bytes 6152 | tf_op jit(solution)/shard_map/ppermute | solution.py:21
  269.2 5.6 %collective-permute-start.14 = (f32[8,1,130]{2,1,0:T(1,128)S(1)}, f32[8,1,130]{2,1,0:T(1,128)S(1)}, u32[]{:S(2)}, u32[]{:S(2)}) collective-permute-start(f32[8,1,130]{2,1,0:T(1,128)S(1)} %get-tuple-element.194), channel_id=1, source_target_pairs={{1,0},{2,1},{3,2},{5,4},{6,5},{7,6},{9,8},{10,9},{11,10},{13,12},{... | collective-permute-start | bytes 12488 | tf_op jit(solution)/shard_map/ppermute | solution.py:21
  271.5 4.1 %collective-permute-start.15 = (f32[8,1,130]{2,1,0:T(1,128)S(1)}, f32[8,1,130]{2,1,0:T(1,128)S(1)}, u32[]{:S(2)}, u32[]{:S(2)}) collective-permute-start(f32[8,1,130]{2,1,0:T(1,128)S(1)} %get-tuple-element.195), channel_id=1, source_target_pairs={{0,1},{1,2},{2,3},{4,5},{5,6},{6,7},{8,9},{9,10},{10,11},{12,13},{... | collective-permute-start | bytes 12488 | tf_op jit(solution)/shard_map/ppermute | solution.py:19
where the time goes:
time: 281 us; the launch traced here: 277 us
  matrix products  94.8 us (34%)
  starting transfers between devices  72.6 us (26%)
  waiting for transfers between devices  68.6 us (24%)
  local copies, waits for them, and re-layouts  32.3 us (11%)
  other arithmetic  7.34 us (3%)
    dot_general x8, matrix products, accumulate(): jnp.einsum('gmc,gcx->gmx', left_side, right_side, preferred_element_type=...  89.7 us
    all_to_all x1, waiting for transfers between devices, shards(): lax.all_to_all(send_fields.reshape(device_count, capacity, field_count, t...  38.5 us
    ppermute x8, starting transfers between devices, with_halo(): lax.ppermute(tail, axis, [(i, (i + 1) % count) for i in range(ends)])  30.7 us
    ppermute x8, starting transfers between devices, with_halo(): lax.ppermute(head, axis, [((i + 1) % count, i) for i in range(ends)])  17.6 us
    ppermute x8, waiting for transfers between devices, with_halo(): lax.ppermute(tail, axis, [(i, (i + 1) % count) for i in range(ends)])  14 us
    scatter x1, local copies, waits for them, and re-layouts, shards(): jnp.zeros((slot_count, field_count, tile_cells), jnp.bfloat16).at[position]  13.7 us
    ppermute x8, waiting for transfers between devices, with_halo(): lax.ppermute(head, axis, [((i + 1) % count, i) for i in range(ends)])  11.1 us
    squeeze x8, local copies, waits for them, and re-layouts, shards(): totals, unused = lax.scan(accumulate, start_total, batched)  7.79 us
  transfers between devices with their start and end apart: 20, of which 10 were waited for; matrix products, arithmetic and copies ran while one was open for 46% of the time, Pallas kernels for 0%

commit v1 on v0

v1 whole, which is shorter than its diff:
```python
import functools

import jax
import jax.numpy as jnp
from jax import lax
from jax.experimental import pallas as pl
from jax.experimental.pallas import tpu as pltpu
from jax.sharding import PartitionSpec as P

TILE_ROWS = 8
ATM_COLS = 128
SWEEPS = 3
LAYERS = 4
EDGE = 4
LANE_BLOCK = 16

BF16 = jnp.bfloat16
F32 = jnp.float32
I32 = jnp.int32
VMEM = pl.BlockSpec(memory_space=pltpu.VMEM)
SMEM = pl.BlockSpec(memory_space=pltpu.SMEM)


def iota(shape, dim):
    return lax.broadcasted_iota(I32, shape, dim)


def params():
    return pltpu.CompilerParams(vmem_limit_bytes=40 << 20)


def pack_kernel(cap, group_s, group_v, fields, weights, codes, far_out, near_out, count):
    crossings, tiles = group_v.shape
    groups = 2 * far_out.shape[0]
    half = groups // 2
    slots = groups * cap

    hot = [
        (iota((groups, tiles), 0) == group_v[k : k + 1, :]).astype(F32) for k in range(crossings)
    ]
    before = (iota((tiles, tiles), 0) < iota((tiles, tiles), 1)).astype(BF16)
    offset = jnp.zeros((groups, 1), F32)
    packed_w = jnp.zeros((slots, weights.shape[2]), F32)
    packed_c = jnp.zeros((slots, weights.shape[2]), F32)
    for k in range(crossings):
        earlier = jnp.dot(hot[k].astype(BF16), before, preferred_element_type=F32) + offset
        offset = offset + jnp.sum(hot[k], axis=1, keepdims=True)
        within = jnp.sum(hot[k] * earlier, axis=0, keepdims=True).astype(I32)
        place = group_v[k : k + 1, :] * cap + within
        chosen = (iota((slots, tiles), 0) == place).astype(BF16)
        packed_w = packed_w + jnp.dot(chosen, weights[k], preferred_element_type=F32)
        packed_c = packed_c + jnp.dot(chosen, codes[k], preferred_element_type=F32)
    packed_w = packed_w.astype(BF16)
    packed_c = packed_c.astype(BF16)
    spare = jnp.zeros((8 - cap, weights.shape[2]), BF16)
    for g in range(groups):
        out, at = (far_out, g) if g < half else (near_out, g - half)
        for row, packed in ((cap, packed_w), (cap + 1, packed_c)):
            rows = packed[g * cap : (g + 1) * cap]
            out[at, row] = rows if cap == 8 else jnp.concatenate([rows, spare], axis=0)

    for g in range(groups):
        count[g] = 0

    for k in range(crossings):

        def place_pair(o, carry):
            g = group_s[k, o]
            n = count[g]
            count[g] = n + 1

            @pl.when(g < half)
            def _():
                far_out[g, n] = fields[o]

            @pl.when(g >= half)
            def _():
                near_out[g - half, n] = fields[o]

            return carry

        lax.fori_loop(0, tiles, place_pair, 0, unroll=4)

    empty = jnp.zeros(fields.shape[1:], BF16)
    for out, first in ((far_out, 0), (near_out, half)):

        def fill_group(g, carry):
            def fill(n, inner):
                out[g, n] = empty
                return inner

            return lax.fori_loop(count[first + g], cap, fill, carry)

        lax.fori_loop(0, half, fill_group, 0)


def pack(group, fields, weights, codes, cap, groups):
    shape = (groups // 2, cap + 2) + fields.shape[1:]
    return pl.pallas_call(
        functools.partial(pack_kernel, cap),
        out_shape=[jax.ShapeDtypeStruct(shape, BF16)] * 2,
        in_specs=[SMEM, VMEM, VMEM, VMEM, VMEM],
        out_specs=[VMEM, VMEM],
        scratch_shapes=[pltpu.SMEM((groups,), I32)],
        compiler_params=params(),
    )(group, group, fields, weights, codes)


def decode(code):
    tile = jnp.zeros(code.shape, I32)
    for k in range(1, 8):
        tile = tile + jnp.where(code >= 2.0 ** (7 + 8 * k), 1, 0)
    scaled = code
    for bit in (1, 2, 4):
        scaled = jnp.where((tile & bit) != 0, scaled * 2.0 ** (-8 * bit), scaled)
    cell = scaled.astype(I32)
    row = jnp.zeros(code.shape, I32)
    for k in range(1, 8):
        row = row + jnp.where(cell >= (1 << (7 + k)), 1, 0)
    return tile, row, lax.shift_right_logical(cell, row) - ATM_COLS


def bin_slots(cap, slots, total):
    sources, _, field_count, cells = slots.shape
    rows_here = total.shape[0] * TILE_ROWS // (TILE_ROWS + 1)
    zero = jnp.zeros((), BF16)
    total[...] = jnp.zeros_like(total)

    def source(g, carry):
        weight = slots[g, cap].astype(F32)
        tile, row, col = decode(slots[g, cap + 1].astype(F32))
        row16 = row.astype(F32).astype(BF16)
        col16 = col.astype(F32).astype(BF16)
        weight16 = weight.astype(BF16)
        for n in range(cap):
            field = slots[g, n]
            t = tile[n, 0]
            row_n = jnp.broadcast_to(row16[n : n + 1], (16, cells))
            twice = jnp.concatenate([field, field], axis=0)
            sub = iota((16, cells), 0)
            left = []
            for q in range(0, TILE_ROWS, 2):
                want = jnp.where(sub >= 8, q + 1.0, q + 0.0).astype(BF16)
                left.append(jnp.where(row_n == want, twice, zero))
            ones = jnp.ones((), BF16)
            left.append(jnp.where(row_n == sub.astype(F32).astype(BF16), ones, zero))
            right = jnp.where(
                jnp.broadcast_to(col16[n : n + 1], (ATM_COLS, cells))
                == iota((ATM_COLS, cells), 0).astype(F32).astype(BF16),
                jnp.broadcast_to(weight16[n : n + 1], (ATM_COLS, cells)),
                zero,
            )
            added = lax.dot_general(
                jnp.concatenate(left, axis=0),
                right,
                (((1,), (1,)), ((), ())),
                preferred_element_type=F32,
            )
            main = TILE_ROWS * field_count
            total[pl.ds(t * TILE_ROWS, TILE_ROWS)] += added[:main].reshape(
                TILE_ROWS, field_count, ATM_COLS
            )
            total[pl.ds(rows_here + t, 1)] += added[main : main + TILE_ROWS].reshape(
                1, TILE_ROWS, ATM_COLS
            )
        return carry

    lax.fori_loop(0, sources, source, 0, unroll=2)


def far_kernel(cap, slots, total):
    bin_slots(cap, slots, total)


def near_kernel(cap, slots, passed, land_flux, land_area, merged, strips, edges, total):
    bin_slots(cap, slots, total)
    field_count, rows_here, cols_here = land_flux.shape
    area = land_area[...]
    denom = (total[rows_here:] + passed[rows_here:]).reshape(rows_here, cols_here) + area
    lane = iota((rows_here, cols_here), 1)
    border = (lane < SWEEPS) | (lane >= cols_here - SWEEPS)
    numer = jnp.swapaxes(total[:rows_here] + passed[:rows_here], 0, 1)
    packed = jnp.zeros((rows_here, cols_here), F32)
    for f in range(field_count):
        value = (numer[f] + area * land_flux[f]) / denom
        merged[f] = value
        edges[f] = jnp.concatenate([value[:EDGE], value[rows_here - EDGE :]], axis=0)
        strip = jnp.where(border, value, 0.0)
        packed = packed + (pltpu.roll(strip, f * LANE_BLOCK, 1) if f else strip)
    strips[...] = packed


def cost(slots):
    sources, _, field_count, cells = slots.shape
    each = 2 * (field_count + 1) * TILE_ROWS * cells * ATM_COLS
    return pl.CostEstimate(
        flops=sources * 8 * each, bytes_accessed=slots.size * 2, transcendentals=0
    )


def bin_far(slots, cap, rows_here, field_count):
    shape = (rows_here // TILE_ROWS * (TILE_ROWS + 1), field_count, ATM_COLS)
    return pl.pallas_call(
        functools.partial(far_kernel, cap),
        out_shape=jax.ShapeDtypeStruct(shape, F32),
        in_specs=[VMEM],
        out_specs=VMEM,
        compiler_params=params(),
        cost_estimate=cost(slots),
    )(slots)


def bin_near(slots, passed, land_flux, land_area, cap):
    field_count, rows_here, cols_here = land_flux.shape
    return pl.pallas_call(
        functools.partial(near_kernel, cap),
        out_shape=[
            jax.ShapeDtypeStruct(land_flux.shape, F32),
            jax.ShapeDtypeStruct((rows_here, cols_here), F32),
            jax.ShapeDtypeStruct((field_count, 2 * EDGE, cols_here), F32),
        ],
        in_specs=[VMEM] * 4,
        out_specs=[VMEM] * 3,
        scratch_shapes=[pltpu.VMEM(passed.shape, F32)],
        compiler_params=params(),
        cost_estimate=cost(slots),
    )(slots, passed, land_flux, land_area)


def swaps(axis):
    count = lax.axis_size(axis)
    first = [(i, i ^ 1) for i in range(count) if i ^ 1 < count]
    second = [(i, i + 1) for i in range(1, count - 1, 2)]
    return first, second + [(b, a) for a, b in second]


def neighbours(values, axis):
    first, second = swaps(axis)
    one = lax.ppermute(values, axis, first)
    two = lax.ppermute(values, axis, second)
    odd = lax.axis_index(axis) % 2 == 1
    return jnp.where(odd, one, two), jnp.where(odd, two, one)


def select_columns(before, after, block):
    lane = iota(before.shape, 1) % block
    return jnp.where(lane < block // 2, after, before)


def ends(values):
    rows = values.shape[0]
    return jnp.concatenate([values[:EDGE], values[rows - EDGE :]], axis=0)


def coefficient_kernel(kappa, columns, above, below, out):
    padded = jnp.concatenate(
        [
            jnp.concatenate([kappa[...], below[0][:EDGE], above[0][EDGE:]], axis=0),
            jnp.concatenate([columns[...], below[1][:EDGE], above[1][EDGE:]], axis=0),
        ],
        axis=1,
    )
    lane = iota(padded.shape, 1)
    cols_here = kappa.shape[1]
    known = (lane < cols_here + SWEEPS) | (lane >= 2 * cols_here - SWEEPS)
    padded = jnp.where(known, padded, 0.0)
    inside = padded > 0.0
    for i, (shift, axis) in enumerate(NEIGHBOURS):
        near = pltpu.roll(padded, shift % padded.shape[axis], axis)
        out[i] = jnp.where(inside, 0.5 * (padded + near), 0.0)


NEIGHBOURS = ((-1, 0), (1, 0), (-1, 1), (1, 1))


def sweep_kernel(merged, before, after, above, below, coefficients, out):
    field_count, rows_here, cols_here = merged.shape
    lane = iota((rows_here, cols_here), 1)
    border = (lane < SWEEPS) | (lane >= cols_here - SWEEPS)
    columns = select_columns(before[...], after[...], LANE_BLOCK)
    lane8 = iota((2 * EDGE, cols_here), 1)
    border8 = (lane8 < SWEEPS) | (lane8 >= cols_here - SWEEPS)
    corner = jnp.concatenate([below[field_count][:EDGE], above[field_count][EDGE:]], axis=0)
    for f in range(field_count):
        shift = (cols_here - f * LANE_BLOCK) % cols_here
        side = pltpu.roll(columns, shift, 1) if f else columns
        far = pltpu.roll(corner, shift, 1) if f else corner
        rows = jnp.concatenate([below[f][:EDGE], above[f][EDGE:]], axis=0)
        u = jnp.concatenate(
            [
                jnp.concatenate([merged[f], rows], axis=0),
                jnp.concatenate(
                    [jnp.where(border, side, 0.0), jnp.where(border8, far, 0.0)], axis=0
                ),
            ],
            axis=1,
        )
        for _ in range(SWEEPS):
            new = u
            for i, (step, axis) in enumerate(NEIGHBOURS):
                near = pltpu.roll(u, step % u.shape[axis], axis)
                new = new + coefficients[i] * (near - u)
            u = new
        out[f] = u[:rows_here, :cols_here]


def shards(
    ocean_fields,
    dest_device,
    dest_tile,
    cell_target,
    cell_weight,
    sea_mask,
    land_flux,
    land_area,
    kappa,
):
    tiles_here, field_count, tile_cells = ocean_fields.shape
    crossing_count = dest_device.shape[1]
    width_x = lax.axis_size("gx")
    width_y = lax.axis_size("gy")
    device_count = width_x * width_y
    cap = max(2, tiles_here * crossing_count * 2 // device_count)
    half_x = width_x // 2
    layer_x = width_x // LAYERS
    rows_here, cols_here = land_area.shape

    owner = dest_device.T
    owner_x, owner_y = owner // width_y, owner % width_y
    mirror_x = (LAYERS - 1 - owner_x // layer_x) * layer_x + owner_x % layer_x
    near = owner_x // half_x == lax.axis_index("gx") // half_x
    stop_x = jnp.where(near, owner_x, mirror_x) % half_x
    group = stop_x * width_y + owner_y + jnp.where(near, device_count // 2, 0)

    weights = jnp.swapaxes(cell_weight * sea_mask[:, None, :].astype(BF16), 0, 1)
    scale = jnp.ones(dest_tile.shape, F32)
    for bit in (1, 2, 4):
        scale = scale * jnp.where((dest_tile & bit) != 0, 2.0 ** (8 * bit), 1.0)
    cell = (cell_target % ATM_COLS + ATM_COLS) << (cell_target // ATM_COLS)
    codes = jnp.swapaxes((cell.astype(F32) * scale[:, :, None]).astype(BF16), 0, 1)

    far_slots, near_slots = pack(group, ocean_fields, weights, codes, cap, device_count)
    halves = [
        [h * (device_count // 2) + i for i in range(device_count // 2)] for h in range(2)
    ]
    exchange = functools.partial(
        lax.all_to_all,
        axis_name=("gx", "gy"),
        split_axis=0,
        concat_axis=0,
        axis_index_groups=halves,
        tiled=True,
    )
    far_got = exchange(far_slots)
    near_got = exchange(near_slots)
    far_total = bin_far(far_got, cap, rows_here, field_count)
    mirror = [
        (i, (LAYERS - 1 - i // layer_x) * layer_x + i % layer_x) for i in range(width_x)
    ]
    passed = lax.ppermute(far_total, "gx", mirror)

    k_before, k_after = neighbours(kappa, "gx")
    k_columns = select_columns(k_before, k_after, cols_here)
    k_above, k_below = neighbours(jnp.stack([ends(kappa), ends(k_columns)]), "gy")
    coefficients = pl.pallas_call(
        coefficient_kernel,
        out_shape=jax.ShapeDtypeStruct((4, rows_here + 2 * EDGE, 2 * cols_here), F32),
        in_specs=[VMEM] * 4,
        out_specs=VMEM,
        compiler_params=params(),
    )(kappa, k_columns, k_above, k_below)

    merged, strips, edges = bin_near(near_got, passed, land_flux, land_area, cap)
    before, after = neighbours(strips, "gx")
    corners = ends(select_columns(before, after, LANE_BLOCK))
    above, below = neighbours(jnp.concatenate([edges, corners[None]], axis=0), "gy")
    return pl.pallas_call(
        sweep_kernel,
        out_shape=jax.ShapeDtypeStruct(merged.shape, F32),
        in_specs=[VMEM] * 6,
        out_specs=VMEM,
        compiler_params=params(),
    )(merged, before, after, above, below, coefficients)


def solution(mesh):
    return jax.shard_map(
        shards,
        mesh=mesh,
        in_specs=(
            P(("gx", "gy"), None, None),
            P(("gx", "gy"), None),
            P(("gx", "gy"), None),
            P(("gx", "gy"), None, None),
            P(("gx", "gy"), None, None),
            P(("gx", "gy"), None),
            P(None, "gy", "gx"),
            P("gy", "gx"),
            P("gy", "gx"),
        ),
        out_specs=P(None, "gy", "gx"),
        check_vma=False,
    )
```

time: 281 us -> 102 us (0.36); the launches traced: 277 us -> 101 us
  matrix products: 94.8 us -> 0 us
  starting transfers between devices: 72.6 us -> 22.1 us
  waiting for transfers between devices: 68.6 us -> 29 us
  local copies, waits for them, and re-layouts: 32.3 us -> 0.03 us
  blocking collectives: 0 us -> 22.5 us
  Pallas kernels: 0 us -> 22.2 us
    dot_general x16 -> x0, matrix products: 94.8 us -> none  [the longest x8 89.7 us: accumulate(): jnp.einsum('gmc,gcx->gmx', left_side, right_side, preferred_element_type=...]
    all_to_all x4 -> x1, waiting for transfers between devices: 43.5 us -> 0.01 us  [shards(): near_got = exchange(near_slots)]
    ppermute x16 -> x9, starting transfers between devices: 48.4 us -> 16.5 us  [the longest x4 15 us: neighbours(): two = lax.ppermute(values, axis, second)]
    all_to_all x0 -> x1, blocking collectives: none -> 22.5 us  [shards(): far_got = exchange(far_slots)]
    pallas_call x0 -> x5, Pallas kernels: none -> 22.2 us  [the longest x1 6.92 us: bin_near(): pl.pallas_call(functools.partial(near_kernel, cap), out_shape=[jax.ShapeD...]
    all_to_all x4 -> x1, starting transfers between devices: 24.3 us -> 5.61 us  [shards(): near_got = exchange(near_slots)]
    scatter x4 -> x0, local copies, waits for them, and re-layouts: 18.2 us -> none  [the longest x1 13.7 us: shards(): jnp.zeros((slot_count, field_count, tile_cells), jnp.bfloat16).at[position]]
    squeeze x8 -> x0, local copies, waits for them, and re-layouts: 7.79 us -> none  [shards(): totals, unused = lax.scan(accumulate, start_total, batched)]
  transfers between devices with their start and end apart: 20 -> 10, of which waited for: 10 -> 3; matrix products, arithmetic and copies ran while one was open for 46% -> 0% of each run, Pallas kernels for 0% -> 7%
where the time goes in v1:
time: 102 us; the launch traced here: 101 us
  waiting for transfers between devices  29 us (28%)
  blocking collectives  22.5 us (22%)
  Pallas kernels  22.2 us (22%)
  starting transfers between devices  22.1 us (22%)
  other arithmetic  4.61 us (5%)
    all_to_all x1, blocking collectives, shards(): far_got = exchange(far_slots)  22.5 us
    ppermute x4, waiting for transfers between devices, neighbours(): two = lax.ppermute(values, axis, second)  15.2 us
    ppermute x4, starting transfers between devices, neighbours(): two = lax.ppermute(values, axis, second)  15 us
    ppermute x1, waiting for transfers between devices, shards(): passed = lax.ppermute(far_total, 'gx', mirror)  13.8 us
    pallas_call x1, Pallas kernels, bin_near(): pl.pallas_call(functools.partial(near_kernel, cap), out_shape=[jax.ShapeD...  6.92 us
    pallas_call x1, Pallas kernels, bin_far(): pl.pallas_call(functools.partial(far_kernel, cap), out_shape=jax.ShapeDty...  6.76 us
    all_to_all x1, starting transfers between devices, shards(): near_got = exchange(near_slots)  5.61 us
    pallas_call x1, Pallas kernels, pack(): pl.pallas_call(functools.partial(pack_kernel, cap), out_shape=[jax.ShapeD...  5.43 us
  transfers between devices with their start and end apart: 10, of which 3 were waited for; matrix products, arithmetic and copies ran while one was open for 0% of the time, Pallas kernels for 7%

profile of v1, /device:TPU:21, one launch (start us, length us, event | category | flops | bytes accessed | tf_op | source)
XLA Modules:
  0.0 100.7 jit_solution(6902856045039243815)
XLA Ops:
  0.0 1.0 convert_element_type.10
  1.0 0.7 fusion.18
  1.7 0.7 fusion.16.group_s.group_v
  2.4 0.9 fusion.9.weights
  3.3 1.2 %fusion.10.codes = bf16[2,64,512]{2,1,0:T(8,128)(2,1)S(1)} fusion(f32[64,2]{0,1:T(2,128)S(1)} %fusion.18, s32[64,2,512]{2,1,0:T(2,128)} %param.12), kind=kLoop, calls=%fused_computation.17 | loop fusion | flops 1572864 | bytes 393728 | tf_op jit(solution)/shard_map/transpose | solution.py:340
  4.5 5.4 %shard_map.91 = (bf16[16,10,8,512]{3,2,1,0:T(8,128)(2,1)S(1)}, bf16[16,10,8,512]{3,2,1,0:T(8,128)(2,1)}) custom-call(s32[2,64]{1,0:T(2,128)S(1)} %fusion.16.group_s.group_v, s32[2,64]{1,0:T(2,128)S(1)} %fusion.16.group_s.group_v, bf16[64,8,512]{2,1,0:T(8,128)(2,1)S(1)} %copy-done, bf16[2,64,512]{2,1,0:T(8,128)(2,1)S(1)} %fusion.9.weights, ...), custom_call_target="tpu_custom_call" | custom-call | tf_op jit(solution)/shard_map/pallas_call | solution.py:99
  10.0 22.5 %all_to_all.10.slots = bf16[16,10,8,512]{3,2,1,0:T(8,128)(2,1)S(1)} all-to-all(bf16[16,10,8,512]{3,2,1,0:T(8,128)(2,1)S(1)} %get-tuple-element.11), channel_id=1, replica_groups={{0,1,2,3,4,5,6,7,8,9,10,11,12,13,14,15},{16,17,18,19,20,21,22,23,24,25,..., dimensions={0} | all-to-all | bytes 2621440 | tf_op jit(solution)/shard_map/all_to_all | solution.py:354
  32.4 5.6 %all-to-all-start = ((bf16[16,10,8,512]{3,2,1,0:T(8,128)(2,1)}), bf16[16,10,8,512]{3,2,1,0:T(8,128)(2,1)S(1)}, u32[]{:S(2)}, u32[]{:S(2)}) async-start(bf16[16,10,8,512]{3,2,1,0:T(8,128)(2,1)} %get-tuple-element.10), calls=%async_computation | async-start | bytes 2621440 | tf_op jit(solution)/shard_map/all_to_all | solution.py:355
  38.1 3.1 %collective-permute-start.5 = (f32[64,128]{1,0:T(8,128)S(1)}, f32[64,128]{1,0:T(8,128)S(1)}, u32[]{:S(2)}, u32[]{:S(2)}) collective-permute-start(f32[64,128]{1,0:T(8,128)S(1)} %copy-done.1), channel_id=1, source_target_pairs={{4,8},{12,16},{20,24},{8,4},{16,12},{24,20},{5,9},{13,17},{21,25},... | collective-permute-start | bytes 98312 | tf_op jit(solution)/shard_map/ppermute | solution.py:240
  41.2 0.1 collective-permute-start.6
  41.4 13.7 %collective-permute-done.5 = f32[64,128]{1,0:T(8,128)S(1)} collective-permute-done((f32[64,128]{1,0:T(8,128)S(1)}, f32[64,128]{1,0:T(8,128)S(1)}, u32[]{:S(2)}, u32[]{:S(2)}) %collective-permute-start.5) | collective-permute-done | bytes 32800 | tf_op jit(solution)/shard_map/ppermute | solution.py:240
  55.1 0.0 collective-permute-done.6
  55.1 0.0 copy-start.2
  55.1 0.0 copy-start.3
  55.1 6.8 %shard_map.92 = f32[72,8,128]{2,1,0:T(8,128)S(1)} custom-call(bf16[16,10,8,512]{3,2,1,0:T(8,128)(2,1)S(1)} %all_to_all.10.slots), custom_call_target="tpu_custom_call" | custom-call | flops 1207959552 | bytes 1310720 | tf_op jit(solution)/shard_map/pallas_call | solution.py:203
  61.9 0.1 collective-permute-start
  62.0 0.0 all-to-all-done.slots
  62.0 13.8 %collective-permute-done.passed = f32[72,8,128]{2,1,0:T(8,128)S(1)} collective-permute-done((f32[72,8,128]{2,1,0:T(8,128)S(1)}, f32[72,8,128]{2,1,0:T(8,128)S(1)}, u32[]{:S(2)}, u32[]{:S(2)}) %collective-permute-start) | collective-permute-done | bytes 294944 | tf_op jit(solution)/shard_map/ppermute | solution.py:360
  75.8 6.9 %shard_map.93 = (f32[8,64,128]{2,1,0:T(8,128)S(1)}, f32[64,128]{1,0:T(8,128)S(1)}, f32[8,8,128]{2,1,0:T(8,128)S(1)}) custom-call(bf16[16,10,8,512]{3,2,1,0:T(8,128)(2,1)S(1)} %all-to-all-done.slots, f32[72,8,128]{2,1,0:T(8,128)S(1)} %collective-permute-done.passed, f32[8,64,128]{2,1,0:T(8,128)S(1)} %copy-done.2, f32[64,128]{1,0:T(8,128)S(1)} %copy-done.3), custom_call_target="tpu_custom_call" | custom-call | flops 1207959552 | bytes 1310720 | tf_op jit(solution)/shard_map/pallas_call | solution.py:215
  82.8 0.1 collective-permute-start.1
  82.8 1.9 %collective-permute-start.2 = (f32[64,128]{1,0:T(8,128)S(1)}, f32[64,128]{1,0:T(8,128)S(1)}, u32[]{:S(2)}, u32[]{:S(2)}) collective-permute-start(f32[64,128]{1,0:T(8,128)S(1)} %get-tuple-element.13), channel_id=1, source_target_pairs={{4,8},{12,16},{20,24},{8,4},{16,12},{24,20},{5,9},{13,17},{21,25},... | collective-permute-start | bytes 98312 | tf_op jit(solution)/shard_map/ppermute | solution.py:240
  84.8 1.2 %collective-permute-start.7 = (f32[2,8,128]{2,1,0:T(8,128)S(1)}, f32[2,8,128]{2,1,0:T(8,128)S(1)}, u32[]{:S(2)}, u32[]{:S(2)}) collective-permute-start(f32[2,8,128]{2,1,0:T(8,128)S(1)} %pad_maximum_fusion.1), channel_id=1, source_target_pairs={{0,1},{1,0},{2,3},{3,2},{4,5},{5,4},{6,7},{7,6},{8,9},{9,8},{10,11... | collective-permute-start | bytes 24584 | tf_op jit(solution)/shard_map/ppermute | solution.py:239
  86.0 5.3 %collective-permute-start.8 = (f32[2,8,128]{2,1,0:T(8,128)S(1)}, f32[2,8,128]{2,1,0:T(8,128)S(1)}, u32[]{:S(2)}, u32[]{:S(2)}) collective-permute-start(f32[2,8,128]{2,1,0:T(8,128)S(1)} %pad_maximum_fusion.1), channel_id=1, source_target_pairs={{1,2},{2,1},{5,6},{6,5},{9,10},{10,9},{13,14},{14,13},{17,18},{18,... | collective-permute-start | bytes 24584 | tf_op jit(solution)/shard_map/ppermute | solution.py:240
  91.2 0.0 collective-permute-done.1
  91.3 0.0 collective-permute-done.2
  91.3 0.1 collective-permute-start.3
  91.4 4.7 %collective-permute-start.4 = (f32[9,8,128]{2,1,0:T(8,128)S(1)}, f32[9,8,128]{2,1,0:T(8,128)S(1)}, u32[]{:S(2)}, u32[]{:S(2)}) collective-permute-start(f32[9,8,128]{2,1,0:T(8,128)S(1)} %pad_maximum_fusion), channel_id=1, source_target_pairs={{1,2},{2,1},{5,6},{6,5},{9,10},{10,9},{13,14},{14,13},{17,18},{18,... | collective-permute-start | bytes 110600 | tf_op jit(solution)/shard_map/ppermute | solution.py:240
  96.1 0.0 collective-permute-done.8
  96.1 0.1 shard_map.94.coefficients
  96.2 0.0 collective-permute-done.3
  96.2 1.5 %collective-permute-done.4 = f32[9,8,128]{2,1,0:T(8,128)S(1)} collective-permute-done((f32[9,8,128]{2,1,0:T(8,128)S(1)}, f32[9,8,128]{2,1,0:T(8,128)S(1)}, u32[]{:S(2)}, u32[]{:S(2)}) %collective-permute-start.4) | collective-permute-done | bytes 36896 | tf_op jit(solution)/shard_map/ppermute | solution.py:240
  97.7 3.0 %shard_map.95 = f32[8,64,128]{2,1,0:T(8,128)} custom-call(f32[8,64,128]{2,1,0:T(8,128)S(1)} %get-tuple-element.12.merged, f32[64,128]{1,0:T(8,128)S(1)} %get-tuple-element.17.before, f32[64,128]{1,0:T(8,128)S(1)} %get-tuple-element.16.after, f32[9,8,128]{2,1,0:T(8,128)S(1)} %get-tuple-element.19.above, f32[9,8,128]{2,1,0:T(8,128)S(1)} %get-tuple-element.18.below, ...), custom_call_target="tpu_custom_call" | custom-call | tf_op jit(solution)/shard_map/pallas_call | solution.py:377
  (23 shorter events, 0.1 us)
Async XLA Ops:
  0.0 4.5 %copy-start = (bf16[64,8,512]{2,1,0:T(8,128)(2,1)S(1)}, bf16[64,8,512]{2,1,0:T(8,128)(2,1)}, u32[]{:S(2)}) copy-start(bf16[64,8,512]{2,1,0:T(8,128)(2,1)} %fields.1) | copy-start | bytes 1572868
  32.4 5.6 %copy-start.1 = (f32[64,128]{1,0:T(8,128)S(1)}, f32[64,128]{1,0:T(8,128)}, u32[]{:S(2)}) copy-start(f32[64,128]{1,0:T(8,128)} %kappa.1) | copy-start | bytes 98308
  32.4 29.6 %all-to-all-start = ((bf16[16,10,8,512]{3,2,1,0:T(8,128)(2,1)}), bf16[16,10,8,512]{3,2,1,0:T(8,128)(2,1)S(1)}, u32[]{:S(2)}, u32[]{:S(2)}) async-start(bf16[16,10,8,512]{3,2,1,0:T(8,128)(2,1)} %get-tuple-element.10), calls=%async_computation | async-start | bytes 2621440 | tf_op jit(solution)/shard_map/all_to_all | solution.py:355
  38.1 17.1 %collective-permute-start.5 = (f32[64,128]{1,0:T(8,128)S(1)}, f32[64,128]{1,0:T(8,128)S(1)}, u32[]{:S(2)}, u32[]{:S(2)}) collective-permute-start(f32[64,128]{1,0:T(8,128)S(1)} %copy-done.1), channel_id=1, source_target_pairs={{4,8},{12,16},{20,24},{8,4},{16,12},{24,20},{5,9},{13,17},{21,25},... | collective-permute-start | bytes 98312 | tf_op jit(solution)/shard_map/ppermute | solution.py:240
  41.2 13.9 %collective-permute-start.6 = (f32[64,128]{1,0:T(8,128)S(1)}, f32[64,128]{1,0:T(8,128)S(1)}, u32[]{:S(2)}, u32[]{:S(2)}) collective-permute-start(f32[64,128]{1,0:T(8,128)S(1)} %copy-done.1), channel_id=1, source_target_pairs={{0,4},{4,0},{8,12},{12,8},{16,20},{20,16},{24,28},{28,24},{1,5},{5... | collective-permute-start | bytes 98312 | tf_op jit(solution)/shard_map/ppermute | solution.py:239
  55.1 20.7 %copy-start.2 = (f32[8,64,128]{2,1,0:T(8,128)S(1)}, f32[8,64,128]{2,1,0:T(8,128)}, u32[]{:S(2)}) copy-start(f32[8,64,128]{2,1,0:T(8,128)} %land_flux.1) | copy-start | bytes 786436
  55.1 20.7 %copy-start.3 = (f32[64,128]{1,0:T(8,128)S(1)}, f32[64,128]{1,0:T(8,128)}, u32[]{:S(2)}) copy-start(f32[64,128]{1,0:T(8,128)} %land_area.1) | copy-start | bytes 98308
  61.9 13.9 %collective-permute-start = (f32[72,8,128]{2,1,0:T(8,128)S(1)}, f32[72,8,128]{2,1,0:T(8,128)S(1)}, u32[]{:S(2)}, u32[]{:S(2)}) collective-permute-start(f32[72,8,128]{2,1,0:T(8,128)S(1)} %shard_map.92), channel_id=1, source_target_pairs={{0,24},{4,28},{8,16},{12,20},{16,8},{20,12},{24,0},{28,4},{1,25},{... | collective-permute-start | bytes 884744 | tf_op jit(solution)/shard_map/ppermute | solution.py:360
  82.8 8.5 %collective-permute-start.1 = (f32[64,128]{1,0:T(8,128)S(1)}, f32[64,128]{1,0:T(8,128)S(1)}, u32[]{:S(2)}, u32[]{:S(2)}) collective-permute-start(f32[64,128]{1,0:T(8,128)S(1)} %get-tuple-element.13), channel_id=1, source_target_pairs={{0,4},{4,0},{8,12},{12,8},{16,20},{20,16},{24,28},{28,24},{1,5},{5... | collective-permute-start | bytes 98312 | tf_op jit(solution)/shard_map/ppermute | solution.py:239
  82.8 8.4 %collective-permute-start.2 = (f32[64,128]{1,0:T(8,128)S(1)}, f32[64,128]{1,0:T(8,128)S(1)}, u32[]{:S(2)}, u32[]{:S(2)}) collective-permute-start(f32[64,128]{1,0:T(8,128)S(1)} %get-tuple-element.13), channel_id=1, source_target_pairs={{4,8},{12,16},{20,24},{8,4},{16,12},{24,20},{5,9},{13,17},{21,25},... | collective-permute-start | bytes 98312 | tf_op jit(solution)/shard_map/ppermute | solution.py:240
  84.8 11.3 %collective-permute-start.7 = (f32[2,8,128]{2,1,0:T(8,128)S(1)}, f32[2,8,128]{2,1,0:T(8,128)S(1)}, u32[]{:S(2)}, u32[]{:S(2)}) collective-permute-start(f32[2,8,128]{2,1,0:T(8,128)S(1)} %pad_maximum_fusion.1), channel_id=1, source_target_pairs={{0,1},{1,0},{2,3},{3,2},{4,5},{5,4},{6,7},{7,6},{8,9},{9,8},{10,11... | collective-permute-start | bytes 24584 | tf_op jit(solution)/shard_map/ppermute | solution.py:239
  86.0 10.1 %collective-permute-start.8 = (f32[2,8,128]{2,1,0:T(8,128)S(1)}, f32[2,8,128]{2,1,0:T(8,128)S(1)}, u32[]{:S(2)}, u32[]{:S(2)}) collective-permute-start(f32[2,8,128]{2,1,0:T(8,128)S(1)} %pad_maximum_fusion.1), channel_id=1, source_target_pairs={{1,2},{2,1},{5,6},{6,5},{9,10},{10,9},{13,14},{14,13},{17,18},{18,... | collective-permute-start | bytes 24584 | tf_op jit(solution)/shard_map/ppermute | solution.py:240
  91.3 4.9 %collective-permute-start.3 = (f32[9,8,128]{2,1,0:T(8,128)S(1)}, f32[9,8,128]{2,1,0:T(8,128)S(1)}, u32[]{:S(2)}, u32[]{:S(2)}) collective-permute-start(f32[9,8,128]{2,1,0:T(8,128)S(1)} %pad_maximum_fusion), channel_id=1, source_target_pairs={{0,1},{1,0},{2,3},{3,2},{4,5},{5,4},{6,7},{7,6},{8,9},{9,8},{10,11... | collective-permute-start | bytes 110600 | tf_op jit(solution)/shard_map/ppermute | solution.py:239
  91.4 6.3 %collective-permute-start.4 = (f32[9,8,128]{2,1,0:T(8,128)S(1)}, f32[9,8,128]{2,1,0:T(8,128)S(1)}, u32[]{:S(2)}, u32[]{:S(2)}) collective-permute-start(f32[9,8,128]{2,1,0:T(8,128)S(1)} %pad_maximum_fusion), channel_id=1, source_target_pairs={{1,2},{2,1},{5,6},{6,5},{9,10},{10,9},{13,14},{14,13},{17,18},{18,... | collective-permute-start | bytes 110600 | tf_op jit(solution)/shard_map/ppermute | solution.py:240

commit v2 on v1

v2 whole, which is shorter than its diff:
```python
import functools

import jax
import jax.numpy as jnp
from jax import lax
from jax.experimental import pallas as pl
from jax.experimental.pallas import tpu as pltpu
from jax.sharding import PartitionSpec as P

TILE_ROWS = 8
ATM_COLS = 128
COL_BITS = 7
SWEEPS = 3
LAYERS = 4
EDGE = 4
LANE_BLOCK = 16

BF16 = jnp.bfloat16
F32 = jnp.float32
I32 = jnp.int32
VMEM = pl.BlockSpec(memory_space=pltpu.VMEM)
HBM = pl.BlockSpec(memory_space=pltpu.HBM)


def iota(shape, dim):
    return lax.broadcasted_iota(I32, shape, dim)


def params(megabytes=40):
    return pltpu.CompilerParams(vmem_limit_bytes=megabytes << 20)


def pack_kernel(
    cap,
    mirror,
    *refs,
):
    given, out, held, out_held = refs[:7], refs[7], refs[8:15], refs[15]
    count, source, in_sems, out_sems = refs[16:]
    copies = [
        pltpu.make_async_copy(given[i], held[i], in_sems.at[i]) for i in range(len(given))
    ]
    for copy in copies:
        copy.start()
    dest_s, dest_v, tile_v, target, weight, mask, fields = held
    crossings, tiles = dest_v.shape
    half, cells = out_held.shape[0], fields.shape[2]
    owners, slots = 2 * half, half * cap
    first = lax.axis_index("gx") // (lax.axis_size("gx") // 2) * half

    for d in range(owners):
        count[d] = 0

    def clear(i, carry):
        source[i] = 0
        return carry

    lax.fori_loop(0, owners * cap, clear, 0, unroll=16)
    copies[0].wait()
    for k in range(crossings):

        def enter(o, carry):
            d = dest_s[k, o]
            n = count[d]
            count[d] = n + 1
            source[d * cap + n] = o
            return carry

        lax.fori_loop(0, tiles, enter, 0, unroll=16)

    for copy in copies[1:6]:
        copy.wait()
    sea = mask[...] != 0
    every_weight = weight[...].astype(F32)
    before = (iota((tiles, tiles), 0) < iota((tiles, tiles), 1)).astype(BF16)
    offset = jnp.zeros((owners, 1), F32)
    packed_w = jnp.zeros((slots, cells), F32)
    packed_c = jnp.zeros((slots, cells), F32)
    for k in range(crossings):
        dest = dest_v[k : k + 1, :]
        hot = (iota((owners, tiles), 0) == dest).astype(F32)
        earlier = jnp.dot(hot.astype(BF16), before, preferred_element_type=F32) + offset
        offset = offset + jnp.sum(hot, axis=1, keepdims=True)
        within = jnp.sum(hot * earlier, axis=0, keepdims=True).astype(I32)
        place = ((dest ^ mirror) - first) * cap + within
        chosen = (iota((slots, tiles), 0) == place).astype(BF16)
        scale = jnp.ones(dest.shape, F32)
        for bit in (1, 2, 4):
            scale = scale * jnp.where((tile_v[k : k + 1, :] & bit) != 0, 2.0 ** (8 * bit), 1.0)
        cell = target[:, k, :]
        code = ((cell & (ATM_COLS - 1)) + ATM_COLS) << (cell >> COL_BITS)
        packed_w = packed_w + jnp.dot(
            chosen,
            jnp.where(sea, every_weight[:, k, :], 0.0).astype(BF16),
            preferred_element_type=F32,
        )
        packed_c = packed_c + jnp.dot(
            chosen * scale.astype(BF16), code.astype(F32).astype(BF16), preferred_element_type=F32
        )
    packed_w = packed_w.astype(BF16)
    packed_c = packed_c.astype(BF16)
    spare = jnp.zeros((8 - cap, cells), BF16)
    for g in range(half):
        for row, packed in ((cap, packed_w), (cap + 1, packed_c)):
            rows = packed[g * cap : (g + 1) * cap]
            out_held[g, row] = rows if cap == 8 else jnp.concatenate([rows, spare], axis=0)

    copies[6].wait()
    parts = out_sems.shape[0]
    step = half // parts
    sent = []
    for part in range(parts):

        def fill(g, carry):
            owner = (first + g) ^ mirror
            for n in range(cap):
                out_held[g, n] = fields[source[owner * cap + n]]
            return carry

        lax.fori_loop(part * step, (part + 1) * step, fill, 0, unroll=2)
        block = pl.ds(part * step, step)
        sent.append(pltpu.make_async_copy(out_held.at[block], out.at[block], out_sems.at[part]))
        sent[-1].start()
    for copy in sent:
        copy.wait()


def pack(dest, tile, target, weight, mask, fields, cap, owners, mirror):
    shape = (owners // 2, cap + 2) + fields.shape[1:]
    given = (dest, dest, tile, target, weight, mask, fields)
    return pl.pallas_call(
        functools.partial(pack_kernel, cap, mirror),
        out_shape=jax.ShapeDtypeStruct(shape, BF16),
        in_specs=[HBM] * len(given),
        out_specs=HBM,
        scratch_shapes=[pltpu.SMEM(dest.shape, I32)]
        + [pltpu.VMEM(a.shape, a.dtype) for a in given[1:]]
        + [
            pltpu.VMEM(shape, BF16),
            pltpu.SMEM((owners,), I32),
            pltpu.SMEM((owners * cap,), I32),
            pltpu.SemaphoreType.DMA((len(given),)),
            pltpu.SemaphoreType.DMA((4,)),
        ],
        compiler_params=params(62),
        cost_estimate=pl.CostEstimate(
            flops=10**8, bytes_accessed=4 * 10**6, transcendentals=0
        ),
    )(*given)


def decode(code):
    tile = jnp.zeros(code.shape, I32)
    for k in range(1, 8):
        tile = tile + jnp.where(code >= 2.0 ** (7 + 8 * k), 1, 0)
    scaled = code
    for bit in (1, 2, 4):
        scaled = jnp.where((tile & bit) != 0, scaled * 2.0 ** (-8 * bit), scaled)
    cell = scaled.astype(I32)
    row = jnp.zeros(code.shape, I32)
    for k in range(1, 8):
        row = row + jnp.where(cell >= (1 << (7 + k)), 1, 0)
    return tile, row, lax.shift_right_logical(cell, row) - ATM_COLS


def bin_slots(cap, slots, total):
    sources, _, field_count, cells = slots.shape
    rows_here = total.shape[0] * TILE_ROWS // (TILE_ROWS + 1)
    zero = jnp.zeros((), BF16)
    total[...] = jnp.zeros_like(total)

    def source(g, carry):
        weight = slots[g, cap].astype(F32)
        tile, row, col = decode(slots[g, cap + 1].astype(F32))
        row16 = row.astype(F32).astype(BF16)
        col16 = col.astype(F32).astype(BF16)
        weight16 = weight.astype(BF16)
        for n in range(cap):
            field = slots[g, n]
            t = tile[n, 0]
            row_n = jnp.broadcast_to(row16[n : n + 1], (16, cells))
            twice = jnp.concatenate([field, field], axis=0)
            sub = iota((16, cells), 0)
            left = []
            for q in range(0, TILE_ROWS, 2):
                want = jnp.where(sub >= 8, q + 1.0, q + 0.0).astype(BF16)
                left.append(jnp.where(row_n == want, twice, zero))
            ones = jnp.ones((), BF16)
            left.append(jnp.where(row_n == sub.astype(F32).astype(BF16), ones, zero))
            right = jnp.where(
                jnp.broadcast_to(col16[n : n + 1], (ATM_COLS, cells))
                == iota((ATM_COLS, cells), 0).astype(F32).astype(BF16),
                jnp.broadcast_to(weight16[n : n + 1], (ATM_COLS, cells)),
                zero,
            )
            added = lax.dot_general(
                jnp.concatenate(left, axis=0),
                right,
                (((1,), (1,)), ((), ())),
                preferred_element_type=F32,
            )
            main = TILE_ROWS * field_count
            total[pl.ds(t * TILE_ROWS, TILE_ROWS)] += added[:main].reshape(
                TILE_ROWS, field_count, ATM_COLS
            )
            total[pl.ds(rows_here + t, 1)] += added[main : main + TILE_ROWS].reshape(
                1, TILE_ROWS, ATM_COLS
            )
        return carry

    lax.fori_loop(0, sources, source, 0, unroll=2)


def merge_kernel(total, passed, land_flux, land_area, merged, strips, edges):
    field_count, rows_here, cols_here = land_flux.shape
    area = land_area[...]
    denom = (total[rows_here:] + passed[rows_here:]).reshape(rows_here, cols_here) + area
    lane = iota((rows_here, cols_here), 1)
    border = (lane < SWEEPS) | (lane >= cols_here - SWEEPS)
    numer = jnp.swapaxes(total[:rows_here] + passed[:rows_here], 0, 1)
    packed = jnp.zeros((rows_here, cols_here), F32)
    for f in range(field_count):
        value = (numer[f] + area * land_flux[f]) / denom
        merged[f] = value
        edges[f] = jnp.concatenate([value[:EDGE], value[rows_here - EDGE :]], axis=0)
        strip = jnp.where(border, value, 0.0)
        packed = packed + (pltpu.roll(strip, f * LANE_BLOCK, 1) if f else strip)
    strips[...] = packed


def cost(slots):
    sources, _, field_count, cells = slots.shape
    each = 2 * (field_count + 1) * TILE_ROWS * cells * ATM_COLS
    return pl.CostEstimate(
        flops=sources * 8 * each, bytes_accessed=slots.size * 2, transcendentals=0
    )


def bin_all(slots, cap, rows_here, field_count):
    shape = (rows_here // TILE_ROWS * (TILE_ROWS + 1), field_count, ATM_COLS)
    return pl.pallas_call(
        functools.partial(bin_slots, cap),
        out_shape=jax.ShapeDtypeStruct(shape, F32),
        in_specs=[VMEM],
        out_specs=VMEM,
        compiler_params=params(),
        cost_estimate=cost(slots),
    )(slots)


def merge(total, passed, land_flux, land_area):
    field_count, rows_here, cols_here = land_flux.shape
    return pl.pallas_call(
        merge_kernel,
        out_shape=[
            jax.ShapeDtypeStruct(land_flux.shape, F32),
            jax.ShapeDtypeStruct((rows_here, cols_here), F32),
            jax.ShapeDtypeStruct((field_count, 2 * EDGE, cols_here), F32),
        ],
        in_specs=[VMEM] * 4,
        out_specs=[VMEM] * 3,
        compiler_params=params(),
    )(total, passed, land_flux, land_area)


def swaps(axis):
    count = lax.axis_size(axis)
    first = [(i, i ^ 1) for i in range(count) if i ^ 1 < count]
    second = [(i, i + 1) for i in range(1, count - 1, 2)]
    return first, second + [(b, a) for a, b in second]


def neighbours(values, axis):
    first, second = swaps(axis)
    one = lax.ppermute(values, axis, first)
    two = lax.ppermute(values, axis, second)
    odd = lax.axis_index(axis) % 2 == 1
    return jnp.where(odd, one, two), jnp.where(odd, two, one)


def select_columns(before, after, block):
    lane = iota(before.shape, 1) % block
    return jnp.where(lane < block // 2, after, before)


def ends(values):
    rows = values.shape[0]
    return jnp.concatenate([values[:EDGE], values[rows - EDGE :]], axis=0)


NEIGHBOURS = ((-1, 0), (1, 0), (-1, 1), (1, 1))


def sweep_kernel(merged, before, after, above, below, kappa, k_columns, out):
    field_count, rows_here, cols_here = merged.shape

    def near(values, i):
        step, axis = NEIGHBOURS[i]
        return pltpu.roll(values, step % values.shape[axis], axis)

    def halo_rows(i):
        return jnp.concatenate([below[i][:EDGE], above[i][EDGE:]], axis=0)

    def whole(cells, rows, columns, corners):
        lane = iota((rows_here + 2 * EDGE, cols_here), 1)
        border = (lane < SWEEPS) | (lane >= cols_here - SWEEPS)
        side = jnp.concatenate([columns, corners], axis=0)
        return jnp.concatenate(
            [jnp.concatenate([cells, rows], axis=0), jnp.where(border, side, 0.0)], axis=1
        )

    k = whole(kappa[...], halo_rows(field_count + 1), k_columns[...], halo_rows(field_count + 2))
    coefficients = [
        jnp.where(k > 0.0, 0.5 * (k + near(k, i)), 0.0) for i in range(len(NEIGHBOURS))
    ]
    columns = select_columns(before[...], after[...], LANE_BLOCK)
    corners = halo_rows(field_count)
    for f in range(field_count):
        shift = (cols_here - f * LANE_BLOCK) % cols_here
        u = whole(
            merged[f],
            halo_rows(f),
            pltpu.roll(columns, shift, 1) if f else columns,
            pltpu.roll(corners, shift, 1) if f else corners,
        )
        for _ in range(SWEEPS):
            new = u
            for i, coefficient in enumerate(coefficients):
                new = new + coefficient * (near(u, i) - u)
            u = new
        out[f] = u[:rows_here, :cols_here]


def shards(
    ocean_fields,
    dest_device,
    dest_tile,
    cell_target,
    cell_weight,
    sea_mask,
    land_flux,
    land_area,
    kappa,
):
    tiles_here, field_count, tile_cells = ocean_fields.shape
    crossing_count = dest_device.shape[1]
    width_x = lax.axis_size("gx")
    width_y = lax.axis_size("gy")
    device_count = width_x * width_y
    cap = max(2, tiles_here * crossing_count * 2 // device_count)
    layer = width_x // LAYERS * width_y
    rows_here, cols_here = land_area.shape

    mirror = (LAYERS - 1) * layer
    pairs = (dest_device.T, dest_tile.T, cell_target, cell_weight, sea_mask, ocean_fields)
    halves = [
        [h * (device_count // 2) + i for i in range(device_count // 2)] for h in range(2)
    ]
    exchange = functools.partial(
        lax.all_to_all,
        axis_name=("gx", "gy"),
        split_axis=0,
        concat_axis=0,
        axis_index_groups=halves,
        tiled=True,
    )
    far_slots = pack(*pairs, cap, device_count, mirror)
    pairs, kappa, far_slots = lax.optimization_barrier((pairs, kappa, far_slots))
    far_got = exchange(far_slots)
    near_slots = pack(*pairs, cap, device_count, 0)
    k_columns = select_columns(*neighbours(kappa, "gx"), cols_here)
    near_slots, k_columns = lax.optimization_barrier((near_slots, k_columns))

    near_got = exchange(near_slots)
    far_total = bin_all(far_got, cap, rows_here, field_count)
    opposite = [(i, i ^ (mirror // width_y)) for i in range(width_x)]
    passed = lax.ppermute(far_total, "gx", opposite)
    total = bin_all(near_got, cap, rows_here, field_count)

    merged, strips, edges = merge(total, passed, land_flux, land_area)
    before, after = neighbours(strips, "gx")
    corners = ends(select_columns(before, after, LANE_BLOCK))
    rows = jnp.concatenate([edges, corners[None], ends(kappa)[None], ends(k_columns)[None]], axis=0)
    above, below = neighbours(rows, "gy")
    return pl.pallas_call(
        sweep_kernel,
        out_shape=jax.ShapeDtypeStruct(merged.shape, F32),
        in_specs=[VMEM] * 7,
        out_specs=VMEM,
        compiler_params=params(),
    )(merged, before, after, above, below, kappa, k_columns)


def solution(mesh):
    return jax.shard_map(
        shards,
        mesh=mesh,
        in_specs=(
            P(("gx", "gy"), None, None),
            P(("gx", "gy"), None),
            P(("gx", "gy"), None),
            P(("gx", "gy"), None, None),
            P(("gx", "gy"), None, None),
            P(("gx", "gy"), None),
            P(None, "gy", "gx"),
            P("gy", "gx"),
            P("gy", "gx"),
        ),
        out_specs=P(None, "gy", "gx"),
        check_vma=False,
    )
```

time: 102 us -> 76.1 us (0.75)
  blocking collectives: 22.5 us -> 0 us
  other arithmetic: 4.61 us -> 0.08 us
  starting transfers between devices: 22.1 us -> 26.5 us
  waiting for transfers between devices: 29 us -> 25.6 us
  Pallas kernels: 22.2 us -> 23.4 us
    all_to_all x1 -> x0, blocking collectives: 22.5 us -> none  [shards(): far_got = exchange(far_slots)]
    ppermute x1, waiting for transfers between devices: 13.8 us -> 0.01 us  [shards(): passed = lax.ppermute(far_total, 'gx', opposite)]
    all_to_all x1, waiting for transfers between devices: 0.01 us -> 11.1 us  [shards(): near_got = exchange(near_slots)]
    ppermute x4 -> x3, waiting for transfers between devices: 15.2 us -> 5.82 us  [neighbours(): two = lax.ppermute(values, axis, second)]
    ppermute x4 -> x3, waiting for transfers between devices: 0.01 us -> 7.39 us  [neighbours(): one = lax.ppermute(values, axis, first)]
    all_to_all x0 -> x1, starting transfers between devices: none -> 5.58 us  [shards(): far_got = exchange(far_slots)]
    ppermute x4 -> x3, starting transfers between devices: 15 us -> 11.1 us  [neighbours(): two = lax.ppermute(values, axis, second)]
    ppermute x4 -> x3, starting transfers between devices: 1.49 us -> 4.87 us  [neighbours(): one = lax.ppermute(values, axis, first)]
  transfers between devices with their start and end apart: 10 -> 9, of which waited for: 3 -> 7; matrix products, arithmetic and copies ran while one was open for 0% -> 0% of each run, Pallas kernels for 7% -> 22%
where the time goes in v2:
time: 76.1 us; the launch traced here: 75.8 us
  starting transfers between devices  26.5 us (35%)
  waiting for transfers between devices  25.6 us (34%)
  Pallas kernels  23.4 us (31%)
    pallas_call x2, Pallas kernels, bin_all(): pl.pallas_call(functools.partial(bin_slots, cap), out_shape=jax.ShapeDtyp...  13.5 us
    ppermute x3, starting transfers between devices, neighbours(): two = lax.ppermute(values, axis, second)  11.1 us
    all_to_all x1, waiting for transfers between devices, shards(): near_got = exchange(near_slots)  11.1 us
    ppermute x3, waiting for transfers between devices, neighbours(): one = lax.ppermute(values, axis, first)  7.39 us
    pallas_call x2, Pallas kernels, pack(): pl.pallas_call(functools.partial(pack_kernel, cap, mirror), out_shape=jax...  6.66 us
    ppermute x3, waiting for transfers between devices, neighbours(): two = lax.ppermute(values, axis, second)  5.82 us
    all_to_all x1, starting transfers between devices, shards(): far_got = exchange(far_slots)  5.58 us
    ppermute x3, starting transfers between devices, neighbours(): one = lax.ppermute(values, axis, first)  4.87 us
  transfers between devices with their start and end apart: 9, of which 7 were waited for; matrix products, arithmetic and copies ran while one was open for 0% of the time, Pallas kernels for 22%

profile of v2, /device:TPU:21, one launch (start us, length us, event | category | flops | bytes accessed | tf_op | source)
XLA Modules:
  0.0 75.8 jit_solution(15892406573165665008)
XLA Ops:
  0.0 3.3 %shard_map.91 = bf16[16,10,8,512]{3,2,1,0:T(8,128)(2,1)} custom-call(s32[2,64]{1,0:T(2,128)} %bitcast.8, s32[2,64]{1,0:T(2,128)} %bitcast.9, s32[2,64]{1,0:T(2,128)} %bitcast.12, s32[64,2,512]{2,1,0:T(2,128)} %refs_3_.2, bf16[64,2,512]{2,1,0:T(2,128)(2,1)} %refs_4_.2, s32[64,512]{1,0:T(8,128)} %refs_5_.2, bf16[64,8,512]{2,1,0:T(8,128)(2,1)} %refs_6_.2), custom_call_target="tpu_custom_call" | custom-call | flops 100000000 | bytes 4000000 | tf_op jit(solution)/shard_map/pallas_call | solution.py:131
  3.3 0.0 copy-start.1
  3.3 5.6 %all-to-all-start.1 = ((bf16[16,10,8,512]{3,2,1,0:T(8,128)(2,1)}), bf16[16,10,8,512]{3,2,1,0:T(8,128)(2,1)S(1)}, u32[]{:S(2)}, u32[]{:S(2)}) async-start(bf16[16,10,8,512]{3,2,1,0:T(8,128)(2,1)} %shard_map.91), calls=%async_computation.1 | async-start | bytes 2621440 | tf_op jit(solution)/shard_map/all_to_all | solution.py:369
  8.9 0.0 copy-done.1
  8.9 0.2 collective-permute-start.1
  9.1 4.2 %collective-permute-start = (f32[64,128]{1,0:T(8,128)S(1)}, f32[64,128]{1,0:T(8,128)S(1)}, u32[]{:S(2)}, u32[]{:S(2)}) collective-permute-start(f32[64,128]{1,0:T(8,128)S(1)} %copy-done.1), channel_id=1, source_target_pairs={{4,8},{12,16},{20,24},{8,4},{16,12},{24,20},{5,9},{13,17},{21,25},... | collective-permute-start | bytes 98312 | tf_op jit(solution)/shard_map/ppermute | solution.py:276
  13.3 3.3 %shard_map.92 = bf16[16,10,8,512]{3,2,1,0:T(8,128)(2,1)} custom-call(s32[2,64]{1,0:T(2,128)} %bitcast.10, s32[2,64]{1,0:T(2,128)} %bitcast.11, s32[2,64]{1,0:T(2,128)} %bitcast.13, s32[64,2,512]{2,1,0:T(2,128)} %refs_3_.2, bf16[64,2,512]{2,1,0:T(2,128)(2,1)} %refs_4_.2, s32[64,512]{1,0:T(8,128)} %refs_5_.2, bf16[64,8,512]{2,1,0:T(8,128)(2,1)} %refs_6_.2), custom_call_target="tpu_custom_call" | custom-call | flops 100000000 | bytes 4000000 | tf_op jit(solution)/shard_map/pallas_call | solution.py:131
  16.6 6.2 %collective-permute-done.1 = f32[64,128]{1,0:T(8,128)S(1)} collective-permute-done((f32[64,128]{1,0:T(8,128)S(1)}, f32[64,128]{1,0:T(8,128)S(1)}, u32[]{:S(2)}, u32[]{:S(2)}) %collective-permute-start.1) | collective-permute-done | bytes 32800 | tf_op jit(solution)/shard_map/ppermute | solution.py:275
  22.8 3.1 %collective-permute-done = f32[64,128]{1,0:T(8,128)S(1)} collective-permute-done((f32[64,128]{1,0:T(8,128)S(1)}, f32[64,128]{1,0:T(8,128)S(1)}, u32[]{:S(2)}, u32[]{:S(2)}) %collective-permute-start) | collective-permute-done | bytes 32800 | tf_op jit(solution)/shard_map/ppermute | solution.py:276
  26.0 1.3 %all-to-all-done.1.slots = bf16[16,10,8,512]{3,2,1,0:T(8,128)(2,1)S(1)} async-done(((bf16[16,10,8,512]{3,2,1,0:T(8,128)(2,1)}), bf16[16,10,8,512]{3,2,1,0:T(8,128)(2,1)S(1)}, u32[]{:S(2)}, u32[]{:S(2)}) %all-to-all-start.1) | async-done | bytes 1310752 | tf_op jit(solution)/shard_map/all_to_all | solution.py:369
  27.3 4.8 %all-to-all-start = ((bf16[16,10,8,512]{3,2,1,0:T(8,128)(2,1)}), bf16[16,10,8,512]{3,2,1,0:T(8,128)(2,1)S(1)}, u32[]{:S(2)}, u32[]{:S(2)}) async-start(bf16[16,10,8,512]{3,2,1,0:T(8,128)(2,1)} %shard_map.92), calls=%async_computation | async-start | bytes 2621440 | tf_op jit(solution)/shard_map/all_to_all | solution.py:374
  32.1 6.8 %shard_map.94 = f32[72,8,128]{2,1,0:T(8,128)S(1)} custom-call(bf16[16,10,8,512]{3,2,1,0:T(8,128)(2,1)S(1)} %all-to-all-done.1.slots), custom_call_target="tpu_custom_call" | custom-call | flops 1207959552 | bytes 1310720 | tf_op jit(solution)/shard_map/pallas_call | solution.py:241
  38.9 0.1 collective-permute-start.2
  39.0 0.0 copy-start
  39.0 0.0 copy-start.2
  39.0 11.1 %all-to-all-done.slots = bf16[16,10,8,512]{3,2,1,0:T(8,128)(2,1)S(1)} async-done(((bf16[16,10,8,512]{3,2,1,0:T(8,128)(2,1)}), bf16[16,10,8,512]{3,2,1,0:T(8,128)(2,1)S(1)}, u32[]{:S(2)}, u32[]{:S(2)}) %all-to-all-start) | async-done | bytes 1310752 | tf_op jit(solution)/shard_map/all_to_all | solution.py:374
  50.0 6.8 %shard_map.93.total = f32[72,8,128]{2,1,0:T(8,128)S(1)} custom-call(bf16[16,10,8,512]{3,2,1,0:T(8,128)(2,1)S(1)} %all-to-all-done.slots), custom_call_target="tpu_custom_call" | custom-call | flops 1207959552 | bytes 1310720 | tf_op jit(solution)/shard_map/pallas_call | solution.py:241
  56.8 0.0 collective-permute-done.2.passed
  56.8 0.0 copy-done
  56.8 0.0 copy-done.2
  56.8 0.2 shard_map.95
  57.0 2.8 %collective-permute-start.4 = (f32[64,128]{1,0:T(8,128)S(1)}, f32[64,128]{1,0:T(8,128)S(1)}, u32[]{:S(2)}, u32[]{:S(2)}) collective-permute-start(f32[64,128]{1,0:T(8,128)S(1)} %get-tuple-element.28), channel_id=1, source_target_pairs={{4,8},{12,16},{20,24},{8,4},{16,12},{24,20},{5,9},{13,17},{21,25},... | collective-permute-start | bytes 98312 | tf_op jit(solution)/shard_map/ppermute | solution.py:276
  59.8 0.1 collective-permute-start.3
  59.9 2.7 %collective-permute-done.4 = f32[64,128]{1,0:T(8,128)S(1)} collective-permute-done((f32[64,128]{1,0:T(8,128)S(1)}, f32[64,128]{1,0:T(8,128)S(1)}, u32[]{:S(2)}, u32[]{:S(2)}) %collective-permute-start.4) | collective-permute-done | bytes 32800 | tf_op jit(solution)/shard_map/ppermute | solution.py:276
  62.6 0.3 collective-permute-done.3
  63.0 4.2 %collective-permute-start.6 = (f32[11,8,128]{2,1,0:T(8,128)S(1)}, f32[11,8,128]{2,1,0:T(8,128)S(1)}, u32[]{:S(2)}, u32[]{:S(2)}) collective-permute-start(f32[11,8,128]{2,1,0:T(8,128)S(1)} %pad_maximum_fusion), channel_id=1, source_target_pairs={{1,2},{2,1},{5,6},{6,5},{9,10},{10,9},{13,14},{14,13},{17,18},{18,... | collective-permute-start | bytes 135176 | tf_op jit(solution)/shard_map/ppermute | solution.py:276
  67.2 4.6 %collective-permute-start.5 = (f32[11,8,128]{2,1,0:T(8,128)S(1)}, f32[11,8,128]{2,1,0:T(8,128)S(1)}, u32[]{:S(2)}, u32[]{:S(2)}) collective-permute-start(f32[11,8,128]{2,1,0:T(8,128)S(1)} %pad_maximum_fusion), channel_id=1, source_target_pairs={{0,1},{1,0},{2,3},{3,2},{4,5},{5,4},{6,7},{7,6},{8,9},{9,8},{10,11... | collective-permute-start | bytes 135176 | tf_op jit(solution)/shard_map/ppermute | solution.py:275
  71.8 0.0 collective-permute-done.6
  71.8 0.9 %collective-permute-done.5 = f32[11,8,128]{2,1,0:T(8,128)S(1)} collective-permute-done((f32[11,8,128]{2,1,0:T(8,128)S(1)}, f32[11,8,128]{2,1,0:T(8,128)S(1)}, u32[]{:S(2)}, u32[]{:S(2)}) %collective-permute-start.5) | collective-permute-done | bytes 45088 | tf_op jit(solution)/shard_map/ppermute | solution.py:275
  72.7 3.1 %shard_map.96 = f32[8,64,128]{2,1,0:T(8,128)} custom-call(f32[8,64,128]{2,1,0:T(8,128)S(1)} %get-tuple-element.27.merged, f32[64,128]{1,0:T(8,128)S(1)} %get-tuple-element.33.before, f32[64,128]{1,0:T(8,128)S(1)} %get-tuple-element.32.after, f32[11,8,128]{2,1,0:T(8,128)S(1)} %get-tuple-element.35.above, f32[11,8,128]{2,1,0:T(8,128)S(1)} %get-tuple-element.34.below, ...), custom_call_target="tpu_custom_call" | custom-call | tf_op jit(solution)/shard_map/pallas_call | solution.py:385
  (14 shorter events, 0.1 us)
Async XLA Ops:
  3.3 5.6 %copy-start.1 = (f32[64,128]{1,0:T(8,128)S(1)}, f32[64,128]{1,0:T(8,128)}, u32[]{:S(2)}) copy-start(f32[64,128]{1,0:T(8,128)} %kappa) | copy-start | bytes 98308
  3.3 23.9 %all-to-all-start.1 = ((bf16[16,10,8,512]{3,2,1,0:T(8,128)(2,1)}), bf16[16,10,8,512]{3,2,1,0:T(8,128)(2,1)S(1)}, u32[]{:S(2)}, u32[]{:S(2)}) async-start(bf16[16,10,8,512]{3,2,1,0:T(8,128)(2,1)} %shard_map.91), calls=%async_computation.1 | async-start | bytes 2621440 | tf_op jit(solution)/shard_map/all_to_all | solution.py:369
  8.9 13.9 %collective-permute-start.1 = (f32[64,128]{1,0:T(8,128)S(1)}, f32[64,128]{1,0:T(8,128)S(1)}, u32[]{:S(2)}, u32[]{:S(2)}) collective-permute-start(f32[64,128]{1,0:T(8,128)S(1)} %copy-done.1), channel_id=1, source_target_pairs={{0,4},{4,0},{8,12},{12,8},{16,20},{20,16},{24,28},{28,24},{1,5},{5... | collective-permute-start | bytes 98312 | tf_op jit(solution)/shard_map/ppermute | solution.py:275
  9.1 16.9 %collective-permute-start = (f32[64,128]{1,0:T(8,128)S(1)}, f32[64,128]{1,0:T(8,128)S(1)}, u32[]{:S(2)}, u32[]{:S(2)}) collective-permute-start(f32[64,128]{1,0:T(8,128)S(1)} %copy-done.1), channel_id=1, source_target_pairs={{4,8},{12,16},{20,24},{8,4},{16,12},{24,20},{5,9},{13,17},{21,25},... | collective-permute-start | bytes 98312 | tf_op jit(solution)/shard_map/ppermute | solution.py:276
  27.3 22.8 %all-to-all-start = ((bf16[16,10,8,512]{3,2,1,0:T(8,128)(2,1)}), bf16[16,10,8,512]{3,2,1,0:T(8,128)(2,1)S(1)}, u32[]{:S(2)}, u32[]{:S(2)}) async-start(bf16[16,10,8,512]{3,2,1,0:T(8,128)(2,1)} %shard_map.92), calls=%async_computation | async-start | bytes 2621440 | tf_op jit(solution)/shard_map/all_to_all | solution.py:374
  38.9 18.0 %collective-permute-start.2 = (f32[72,8,128]{2,1,0:T(8,128)S(1)}, f32[72,8,128]{2,1,0:T(8,128)S(1)}, u32[]{:S(2)}, u32[]{:S(2)}) collective-permute-start(f32[72,8,128]{2,1,0:T(8,128)S(1)} %shard_map.94), channel_id=1, source_target_pairs={{0,24},{4,28},{8,16},{12,20},{16,8},{20,12},{24,0},{28,4},{1,25},{... | collective-permute-start | bytes 884744 | tf_op jit(solution)/shard_map/ppermute | solution.py:377
  39.0 17.8 %copy-start = (f32[8,64,128]{2,1,0:T(8,128)S(1)}, f32[8,64,128]{2,1,0:T(8,128)}, u32[]{:S(2)}) copy-start(f32[8,64,128]{2,1,0:T(8,128)} %land_flux.1) | copy-start | bytes 786436
  39.0 17.8 %copy-start.2 = (f32[64,128]{1,0:T(8,128)S(1)}, f32[64,128]{1,0:T(8,128)}, u32[]{:S(2)}) copy-start(f32[64,128]{1,0:T(8,128)} %land_area.1) | copy-start | bytes 98308
  57.0 5.6 %collective-permute-start.4 = (f32[64,128]{1,0:T(8,128)S(1)}, f32[64,128]{1,0:T(8,128)S(1)}, u32[]{:S(2)}, u32[]{:S(2)}) collective-permute-start(f32[64,128]{1,0:T(8,128)S(1)} %get-tuple-element.28), channel_id=1, source_target_pairs={{4,8},{12,16},{20,24},{8,4},{16,12},{24,20},{5,9},{13,17},{21,25},... | collective-permute-start | bytes 98312 | tf_op jit(solution)/shard_map/ppermute | solution.py:276
  59.8 3.1 %collective-permute-start.3 = (f32[64,128]{1,0:T(8,128)S(1)}, f32[64,128]{1,0:T(8,128)S(1)}, u32[]{:S(2)}, u32[]{:S(2)}) collective-permute-start(f32[64,128]{1,0:T(8,128)S(1)} %get-tuple-element.28), channel_id=1, source_target_pairs={{0,4},{4,0},{8,12},{12,8},{16,20},{20,16},{24,28},{28,24},{1,5},{5... | collective-permute-start | bytes 98312 | tf_op jit(solution)/shard_map/ppermute | solution.py:275
  63.0 8.8 %collective-permute-start.6 = (f32[11,8,128]{2,1,0:T(8,128)S(1)}, f32[11,8,128]{2,1,0:T(8,128)S(1)}, u32[]{:S(2)}, u32[]{:S(2)}) collective-permute-start(f32[11,8,128]{2,1,0:T(8,128)S(1)} %pad_maximum_fusion), channel_id=1, source_target_pairs={{1,2},{2,1},{5,6},{6,5},{9,10},{10,9},{13,14},{14,13},{17,18},{18,... | collective-permute-start | bytes 135176 | tf_op jit(solution)/shard_map/ppermute | solution.py:276
  67.2 5.5 %collective-permute-start.5 = (f32[11,8,128]{2,1,0:T(8,128)S(1)}, f32[11,8,128]{2,1,0:T(8,128)S(1)}, u32[]{:S(2)}, u32[]{:S(2)}) collective-permute-start(f32[11,8,128]{2,1,0:T(8,128)S(1)} %pad_maximum_fusion), channel_id=1, source_target_pairs={{0,1},{1,0},{2,3},{3,2},{4,5},{5,4},{6,7},{7,6},{8,9},{9,8},{10,11... | collective-permute-start | bytes 135176 | tf_op jit(solution)/shard_map/ppermute | solution.py:275

commit v3 on v2

--- a/solution.py
+++ b/solution.py
@@ -13,13 +13,14 @@
 SWEEPS = 3
 LAYERS = 4
 EDGE = 4
-LANE_BLOCK = 16
+LANE_BLOCK = 14
 
 BF16 = jnp.bfloat16
 F32 = jnp.float32
 I32 = jnp.int32
 VMEM = pl.BlockSpec(memory_space=pltpu.VMEM)
 HBM = pl.BlockSpec(memory_space=pltpu.HBM)
+ANY = pl.BlockSpec(memory_space=pl.ANY)
 
 
 def iota(shape, dim):
@@ -30,13 +31,19 @@
     return pltpu.CompilerParams(vmem_limit_bytes=megabytes << 20)
 
 
-def pack_kernel(
-    cap,
-    mirror,
-    *refs,
-):
-    given, out, held, out_held = refs[:7], refs[7], refs[8:15], refs[15]
-    count, source, in_sems, out_sems = refs[16:]
+def parity(number):
+    for shift in (16, 8, 4, 2, 1):
+        number = number ^ (number >> shift)
+    return number & 1
+
+
+def carried(position, core):
+    return 2 * position + (parity(position) ^ 1 ^ core)
+
+
+def pack_kernel(cap, near, mirror, *refs):
+    given, outs, held, out_held = refs[:7], refs[7:-12], refs[-12:-5], refs[-5]
+    count, source, in_sems, out_sems = refs[-4:]
     copies = [
         pltpu.make_async_copy(given[i], held[i], in_sems.at[i]) for i in range(len(given))
     ]
@@ -46,7 +53,26 @@
     crossings, tiles = dest_v.shape
     half, cells = out_held.shape[0], fields.shape[2]
     owners, slots = 2 * half, half * cap
-    first = lax.axis_index("gx") // (lax.axis_size("gx") // 2) * half
+    me = lax.axis_index("gx") * lax.axis_size("gy") + lax.axis_index("gy")
+    first = me // half * half
+    here = me - first
+    core = here & 1
+
+    def block_of(owner):
+        if not near:
+            return (owner ^ mirror) - first
+        index = owner - first
+        distance = (index ^ here) >> 1
+        carrier = 1 - parity(distance)
+        block = (carrier ^ core) * (half // 2) + (distance >> 1) * 2 + ((index & 1) ^ carrier)
+        return jnp.where((index >= 0) & (index < half), block, -1)
+
+    def owner_of(block):
+        if not near:
+            return (first + block) ^ mirror
+        carrier = core ^ (block // (half // 2))
+        distance = carried((block % (half // 2)) >> 1, carrier)
+        return first + (((here >> 1) ^ distance) << 1) + ((block & 1) ^ carrier)
 
     for d in range(owners):
         count[d] = 0
@@ -82,8 +108,7 @@
         earlier = jnp.dot(hot.astype(BF16), before, preferred_element_type=F32) + offset
         offset = offset + jnp.sum(hot, axis=1, keepdims=True)
         within = jnp.sum(hot * earlier, axis=0, keepdims=True).astype(I32)
-        place = ((dest ^ mirror) - first) * cap + within
-        chosen = (iota((slots, tiles), 0) == place).astype(BF16)
+        chosen = (iota((slots, tiles), 0) == block_of(dest) * cap + within).astype(BF16)
         scale = jnp.ones(dest.shape, F32)
         for bit in (1, 2, 4):
             scale = scale * jnp.where((tile_v[k : k + 1, :] & bit) != 0, 2.0 ** (8 * bit), 1.0)
@@ -106,33 +131,36 @@
             out_held[g, row] = rows if cap == 8 else jnp.concatenate([rows, spare], axis=0)
 
     copies[6].wait()
-    parts = out_sems.shape[0]
-    step = half // parts
+    step = half // out_sems.shape[0]
     sent = []
-    for part in range(parts):
+    for part in range(out_sems.shape[0]):
 
         def fill(g, carry):
-            owner = (first + g) ^ mirror
+            owner = owner_of(g)
             for n in range(cap):
                 out_held[g, n] = fields[source[owner * cap + n]]
             return carry
 
         lax.fori_loop(part * step, (part + 1) * step, fill, 0, unroll=2)
         block = pl.ds(part * step, step)
-        sent.append(pltpu.make_async_copy(out_held.at[block], out.at[block], out_sems.at[part]))
+        out = outs[part * step // outs[0].shape[0]]
+        into = out.at[pl.ds(part * step % out.shape[0], step)]
+        sent.append(pltpu.make_async_copy(out_held.at[block], into, out_sems.at[part]))
         sent[-1].start()
     for copy in sent:
         copy.wait()
 
 
-def pack(dest, tile, target, weight, mask, fields, cap, owners, mirror):
-    shape = (owners // 2, cap + 2) + fields.shape[1:]
+def pack(dest, tile, target, weight, mask, fields, cap, owners, near, mirror):
+    half = owners // 2
+    shape = (half, cap + 2) + fields.shape[1:]
+    parts = 2 if near else 1
     given = (dest, dest, tile, target, weight, mask, fields)
     return pl.pallas_call(
-        functools.partial(pack_kernel, cap, mirror),
-        out_shape=jax.ShapeDtypeStruct(shape, BF16),
+        functools.partial(pack_kernel, cap, near, mirror),
+        out_shape=[jax.ShapeDtypeStruct((half // parts,) + shape[1:], BF16)] * parts,
         in_specs=[HBM] * len(given),
-        out_specs=HBM,
+        out_specs=[HBM] * parts,
         scratch_shapes=[pltpu.SMEM(dest.shape, I32)]
         + [pltpu.VMEM(a.shape, a.dtype) for a in given[1:]]
         + [
@@ -149,6 +177,45 @@
     )(*given)
 
 
+def join_kernel(kept, taken, *refs):
+    outs, (held, in_sems, out_sems) = refs[:-3], refs[-3:]
+    arriving = []
+    for j in range(len(outs)):
+        for rel in range(2):
+            for src, blocks in enumerate((kept, taken)):
+                at = 4 * j + 2 * rel + src
+                copy = pltpu.make_async_copy(blocks.at[2 * j + rel], held.at[at], in_sems.at[at])
+                copy.start()
+                arriving.append(copy)
+    leaving = []
+    for j, out in enumerate(outs):
+        for copy in arriving[4 * j : 4 * j + 4]:
+            copy.wait()
+        leaving.append(pltpu.make_async_copy(held.at[pl.ds(4 * j, 4)], out, out_sems.at[j]))
+        leaving[-1].start()
+    for copy in leaving:
+        copy.wait()
+
+
+def join(kept, taken):
+    number = taken.shape[0] // 2
+    return pl.pallas_call(
+        join_kernel,
+        out_shape=[jax.ShapeDtypeStruct((4,) + taken.shape[1:], BF16)] * number,
+        in_specs=[HBM] * 2,
+        out_specs=[HBM] * number,
+        scratch_shapes=[
+            pltpu.VMEM((4 * number,) + taken.shape[1:], BF16),
+            pltpu.SemaphoreType.DMA((4 * number,)),
+            pltpu.SemaphoreType.DMA((number,)),
+        ],
+        compiler_params=params(62),
+        cost_estimate=pl.CostEstimate(
+            flops=0, bytes_accessed=4 * taken.size * 2, transcendentals=0
+        ),
+    )(kept, taken)
+
+
 def decode(code):
     tile = jnp.zeros(code.shape, I32)
     for k in range(1, 8):
@@ -163,11 +230,38 @@
     return tile, row, lax.shift_right_logical(cell, row) - ATM_COLS
 
 
-def bin_slots(cap, slots, total):
+def bin_slots(cap, picked, earlier, *refs):
+    arrays = len(refs) - 2 - (2 if earlier else 1) * len(picked)
+    given, refs = refs[:arrays], refs[arrays:]
+    before = refs[: len(picked)] if earlier else ()
+    totals = refs[len(before) : len(before) + len(picked)]
+    slots, sems = refs[-2:]
+    copies, bounds = [], []
+    for pick in picked:
+        low = sum(copy[2] for copy in copies)
+        for array, first, number in pick:
+            at = sum(copy[2] for copy in copies)
+            copies.append((array, first, number, at))
+        bounds.append((low, sum(copy[2] for copy in copies)))
+    started = []
+    for i, (array, first, number, at) in enumerate(copies):
+        copy = pltpu.make_async_copy(
+            given[array].at[pl.ds(first, number)], slots.at[pl.ds(at, number)], sems.at[i]
+        )
+        copy.start()
+        started.append(copy)
+    for i, total in enumerate(totals):
+        total[...] = before[i][...] if earlier else jnp.zeros_like(total)
+    for copy in started:
+        copy.wait()
+    for total, (low, high) in zip(totals, bounds, strict=True):
+        bin_range(cap, slots, low, high, total)
+
+
+def bin_range(cap, slots, low, high, total):
     sources, _, field_count, cells = slots.shape
     rows_here = total.shape[0] * TILE_ROWS // (TILE_ROWS + 1)
     zero = jnp.zeros((), BF16)
-    total[...] = jnp.zeros_like(total)
 
     def source(g, carry):
         weight = slots[g, cap].astype(F32)
@@ -208,59 +302,67 @@
             )
         return carry
 
-    lax.fori_loop(0, sources, source, 0, unroll=2)
-
-
-def merge_kernel(total, passed, land_flux, land_area, merged, strips, edges):
+    lax.fori_loop(low, high, source, 0, unroll=2 if (high - low) % 2 == 0 else 1)
+
+
+def merge_kernel(total, other, passed, land_flux, land_area, kappa, merged, strips, edges):
     field_count, rows_here, cols_here = land_flux.shape
     area = land_area[...]
-    denom = (total[rows_here:] + passed[rows_here:]).reshape(rows_here, cols_here) + area
+    denom = total[rows_here:] + other[rows_here:] + passed[rows_here:]
+    denom = denom.reshape(rows_here, cols_here) + area
     lane = iota((rows_here, cols_here), 1)
     border = (lane < SWEEPS) | (lane >= cols_here - SWEEPS)
-    numer = jnp.swapaxes(total[:rows_here] + passed[:rows_here], 0, 1)
+    numer = total[:rows_here] + other[:rows_here] + passed[:rows_here]
+    numer = jnp.swapaxes(numer, 0, 1)
     packed = jnp.zeros((rows_here, cols_here), F32)
-    for f in range(field_count):
-        value = (numer[f] + area * land_flux[f]) / denom
-        merged[f] = value
+    for f in range(field_count + 1):
+        if f < field_count:
+            value = (numer[f] + area * land_flux[f]) / denom
+            merged[f] = value
+        else:
+            value = kappa[...]
         edges[f] = jnp.concatenate([value[:EDGE], value[rows_here - EDGE :]], axis=0)
         strip = jnp.where(border, value, 0.0)
         packed = packed + (pltpu.roll(strip, f * LANE_BLOCK, 1) if f else strip)
     strips[...] = packed
 
 
-def cost(slots):
-    sources, _, field_count, cells = slots.shape
+def bin_all(arrays, picked, earlier, cap, rows_here):
+    _, rows, field_count, cells = arrays[0].shape
+    shape = (rows_here // TILE_ROWS * (TILE_ROWS + 1), field_count, ATM_COLS)
+    number = sum(part[2] for pick in picked for part in pick)
     each = 2 * (field_count + 1) * TILE_ROWS * cells * ATM_COLS
-    return pl.CostEstimate(
-        flops=sources * 8 * each, bytes_accessed=slots.size * 2, transcendentals=0
-    )
-
-
-def bin_all(slots, cap, rows_here, field_count):
-    shape = (rows_here // TILE_ROWS * (TILE_ROWS + 1), field_count, ATM_COLS)
     return pl.pallas_call(
-        functools.partial(bin_slots, cap),
-        out_shape=jax.ShapeDtypeStruct(shape, F32),
-        in_specs=[VMEM],
-        out_specs=VMEM,
+        functools.partial(bin_slots, cap, picked, bool(earlier)),
+        out_shape=[jax.ShapeDtypeStruct(shape, F32)] * len(picked),
+        in_specs=[ANY] * len(arrays) + [VMEM] * len(earlier),
+        out_specs=[VMEM] * len(picked),
+        scratch_shapes=[
+            pltpu.VMEM((number,) + arrays[0].shape[1:], BF16),
+            pltpu.SemaphoreType.DMA((sum(len(pick) for pick in picked),)),
+        ],
         compiler_params=params(),
-        cost_estimate=cost(slots),
-    )(slots)
-
-
-def merge(total, passed, land_flux, land_area):
+        cost_estimate=pl.CostEstimate(
+            flops=number * 8 * each,
+            bytes_accessed=number * rows * field_count * cells * 2,
+            transcendentals=0,
+        ),
+    )(*arrays, *earlier)
+
+
+def merge(total, other, passed, land_flux, land_area, kappa):
     field_count, rows_here, cols_here = land_flux.shape
     return pl.pallas_call(
         merge_kernel,
         out_shape=[
             jax.ShapeDtypeStruct(land_flux.shape, F32),
             jax.ShapeDtypeStruct((rows_here, cols_here), F32),
-            jax.ShapeDtypeStruct((field_count, 2 * EDGE, cols_here), F32),
+            jax.ShapeDtypeStruct((field_count + 1, 2 * EDGE, cols_here), F32),
         ],
-        in_specs=[VMEM] * 4,
+        in_specs=[VMEM] * 6,
         out_specs=[VMEM] * 3,
         compiler_params=params(),
-    )(total, passed, land_flux, land_area)
+    )(total, other, passed, land_flux, land_area, kappa)
 
 
 def swaps(axis):
@@ -278,9 +380,9 @@
     return jnp.where(odd, one, two), jnp.where(odd, two, one)
 
 
-def select_columns(before, after, block):
-    lane = iota(before.shape, 1) % block
-    return jnp.where(lane < block // 2, after, before)
+def select_columns(before, after):
+    lane = (iota(before.shape, 1) + SWEEPS) % before.shape[1] % LANE_BLOCK
+    return jnp.where(lane < SWEEPS, before, after)
 
 
 def ends(values):
@@ -291,7 +393,7 @@
 NEIGHBOURS = ((-1, 0), (1, 0), (-1, 1), (1, 1))
 
 
-def sweep_kernel(merged, before, after, above, below, kappa, k_columns, out):
+def sweep_kernel(merged, before, after, above, below, kappa, out):
     field_count, rows_here, cols_here = merged.shape
 
     def near(values, i):
@@ -301,28 +403,24 @@
     def halo_rows(i):
         return jnp.concatenate([below[i][:EDGE], above[i][EDGE:]], axis=0)
 
-    def whole(cells, rows, columns, corners):
-        lane = iota((rows_here + 2 * EDGE, cols_here), 1)
-        border = (lane < SWEEPS) | (lane >= cols_here - SWEEPS)
+    columns = select_columns(before[...], after[...])
+    corners = halo_rows(field_count + 1)
+    lane = iota((rows_here + 2 * EDGE, cols_here), 1)
+    border = (lane < SWEEPS) | (lane >= cols_here - SWEEPS)
+
+    def whole(cells, f):
         side = jnp.concatenate([columns, corners], axis=0)
+        side = pltpu.roll(side, (cols_here - f * LANE_BLOCK) % cols_here, 1) if f else side
         return jnp.concatenate(
-            [jnp.concatenate([cells, rows], axis=0), jnp.where(border, side, 0.0)], axis=1
+            [jnp.concatenate([cells, halo_rows(f)], axis=0), jnp.where(border, side, 0.0)], axis=1
         )
 
-    k = whole(kappa[...], halo_rows(field_count + 1), k_columns[...], halo_rows(field_count + 2))
+    k = whole(kappa[...], field_count)
     coefficients = [
         jnp.where(k > 0.0, 0.5 * (k + near(k, i)), 0.0) for i in range(len(NEIGHBOURS))
     ]
-    columns = select_columns(before[...], after[...], LANE_BLOCK)
-    corners = halo_rows(field_count)
     for f in range(field_count):
-        shift = (cols_here - f * LANE_BLOCK) % cols_here
-        u = whole(
-            merged[f],
-            halo_rows(f),
-            pltpu.roll(columns, shift, 1) if f else columns,
-            pltpu.roll(corners, shift, 1) if f else corners,
-        )
+        u = whole(merged[f], f)
         for _ in range(SWEEPS):
             new = u
             for i, coefficient in enumerate(coefficients):
@@ -364,31 +462,37 @@
         axis_index_groups=halves,
         tiled=True,
     )
-    far_slots = pack(*pairs, cap, device_count, mirror)
-    pairs, kappa, far_slots = lax.optimization_barrier((pairs, kappa, far_slots))
+    half = device_count // 2
+    everywhere = range(device_count)
+    far_slots = pack(*pairs, cap, device_count, False, mirror)[0]
+    pairs, far_slots = lax.optimization_barrier((pairs, far_slots))
     far_got = exchange(far_slots)
-    near_slots = pack(*pairs, cap, device_count, 0)
-    k_columns = select_columns(*neighbours(kappa, "gx"), cols_here)
-    near_slots, k_columns = lax.optimization_barrier((near_slots, k_columns))
-
-    near_got = exchange(near_slots)
-    far_total = bin_all(far_got, cap, rows_here, field_count)
+    kept, given = pack(*pairs, cap, device_count, True, 0)
+    taken = lax.ppermute(given, ("gx", "gy"), [(i, i ^ 1) for i in everywhere])
+    got = [
+        lax.ppermute(message, ("gx", "gy"), [(i, i ^ 2 * carried(j, i & 1)) for i in everywhere])
+        for j, message in enumerate(join(kept, taken))
+    ]
+
+    far_total = bin_all([far_got], [[(0, 0, half)]], [], cap, rows_here)[0]
     opposite = [(i, i ^ (mirror // width_y)) for i in range(width_x)]
     passed = lax.ppermute(far_total, "gx", opposite)
-    total = bin_all(near_got, cap, rows_here, field_count)
-
-    merged, strips, edges = merge(total, passed, land_flux, land_area)
+    got, far_total = lax.optimization_barrier((got, far_total))
+    other = bin_all(got, [[(j, 2, 2) for j in range(len(got))]], [], cap, rows_here)[0]
+    other = lax.ppermute(other, ("gx", "gy"), [(i, i ^ 1) for i in everywhere])
+    total = bin_all(got, [[(j, 0, 2) for j in range(len(got))]], [], cap, rows_here)[0]
+
+    merged, strips, edges = merge(total, other, passed, land_flux, land_area, kappa)
     before, after = neighbours(strips, "gx")
-    corners = ends(select_columns(before, after, LANE_BLOCK))
-    rows = jnp.concatenate([edges, corners[None], ends(kappa)[None], ends(k_columns)[None]], axis=0)
-    above, below = neighbours(rows, "gy")
+    corners = ends(select_columns(before, after))
+    above, below = neighbours(jnp.concatenate([edges, corners[None]], axis=0), "gy")
     return pl.pallas_call(
         sweep_kernel,
         out_shape=jax.ShapeDtypeStruct(merged.shape, F32),
-        in_specs=[VMEM] * 7,
+        in_specs=[VMEM] * 6,
         out_specs=VMEM,
         compiler_params=params(),
-    )(merged, before, after, above, below, kappa, k_columns)
+    )(merged, before, after, above, below, kappa)
 
 
 def solution(mesh):

time: 76.1 us -> 67.9 us (0.89)
  waiting for transfers between devices: 25.6 us -> 17.3 us
  starting transfers between devices: 26.5 us -> 21.5 us
  Pallas kernels: 23.4 us -> 27.6 us
  local copies, waits for them, and re-layouts: 0.03 us -> 0.85 us
    all_to_all x1 -> x0, waiting for transfers between devices: 11.1 us -> none  [shards(): near_got = exchange(near_slots)]
    ppermute x0 -> x6, waiting for transfers between devices: none -> 8.36 us  [the longest x4 6.41 us: shards(): lax.ppermute(message, ('gx', 'gy'), [(i, i ^ 2 * carried(j, i & 1)) for i...]
    ppermute x3 -> x2, waiting for transfers between devices: 7.39 us -> 0.8 us  [neighbours(): one = lax.ppermute(values, axis, first)]
    ppermute x0 -> x6, starting transfers between devices: none -> 6.31 us  [the longest x4 5.18 us: shards(): lax.ppermute(message, ('gx', 'gy'), [(i, i ^ 2 * carried(j, i & 1)) for i...]
    all_to_all x1 -> x0, starting transfers between devices: 4.78 us -> none  [shards(): near_got = exchange(near_slots)]
    ppermute x3 -> x2, starting transfers between devices: 4.87 us -> 0.14 us  [neighbours(): one = lax.ppermute(values, axis, first)]
    pallas_call x4 -> x6, Pallas kernels: 20.2 us -> 24.4 us  [the longest x3 15.4 us: bin_all(): pl.pallas_call(functools.partial(bin_slots, cap, picked, bool(earlier)),...]
    ppermute x3 -> x2, starting transfers between devices: 11.1 us -> 8.15 us  [neighbours(): two = lax.ppermute(values, axis, second)]
  transfers between devices with their start and end apart: 9 -> 12, of which waited for: 7 -> 6; matrix products, arithmetic and copies ran while one was open for 0% -> 0% of each run, Pallas kernels for 22% -> 31%
where the time goes in v3:
time: 67.9 us; the launch traced here: 67.5 us
  Pallas kernels  27.6 us (41%)
  starting transfers between devices  21.5 us (32%)
  waiting for transfers between devices  17.3 us (25%)
  local copies, waits for them, and re-layouts  0.85 us (1%)
    pallas_call x3, Pallas kernels, bin_all(): pl.pallas_call(functools.partial(bin_slots, cap, picked, bool(earlier)),...  15.4 us
    ppermute x2, starting transfers between devices, neighbours(): two = lax.ppermute(values, axis, second)  8.15 us
    pallas_call x2, Pallas kernels, pack(): pl.pallas_call(functools.partial(pack_kernel, cap, near, mirror), out_sha...  6.69 us
    ppermute x4, waiting for transfers between devices, shards(): lax.ppermute(message, ('gx', 'gy'), [(i, i ^ 2 * carried(j, i & 1)) for i...  6.41 us
    all_to_all x1, starting transfers between devices, shards(): far_got = exchange(far_slots)  5.58 us
    ppermute x4, starting transfers between devices, shards(): lax.ppermute(message, ('gx', 'gy'), [(i, i ^ 2 * carried(j, i & 1)) for i...  5.18 us
    all_to_all x1, waiting for transfers between devices, shards(): far_got = exchange(far_slots)  4.23 us
    ppermute x2, waiting for transfers between devices, neighbours(): two = lax.ppermute(values, axis, second)  3.92 us
  transfers between devices with their start and end apart: 12, of which 6 were waited for; matrix products, arithmetic and copies ran while one was open for 0% of the time, Pallas kernels for 31%

profile of v3, /device:TPU:21, one launch (start us, length us, event | category | flops | bytes accessed | tf_op | source)
XLA Modules:
  0.0 67.5 jit_solution(9376912913169760519)
XLA Ops:
  0.0 3.3 %shard_map.91 = bf16[16,10,8,512]{3,2,1,0:T(8,128)(2,1)} custom-call(s32[2,64]{1,0:T(2,128)} %bitcast.4, s32[2,64]{1,0:T(2,128)} %bitcast.5, s32[2,64]{1,0:T(2,128)} %bitcast.8, s32[64,2,512]{2,1,0:T(2,128)} %refs_3_.2, bf16[64,2,512]{2,1,0:T(2,128)(2,1)} %refs_4_.2, s32[64,512]{1,0:T(8,128)} %refs_5_.2, bf16[64,8,512]{2,1,0:T(8,128)(2,1)} %refs_6_.2), custom_call_target="tpu_custom_call" | custom-call | flops 100000000 | bytes 4000000 | tf_op jit(solution)/shard_map/pallas_call | solution.py:159
  3.3 5.6 %all-to-all-start = ((bf16[16,10,8,512]{3,2,1,0:T(8,128)(2,1)}), bf16[16,10,8,512]{3,2,1,0:T(8,128)(2,1)S(1)}, u32[]{:S(2)}, u32[]{:S(2)}) async-start(bf16[16,10,8,512]{3,2,1,0:T(8,128)(2,1)} %shard_map.91), calls=%async_computation | async-start | bytes 2621440 | tf_op jit(solution)/shard_map/all_to_all | solution.py:469
  8.9 3.4 %shard_map.92 = (bf16[8,10,8,512]{3,2,1,0:T(8,128)(2,1)}, bf16[8,10,8,512]{3,2,1,0:T(8,128)(2,1)}) custom-call(s32[2,64]{1,0:T(2,128)} %bitcast.6, s32[2,64]{1,0:T(2,128)} %bitcast.7, s32[2,64]{1,0:T(2,128)} %bitcast.9, s32[64,2,512]{2,1,0:T(2,128)} %refs_3_.2, bf16[64,2,512]{2,1,0:T(2,128)(2,1)} %refs_4_.2, s32[64,512]{1,0:T(8,128)} %refs_5_.2, ...), custom_call_target="tpu_custom_call" | custom-call | flops 100000000 | bytes 4000000 | tf_op jit(solution)/shard_map/pallas_call | solution.py:159
  12.3 0.4 collective-permute-start
  12.7 1.9 %collective-permute-done.taken = bf16[8,10,8,512]{3,2,1,0:T(8,128)(2,1)S(1)} collective-permute-done((bf16[8,10,8,512]{3,2,1,0:T(8,128)(2,1)}, bf16[8,10,8,512]{3,2,1,0:T(8,128)(2,1)S(1)}, u32[]{:S(2)}, u32[]{:S(2)}) %collective-permute-start) | collective-permute-done | bytes 655392 | tf_op jit(solution)/shard_map/ppermute | solution.py:471
  14.7 0.8 %copy-done.3 = bf16[8,10,8,512]{3,2,1,0:T(8,128)(2,1)} copy-done((bf16[8,10,8,512]{3,2,1,0:T(8,128)(2,1)}, bf16[8,10,8,512]{3,2,1,0:T(8,128)(2,1)S(1)}, u32[]{:S(2)}) %copy-start.3) | copy-done | bytes 655384
  15.5 2.3 %shard_map.93 = (bf16[4,10,8,512]{3,2,1,0:T(8,128)(2,1)}, bf16[4,10,8,512]{3,2,1,0:T(8,128)(2,1)}, bf16[4,10,8,512]{3,2,1,0:T(8,128)(2,1)}, bf16[4,10,8,512]{3,2,1,0:T(8,128)(2,1)}) custom-call(bf16[8,10,8,512]{3,2,1,0:T(8,128)(2,1)} %get-tuple-element.31.kept, bf16[8,10,8,512]{3,2,1,0:T(8,128)(2,1)} %copy-done.3), custom_call_target="tpu_custom_call" | custom-call | bytes 2621440 | tf_op jit(solution)/shard_map/pallas_call | solution.py:202
  17.8 1.6 %collective-permute-start.1 = (bf16[4,10,8,512]{3,2,1,0:T(8,128)(2,1)}, bf16[4,10,8,512]{3,2,1,0:T(8,128)(2,1)S(1)}, u32[]{:S(2)}, u32[]{:S(2)}) collective-permute-start(bf16[4,10,8,512]{3,2,1,0:T(8,128)(2,1)} %get-tuple-element.33), channel_id=1, source_target_pairs={{0,2},{1,1},{2,0},{3,3},{4,6},{5,5},{6,4},{7,7},{8,10},{9,9},{10,8... | collective-permute-start | bytes 983048 | tf_op jit(solution)/shard_map/ppermute | solution.py:473
  19.4 1.2 %collective-permute-start.2 = (bf16[4,10,8,512]{3,2,1,0:T(8,128)(2,1)}, bf16[4,10,8,512]{3,2,1,0:T(8,128)(2,1)S(1)}, u32[]{:S(2)}, u32[]{:S(2)}) collective-permute-start(bf16[4,10,8,512]{3,2,1,0:T(8,128)(2,1)} %get-tuple-element.34), channel_id=1, source_target_pairs={{0,4},{1,7},{2,6},{3,5},{4,0},{5,3},{6,2},{7,1},{8,12},{9,15},{10,... | collective-permute-start | bytes 983048 | tf_op jit(solution)/shard_map/ppermute | solution.py:473
  20.6 1.2 %collective-permute-start.3 = (bf16[4,10,8,512]{3,2,1,0:T(8,128)(2,1)}, bf16[4,10,8,512]{3,2,1,0:T(8,128)(2,1)S(1)}, u32[]{:S(2)}, u32[]{:S(2)}) collective-permute-start(bf16[4,10,8,512]{3,2,1,0:T(8,128)(2,1)} %get-tuple-element.35), channel_id=1, source_target_pairs={{0,8},{1,11},{2,10},{3,9},{4,12},{5,15},{6,14},{7,13},{8,0},{9,3},... | collective-permute-start | bytes 983048 | tf_op jit(solution)/shard_map/ppermute | solution.py:473
  21.8 1.2 %collective-permute-start.4 = (bf16[4,10,8,512]{3,2,1,0:T(8,128)(2,1)}, bf16[4,10,8,512]{3,2,1,0:T(8,128)(2,1)S(1)}, u32[]{:S(2)}, u32[]{:S(2)}) collective-permute-start(bf16[4,10,8,512]{3,2,1,0:T(8,128)(2,1)} %get-tuple-element.36), channel_id=1, source_target_pairs={{0,14},{1,13},{2,12},{3,15},{4,10},{5,9},{6,8},{7,11},{8,6},{9,5},... | collective-permute-start | bytes 983048 | tf_op jit(solution)/shard_map/ppermute | solution.py:473
  23.0 4.2 %all-to-all-done.refs_0_ = bf16[16,10,8,512]{3,2,1,0:T(8,128)(2,1)S(1)} async-done(((bf16[16,10,8,512]{3,2,1,0:T(8,128)(2,1)}), bf16[16,10,8,512]{3,2,1,0:T(8,128)(2,1)S(1)}, u32[]{:S(2)}, u32[]{:S(2)}) %all-to-all-start) | async-done | bytes 1310752 | tf_op jit(solution)/shard_map/all_to_all | solution.py:469
  27.2 6.9 %shard_map.94 = f32[72,8,128]{2,1,0:T(8,128)S(1)} custom-call(bf16[16,10,8,512]{3,2,1,0:T(8,128)(2,1)S(1)} %all-to-all-done.refs_0_), custom_call_target="tpu_custom_call" | custom-call | flops 1207959552 | bytes 1310720 | tf_op jit(solution)/shard_map/pallas_call | solution.py:335
  34.1 1.3 %collective-permute-start.6 = (f32[72,8,128]{2,1,0:T(8,128)S(1)}, f32[72,8,128]{2,1,0:T(8,128)S(1)}, u32[]{:S(2)}, u32[]{:S(2)}) collective-permute-start(f32[72,8,128]{2,1,0:T(8,128)S(1)} %shard_map.94), channel_id=1, source_target_pairs={{0,24},{4,28},{8,16},{12,20},{16,8},{20,12},{24,0},{28,4},{1,25},{... | collective-permute-start | bytes 884744 | tf_op jit(solution)/shard_map/ppermute | solution.py:479
  35.4 0.0 collective-permute-done.1.refs_0_
  35.4 6.4 %collective-permute-done.2.refs_1_ = bf16[4,10,8,512]{3,2,1,0:T(8,128)(2,1)S(1)} collective-permute-done((bf16[4,10,8,512]{3,2,1,0:T(8,128)(2,1)}, bf16[4,10,8,512]{3,2,1,0:T(8,128)(2,1)S(1)}, u32[]{:S(2)}, u32[]{:S(2)}) %collective-permute-start.2) | collective-permute-done | bytes 327712 | tf_op jit(solution)/shard_map/ppermute | solution.py:473
  41.8 4.3 %shard_map.96 = f32[72,8,128]{2,1,0:T(8,128)S(1)} custom-call(bf16[4,10,8,512]{3,2,1,0:T(8,128)(2,1)S(1)} %collective-permute-done.1.refs_0_, bf16[4,10,8,512]{3,2,1,0:T(8,128)(2,1)S(1)} %collective-permute-done.2.refs_1_, bf16[4,10,8,512]{3,2,1,0:T(8,128)(2,1)S(1)} %collective-permute-done.3.refs_2_, bf16[4,10,8,512]{3,2,1,0:T(8,128)(2,1)S(1)} %collective-permute-done.4.refs_3_), custom_call_target="tpu_custom_call" | custom-call | flops 603979776 | bytes 655360 | tf_op jit(solution)/shard_map/pallas_call | solution.py:335
  46.1 0.0 copy-start
  46.1 0.0 copy-start.1
  46.1 0.0 copy-start.2
  46.1 0.7 %collective-permute-start.5 = (f32[72,8,128]{2,1,0:T(8,128)S(1)}, f32[72,8,128]{2,1,0:T(8,128)S(1)}, u32[]{:S(2)}, u32[]{:S(2)}) collective-permute-start(f32[72,8,128]{2,1,0:T(8,128)S(1)} %shard_map.96), channel_id=1, source_target_pairs={{0,1},{1,0},{2,3},{3,2},{4,5},{5,4},{6,7},{7,6},{8,9},{9,8},{10,11... | collective-permute-start | bytes 884744 | tf_op jit(solution)/shard_map/ppermute | solution.py:482
  46.8 4.3 %shard_map.95.total = f32[72,8,128]{2,1,0:T(8,128)S(1)} custom-call(bf16[4,10,8,512]{3,2,1,0:T(8,128)(2,1)S(1)} %collective-permute-done.1.refs_0_, bf16[4,10,8,512]{3,2,1,0:T(8,128)(2,1)S(1)} %collective-permute-done.2.refs_1_, bf16[4,10,8,512]{3,2,1,0:T(8,128)(2,1)S(1)} %collective-permute-done.3.refs_2_, ...), custom_call_target="tpu_custom_call" | custom-call | flops 603979776 | bytes 655360 | tf_op jit(solution)/shard_map/pallas_call | solution.py:335
  51.1 0.0 collective-permute-done.6.passed
  51.1 0.2 shard_map.97
  51.3 3.1 %collective-permute-start.8 = (f32[64,128]{1,0:T(8,128)S(1)}, f32[64,128]{1,0:T(8,128)S(1)}, u32[]{:S(2)}, u32[]{:S(2)}) collective-permute-start(f32[64,128]{1,0:T(8,128)S(1)} %get-tuple-element.43), channel_id=1, source_target_pairs={{4,8},{12,16},{20,24},{8,4},{16,12},{24,20},{5,9},{13,17},{21,25},... | collective-permute-start | bytes 98312 | tf_op jit(solution)/shard_map/ppermute | solution.py:378
  54.5 0.1 collective-permute-start.7
  54.6 2.3 %collective-permute-done.8 = f32[64,128]{1,0:T(8,128)S(1)} collective-permute-done((f32[64,128]{1,0:T(8,128)S(1)}, f32[64,128]{1,0:T(8,128)S(1)}, u32[]{:S(2)}, u32[]{:S(2)}) %collective-permute-start.8) | collective-permute-done | bytes 32800 | tf_op jit(solution)/shard_map/ppermute | solution.py:378
  56.9 0.8 %collective-permute-done.7 = f32[64,128]{1,0:T(8,128)S(1)} collective-permute-done((f32[64,128]{1,0:T(8,128)S(1)}, f32[64,128]{1,0:T(8,128)S(1)}, u32[]{:S(2)}, u32[]{:S(2)}) %collective-permute-start.7) | collective-permute-done | bytes 32800 | tf_op jit(solution)/shard_map/ppermute | solution.py:377
  57.8 5.0 %collective-permute-start.10 = (f32[10,8,128]{2,1,0:T(8,128)S(1)}, f32[10,8,128]{2,1,0:T(8,128)S(1)}, u32[]{:S(2)}, u32[]{:S(2)}) collective-permute-start(f32[10,8,128]{2,1,0:T(8,128)S(1)} %pad_maximum_fusion), channel_id=1, source_target_pairs={{1,2},{2,1},{5,6},{6,5},{9,10},{10,9},{13,14},{14,13},{17,18},{18,... | collective-permute-start | bytes 122888 | tf_op jit(solution)/shard_map/ppermute | solution.py:378
  62.8 0.1 collective-permute-start.9
  62.9 1.6 %collective-permute-done.10 = f32[10,8,128]{2,1,0:T(8,128)S(1)} collective-permute-done((f32[10,8,128]{2,1,0:T(8,128)S(1)}, f32[10,8,128]{2,1,0:T(8,128)S(1)}, u32[]{:S(2)}, u32[]{:S(2)}) %collective-permute-start.10) | collective-permute-done | bytes 40992 | tf_op jit(solution)/shard_map/ppermute | solution.py:378
  64.5 3.0 %shard_map.98 = f32[8,64,128]{2,1,0:T(8,128)} custom-call(f32[8,64,128]{2,1,0:T(8,128)S(1)} %get-tuple-element.42.merged, f32[64,128]{1,0:T(8,128)S(1)} %get-tuple-element.47.before, f32[64,128]{1,0:T(8,128)S(1)} %get-tuple-element.46.after, f32[10,8,128]{2,1,0:T(8,128)S(1)} %get-tuple-element.49.above, f32[10,8,128]{2,1,0:T(8,128)S(1)} %get-tuple-element.48.below, ...), custom_call_target="tpu_custom_call" | custom-call | tf_op jit(solution)/shard_map/pallas_call | solution.py:489
  (15 shorter events, 0.1 us)
Async XLA Ops:
  3.3 23.9 %all-to-all-start = ((bf16[16,10,8,512]{3,2,1,0:T(8,128)(2,1)}), bf16[16,10,8,512]{3,2,1,0:T(8,128)(2,1)S(1)}, u32[]{:S(2)}, u32[]{:S(2)}) async-start(bf16[16,10,8,512]{3,2,1,0:T(8,128)(2,1)} %shard_map.91), calls=%async_computation | async-start | bytes 2621440 | tf_op jit(solution)/shard_map/all_to_all | solution.py:469
  12.3 2.4 %collective-permute-start = (bf16[8,10,8,512]{3,2,1,0:T(8,128)(2,1)}, bf16[8,10,8,512]{3,2,1,0:T(8,128)(2,1)S(1)}, u32[]{:S(2)}, u32[]{:S(2)}) collective-permute-start(bf16[8,10,8,512]{3,2,1,0:T(8,128)(2,1)} %get-tuple-element.32), channel_id=1, source_target_pairs={{0,1},{1,0},{2,3},{3,2},{4,5},{5,4},{6,7},{7,6},{8,9},{9,8},{10,11... | collective-permute-start | bytes 1966088 | tf_op jit(solution)/shard_map/ppermute | solution.py:471
  14.7 0.8 %copy-start.3 = (bf16[8,10,8,512]{3,2,1,0:T(8,128)(2,1)}, bf16[8,10,8,512]{3,2,1,0:T(8,128)(2,1)S(1)}, u32[]{:S(2)}) copy-start(bf16[8,10,8,512]{3,2,1,0:T(8,128)(2,1)S(1)} %collective-permute-done.taken) | copy-start | bytes 1966084
  17.8 17.6 %collective-permute-start.1 = (bf16[4,10,8,512]{3,2,1,0:T(8,128)(2,1)}, bf16[4,10,8,512]{3,2,1,0:T(8,128)(2,1)S(1)}, u32[]{:S(2)}, u32[]{:S(2)}) collective-permute-start(bf16[4,10,8,512]{3,2,1,0:T(8,128)(2,1)} %get-tuple-element.33), channel_id=1, source_target_pairs={{0,2},{1,1},{2,0},{3,3},{4,6},{5,5},{6,4},{7,7},{8,10},{9,9},{10,8... | collective-permute-start | bytes 983048 | tf_op jit(solution)/shard_map/ppermute | solution.py:473
  19.4 22.4 %collective-permute-start.2 = (bf16[4,10,8,512]{3,2,1,0:T(8,128)(2,1)}, bf16[4,10,8,512]{3,2,1,0:T(8,128)(2,1)S(1)}, u32[]{:S(2)}, u32[]{:S(2)}) collective-permute-start(bf16[4,10,8,512]{3,2,1,0:T(8,128)(2,1)} %get-tuple-element.34), channel_id=1, source_target_pairs={{0,4},{1,7},{2,6},{3,5},{4,0},{5,3},{6,2},{7,1},{8,12},{9,15},{10,... | collective-permute-start | bytes 983048 | tf_op jit(solution)/shard_map/ppermute | solution.py:473
  20.6 21.2 %collective-permute-start.3 = (bf16[4,10,8,512]{3,2,1,0:T(8,128)(2,1)}, bf16[4,10,8,512]{3,2,1,0:T(8,128)(2,1)S(1)}, u32[]{:S(2)}, u32[]{:S(2)}) collective-permute-start(bf16[4,10,8,512]{3,2,1,0:T(8,128)(2,1)} %get-tuple-element.35), channel_id=1, source_target_pairs={{0,8},{1,11},{2,10},{3,9},{4,12},{5,15},{6,14},{7,13},{8,0},{9,3},... | collective-permute-start | bytes 983048 | tf_op jit(solution)/shard_map/ppermute | solution.py:473
  21.8 20.0 %collective-permute-start.4 = (bf16[4,10,8,512]{3,2,1,0:T(8,128)(2,1)}, bf16[4,10,8,512]{3,2,1,0:T(8,128)(2,1)S(1)}, u32[]{:S(2)}, u32[]{:S(2)}) collective-permute-start(bf16[4,10,8,512]{3,2,1,0:T(8,128)(2,1)} %get-tuple-element.36), channel_id=1, source_target_pairs={{0,14},{1,13},{2,12},{3,15},{4,10},{5,9},{6,8},{7,11},{8,6},{9,5},... | collective-permute-start | bytes 983048 | tf_op jit(solution)/shard_map/ppermute | solution.py:473
  34.1 17.0 %collective-permute-start.6 = (f32[72,8,128]{2,1,0:T(8,128)S(1)}, f32[72,8,128]{2,1,0:T(8,128)S(1)}, u32[]{:S(2)}, u32[]{:S(2)}) collective-permute-start(f32[72,8,128]{2,1,0:T(8,128)S(1)} %shard_map.94), channel_id=1, source_target_pairs={{0,24},{4,28},{8,16},{12,20},{16,8},{20,12},{24,0},{28,4},{1,25},{... | collective-permute-start | bytes 884744 | tf_op jit(solution)/shard_map/ppermute | solution.py:479
  46.1 5.0 %copy-start = (f32[8,64,128]{2,1,0:T(8,128)S(1)}, f32[8,64,128]{2,1,0:T(8,128)}, u32[]{:S(2)}) copy-start(f32[8,64,128]{2,1,0:T(8,128)} %land_flux.1) | copy-start | bytes 786436
  46.1 5.0 %copy-start.1 = (f32[64,128]{1,0:T(8,128)S(1)}, f32[64,128]{1,0:T(8,128)}, u32[]{:S(2)}) copy-start(f32[64,128]{1,0:T(8,128)} %kappa.3) | copy-start | bytes 98308
  46.1 5.0 %copy-start.2 = (f32[64,128]{1,0:T(8,128)S(1)}, f32[64,128]{1,0:T(8,128)}, u32[]{:S(2)}) copy-start(f32[64,128]{1,0:T(8,128)} %land_area.1) | copy-start | bytes 98308
  46.1 5.0 %collective-permute-start.5 = (f32[72,8,128]{2,1,0:T(8,128)S(1)}, f32[72,8,128]{2,1,0:T(8,128)S(1)}, u32[]{:S(2)}, u32[]{:S(2)}) collective-permute-start(f32[72,8,128]{2,1,0:T(8,128)S(1)} %shard_map.96), channel_id=1, source_target_pairs={{0,1},{1,0},{2,3},{3,2},{4,5},{5,4},{6,7},{7,6},{8,9},{9,8},{10,11... | collective-permute-start | bytes 884744 | tf_op jit(solution)/shard_map/ppermute | solution.py:482
  51.3 5.6 %collective-permute-start.8 = (f32[64,128]{1,0:T(8,128)S(1)}, f32[64,128]{1,0:T(8,128)S(1)}, u32[]{:S(2)}, u32[]{:S(2)}) collective-permute-start(f32[64,128]{1,0:T(8,128)S(1)} %get-tuple-element.43), channel_id=1, source_target_pairs={{4,8},{12,16},{20,24},{8,4},{16,12},{24,20},{5,9},{13,17},{21,25},... | collective-permute-start | bytes 98312 | tf_op jit(solution)/shard_map/ppermute | solution.py:378
  54.5 3.2 %collective-permute-start.7 = (f32[64,128]{1,0:T(8,128)S(1)}, f32[64,128]{1,0:T(8,128)S(1)}, u32[]{:S(2)}, u32[]{:S(2)}) collective-permute-start(f32[64,128]{1,0:T(8,128)S(1)} %get-tuple-element.43), channel_id=1, source_target_pairs={{0,4},{4,0},{8,12},{12,8},{16,20},{20,16},{24,28},{28,24},{1,5},{5... | collective-permute-start | bytes 98312 | tf_op jit(solution)/shard_map/ppermute | solution.py:377
  57.8 6.7 %collective-permute-start.10 = (f32[10,8,128]{2,1,0:T(8,128)S(1)}, f32[10,8,128]{2,1,0:T(8,128)S(1)}, u32[]{:S(2)}, u32[]{:S(2)}) collective-permute-start(f32[10,8,128]{2,1,0:T(8,128)S(1)} %pad_maximum_fusion), channel_id=1, source_target_pairs={{1,2},{2,1},{5,6},{6,5},{9,10},{10,9},{13,14},{14,13},{17,18},{18,... | collective-permute-start | bytes 122888 | tf_op jit(solution)/shard_map/ppermute | solution.py:378
  62.8 1.7 %collective-permute-start.9 = (f32[10,8,128]{2,1,0:T(8,128)S(1)}, f32[10,8,128]{2,1,0:T(8,128)S(1)}, u32[]{:S(2)}, u32[]{:S(2)}) collective-permute-start(f32[10,8,128]{2,1,0:T(8,128)S(1)} %pad_maximum_fusion), channel_id=1, source_target_pairs={{0,1},{1,0},{2,3},{3,2},{4,5},{5,4},{6,7},{7,6},{8,9},{9,8},{10,11... | collective-permute-start | bytes 122888 | tf_op jit(solution)/shard_map/ppermute | solution.py:377

commit v4 on v3

--- a/solution.py
+++ b/solution.py
@@ -13,6 +13,7 @@
 SWEEPS = 3
 LAYERS = 4
 EDGE = 4
+TOGETHER = 8
 LANE_BLOCK = 14
 
 BF16 = jnp.bfloat16
@@ -230,79 +231,61 @@
     return tile, row, lax.shift_right_logical(cell, row) - ATM_COLS
 
 
-def bin_slots(cap, picked, earlier, *refs):
-    arrays = len(refs) - 2 - (2 if earlier else 1) * len(picked)
-    given, refs = refs[:arrays], refs[arrays:]
-    before = refs[: len(picked)] if earlier else ()
-    totals = refs[len(before) : len(before) + len(picked)]
-    slots, sems = refs[-2:]
-    copies, bounds = [], []
-    for pick in picked:
-        low = sum(copy[2] for copy in copies)
+def bin_slots(cap, picked, arrays, *refs):
+    given, before, totals = refs[:arrays], refs[arrays : -len(picked)], refs[-len(picked) :]
+    for n, (pick, total) in enumerate(zip(picked, totals, strict=True)):
+        total[...] = before[n][...] if before else jnp.zeros_like(total)
         for array, first, number in pick:
-            at = sum(copy[2] for copy in copies)
-            copies.append((array, first, number, at))
-        bounds.append((low, sum(copy[2] for copy in copies)))
-    started = []
-    for i, (array, first, number, at) in enumerate(copies):
-        copy = pltpu.make_async_copy(
-            given[array].at[pl.ds(first, number)], slots.at[pl.ds(at, number)], sems.at[i]
-        )
-        copy.start()
-        started.append(copy)
-    for i, total in enumerate(totals):
-        total[...] = before[i][...] if earlier else jnp.zeros_like(total)
-    for copy in started:
-        copy.wait()
-    for total, (low, high) in zip(totals, bounds, strict=True):
-        bin_range(cap, slots, low, high, total)
-
-
-def bin_range(cap, slots, low, high, total):
-    sources, _, field_count, cells = slots.shape
+            together = min(number, TOGETHER)
+
+            def some(i, carry):
+                for block in range(together):
+                    bin_block(cap, given[array], first + i * together + block, total)
+                return carry
+
+            lax.fori_loop(0, number // together, some, 0, unroll=number == together)
+
+
+def bin_block(cap, slots, i, total):
+    field_count, cells = slots.shape[2:]
     rows_here = total.shape[0] * TILE_ROWS // (TILE_ROWS + 1)
     zero = jnp.zeros((), BF16)
-
-    def source(g, carry):
-        weight = slots[g, cap].astype(F32)
-        tile, row, col = decode(slots[g, cap + 1].astype(F32))
-        row16 = row.astype(F32).astype(BF16)
-        col16 = col.astype(F32).astype(BF16)
-        weight16 = weight.astype(BF16)
-        for n in range(cap):
-            field = slots[g, n]
-            t = tile[n, 0]
-            row_n = jnp.broadcast_to(row16[n : n + 1], (16, cells))
-            twice = jnp.concatenate([field, field], axis=0)
-            sub = iota((16, cells), 0)
-            left = []
-            for q in range(0, TILE_ROWS, 2):
-                want = jnp.where(sub >= 8, q + 1.0, q + 0.0).astype(BF16)
-                left.append(jnp.where(row_n == want, twice, zero))
-            ones = jnp.ones((), BF16)
-            left.append(jnp.where(row_n == sub.astype(F32).astype(BF16), ones, zero))
-            right = jnp.where(
-                jnp.broadcast_to(col16[n : n + 1], (ATM_COLS, cells))
-                == iota((ATM_COLS, cells), 0).astype(F32).astype(BF16),
-                jnp.broadcast_to(weight16[n : n + 1], (ATM_COLS, cells)),
-                zero,
-            )
-            added = lax.dot_general(
-                jnp.concatenate(left, axis=0),
-                right,
-                (((1,), (1,)), ((), ())),
-                preferred_element_type=F32,
-            )
-            main = TILE_ROWS * field_count
-            total[pl.ds(t * TILE_ROWS, TILE_ROWS)] += added[:main].reshape(
-                TILE_ROWS, field_count, ATM_COLS
-            )
-            total[pl.ds(rows_here + t, 1)] += added[main : main + TILE_ROWS].reshape(
-                1, TILE_ROWS, ATM_COLS
-            )
-        return carry
-
-    lax.fori_loop(low, high, source, 0, unroll=2 if (high - low) % 2 == 0 else 1)
+    weight = slots[i, cap].astype(F32)
+    tile, row, col = decode(slots[i, cap + 1].astype(F32))
+    row16 = row.astype(F32).astype(BF16)
+    col16 = col.astype(F32).astype(BF16)
+    weight16 = weight.astype(BF16)
+    for n in range(cap):
+        field = slots[i, n]
+        t = tile[n, 0]
+        row_n = jnp.broadcast_to(row16[n : n + 1], (16, cells))
+        twice = jnp.concatenate([field, field], axis=0)
+        sub = iota((16, cells), 0)
+        left = []
+        for q in range(0, TILE_ROWS, 2):
+            want = jnp.where(sub >= 8, q + 1.0, q + 0.0).astype(BF16)
+            left.append(jnp.where(row_n == want, twice, zero))
+        ones = jnp.ones((), BF16)
+        left.append(jnp.where(row_n == sub.astype(F32).astype(BF16), ones, zero))
+        right = jnp.where(
+            jnp.broadcast_to(col16[n : n + 1], (ATM_COLS, cells))
+            == iota((ATM_COLS, cells), 0).astype(F32).astype(BF16),
+            jnp.broadcast_to(weight16[n : n + 1], (ATM_COLS, cells)),
+            zero,
+        )
+        added = lax.dot_general(
+            jnp.concatenate(left, axis=0),
+            right,
+            (((1,), (1,)), ((), ())),
+            preferred_element_type=F32,
+        )
+        main = TILE_ROWS * field_count
+        total[pl.ds(t * TILE_ROWS, TILE_ROWS)] += added[:main].reshape(
+            TILE_ROWS, field_count, ATM_COLS
+        )
+        total[pl.ds(rows_here + t, 1)] += added[main : main + TILE_ROWS].reshape(
+            1, TILE_ROWS, ATM_COLS
+        )
 
 
 def merge_kernel(total, other, passed, land_flux, land_area, kappa, merged, strips, edges):
@@ -333,14 +316,10 @@
     number = sum(part[2] for pick in picked for part in pick)
     each = 2 * (field_count + 1) * TILE_ROWS * cells * ATM_COLS
     return pl.pallas_call(
-        functools.partial(bin_slots, cap, picked, bool(earlier)),
+        functools.partial(bin_slots, cap, picked, len(arrays)),
         out_shape=[jax.ShapeDtypeStruct(shape, F32)] * len(picked),
-        in_specs=[ANY] * len(arrays) + [VMEM] * len(earlier),
+        in_specs=[VMEM] * (len(arrays) + len(earlier)),
         out_specs=[VMEM] * len(picked),
-        scratch_shapes=[
-            pltpu.VMEM((number,) + arrays[0].shape[1:], BF16),
-            pltpu.SemaphoreType.DMA((sum(len(pick) for pick in picked),)),
-        ],
         compiler_params=params(),
         cost_estimate=pl.CostEstimate(
             flops=number * 8 * each,
@@ -390,43 +369,59 @@
     return jnp.concatenate([values[:EDGE], values[rows - EDGE :]], axis=0)
 
 
-NEIGHBOURS = ((-1, 0), (1, 0), (-1, 1), (1, 1))
-
-
-def sweep_kernel(merged, before, after, above, below, kappa, out):
+def sweep_kernel(merged, before, after, above, below, kappa, out, held):
     field_count, rows_here, cols_here = merged.shape
-
-    def near(values, i):
-        step, axis = NEIGHBOURS[i]
-        return pltpu.roll(values, step % values.shape[axis], axis)
-
-    def halo_rows(i):
-        return jnp.concatenate([below[i][:EDGE], above[i][EDGE:]], axis=0)
-
-    columns = select_columns(before[...], after[...])
-    corners = halo_rows(field_count + 1)
-    lane = iota((rows_here + 2 * EDGE, cols_here), 1)
+    rows = rows_here + 2 * EDGE
+    pad = (held.shape[1] - rows) // 2
+    lane = iota((rows, cols_here), 1)
     border = (lane < SWEEPS) | (lane >= cols_here - SWEEPS)
-
-    def whole(cells, f):
-        side = jnp.concatenate([columns, corners], axis=0)
-        side = pltpu.roll(side, (cols_here - f * LANE_BLOCK) % cols_here, 1) if f else side
-        return jnp.concatenate(
-            [jnp.concatenate([cells, halo_rows(f)], axis=0), jnp.where(border, side, 0.0)], axis=1
-        )
-
-    k = whole(kappa[...], field_count)
+    columns = jnp.concatenate(
+        [
+            above[field_count + 1][EDGE:],
+            select_columns(before[...], after[...]),
+            below[field_count + 1][:EDGE],
+        ],
+        axis=0,
+    )
+
+    def put(f, cells):
+        held[f, pad : pad + rows] = cells
+
+    def put_whole(f, cells):
+        shift = (cols_here - f * LANE_BLOCK) % cols_here
+        side = pltpu.roll(columns, shift, 1) if f else columns
+        middle = jnp.concatenate([above[f][EDGE:], cells, below[f][:EDGE]], axis=0)
+        put(f, jnp.concatenate([middle, jnp.where(border, side, 0.0)], axis=1))
+
+    def neighbours_of(f, cells):
+        return (
+            held[f, pad - 1 : pad - 1 + rows],
+            held[f, pad + 1 : pad + 1 + rows],
+            pltpu.roll(cells, 2 * cols_here - 1, 1),
+            pltpu.roll(cells, 1, 1),
+        )
+
+    empty = jnp.zeros((pad, 2 * cols_here), F32)
+    for f in range(field_count + 1):
+        held[f, :pad] = empty
+        held[f, pad + rows :] = empty
+        put_whole(f, merged[f] if f < field_count else kappa[...])
+
+    k = held[field_count, pad : pad + rows]
+    inside = k > 0.0
     coefficients = [
-        jnp.where(k > 0.0, 0.5 * (k + near(k, i)), 0.0) for i in range(len(NEIGHBOURS))
+        jnp.where(inside, 0.5 * (k + near), 0.0) for near in neighbours_of(field_count, k)
     ]
-    for f in range(field_count):
-        u = whole(merged[f], f)
-        for _ in range(SWEEPS):
+    for sweep_index in range(SWEEPS):
+        for f in range(field_count):
+            u = held[f, pad : pad + rows]
             new = u
-            for i, coefficient in enumerate(coefficients):
-                new = new + coefficient * (near(u, i) - u)
-            u = new
-        out[f] = u[:rows_here, :cols_here]
+            for coefficient, near in zip(coefficients, neighbours_of(f, u), strict=True):
+                new = new + coefficient * (near - u)
+            if sweep_index < SWEEPS - 1:
+                put(f, new)
+            else:
+                out[f] = new[EDGE : EDGE + rows_here, :cols_here]
 
 
 def shards(
@@ -469,20 +464,36 @@
     far_got = exchange(far_slots)
     kept, given = pack(*pairs, cap, device_count, True, 0)
     taken = lax.ppermute(given, ("gx", "gy"), [(i, i ^ 1) for i in everywhere])
-    got = [
-        lax.ppermute(message, ("gx", "gy"), [(i, i ^ 2 * carried(j, i & 1)) for i in everywhere])
-        for j, message in enumerate(join(kept, taken))
-    ]
+    messages = join(kept, taken)
+
+    def deliver(j):
+        pairing = [(i, i ^ 2 * carried(j, i & 1)) for i in everywhere]
+        return lax.ppermute(messages[j], ("gx", "gy"), pairing)
+
+    half_way = len(messages) // 2
+    soon = [deliver(j) for j in reversed(range(half_way))]
+    late = [deliver(j) for j in range(half_way, len(messages))]
 
     far_total = bin_all([far_got], [[(0, 0, half)]], [], cap, rows_here)[0]
     opposite = [(i, i ^ (mirror // width_y)) for i in range(width_x)]
     passed = lax.ppermute(far_total, "gx", opposite)
-    got, far_total = lax.optimization_barrier((got, far_total))
-    other = bin_all(got, [[(j, 2, 2) for j in range(len(got))]], [], cap, rows_here)[0]
+
+    def sums(messages, *which, earlier=()):
+        picked = [[(j, 2 * i, 2) for j in range(len(messages))] for i in which]
+        return bin_all(messages, picked, earlier, cap, rows_here)
+
+    totals = []
+    for message in soon:
+        message, far_total = lax.optimization_barrier((message, far_total))
+        totals = sums([message], 0, 1, earlier=totals)
+        far_total = totals[0]
+    own, other = totals
+    late, own = lax.optimization_barrier((late, own))
+    other = sums(late, 1, earlier=[other])[0]
     other = lax.ppermute(other, ("gx", "gy"), [(i, i ^ 1) for i in everywhere])
-    total = bin_all(got, [[(j, 0, 2) for j in range(len(got))]], [], cap, rows_here)[0]
-
-    merged, strips, edges = merge(total, other, passed, land_flux, land_area, kappa)
+    own = sums(late, 0, earlier=[own])[0]
+
+    merged, strips, edges = merge(own, other, passed, land_flux, land_area, kappa)
     before, after = neighbours(strips, "gx")
     corners = ends(select_columns(before, after))
     above, below = neighbours(jnp.concatenate([edges, corners[None]], axis=0), "gy")
@@ -491,6 +502,9 @@
         out_shape=jax.ShapeDtypeStruct(merged.shape, F32),
         in_specs=[VMEM] * 6,
         out_specs=VMEM,
+        scratch_shapes=[
+            pltpu.VMEM((field_count + 1, rows_here + 2 * EDGE + 16, 2 * cols_here), F32)
+        ],
         compiler_params=params(),
     )(merged, before, after, above, below, kappa)
 

time: 67.9 us -> 64.6 us (0.951)
  Pallas kernels: 27.6 us -> 22.8 us
  waiting for transfers between devices: 17.3 us -> 19.5 us
  local copies, waits for them, and re-layouts: 0.85 us -> 0.03 us
    pallas_call x3 -> x5, Pallas kernels: 15.4 us -> 11.6 us  [bin_all(): pl.pallas_call(functools.partial(bin_slots, cap, picked, len(arrays)), ou...]
    ppermute x4, waiting for transfers between devices: 6.41 us -> 7.93 us  [deliver(): return lax.ppermute(messages[j], ('gx', 'gy'), pairing)]
    pallas_call x1, Pallas kernels: 2.98 us -> 2.04 us  [shards(): pl.pallas_call(sweep_kernel, out_shape=jax.ShapeDtypeStruct(merged.shape,...]
    ppermute x2, starting transfers between devices: 8.15 us -> 9.02 us  [neighbours(): two = lax.ppermute(values, axis, second)]
    unnamed x8 -> x6, local copies, waits for them, and re-layouts: 0.84 us -> 0.02 us
    all_to_all x1, waiting for transfers between devices: 4.23 us -> 4.91 us  [shards(): far_got = exchange(far_slots)]
  transfers between devices with their start and end apart: 12 -> 12, of which waited for: 6 -> 7; matrix products, arithmetic and copies ran while one was open for 0% -> 0% of each run, Pallas kernels for 31% -> 27%
where the time goes in v4:
time: 64.6 us; the launch traced here: 64.3 us
  Pallas kernels  22.8 us (35%)
  starting transfers between devices  21.7 us (34%)
  waiting for transfers between devices  19.5 us (30%)
    pallas_call x5, Pallas kernels, bin_all(): pl.pallas_call(functools.partial(bin_slots, cap, picked, len(arrays)), ou...  11.6 us
    ppermute x2, starting transfers between devices, neighbours(): two = lax.ppermute(values, axis, second)  9.02 us
    ppermute x4, waiting for transfers between devices, deliver(): return lax.ppermute(messages[j], ('gx', 'gy'), pairing)  7.93 us
    pallas_call x2, Pallas kernels, pack(): pl.pallas_call(functools.partial(pack_kernel, cap, near, mirror), out_sha...  6.7 us
    all_to_all x1, starting transfers between devices, shards(): far_got = exchange(far_slots)  5.58 us
    ppermute x4, starting transfers between devices, deliver(): return lax.ppermute(messages[j], ('gx', 'gy'), pairing)  5.23 us
    all_to_all x1, waiting for transfers between devices, shards(): far_got = exchange(far_slots)  4.91 us
    ppermute x2, waiting for transfers between devices, neighbours(): two = lax.ppermute(values, axis, second)  3.39 us
  transfers between devices with their start and end apart: 12, of which 7 were waited for; matrix products, arithmetic and copies ran while one was open for 0% of the time, Pallas kernels for 27%

profile of v4, /device:TPU:21, one launch (start us, length us, event | category | flops | bytes accessed | tf_op | source)
XLA Modules:
  0.0 64.3 jit_solution(17528710051018651286)
XLA Ops:
  0.0 3.3 %shard_map.91 = bf16[16,10,8,512]{3,2,1,0:T(8,128)(2,1)} custom-call(s32[2,64]{1,0:T(2,128)} %bitcast.4, s32[2,64]{1,0:T(2,128)} %bitcast.5, s32[2,64]{1,0:T(2,128)} %bitcast.8, s32[64,2,512]{2,1,0:T(2,128)} %refs_3_.2, bf16[64,2,512]{2,1,0:T(2,128)(2,1)} %refs_4_.2, s32[64,512]{1,0:T(8,128)} %refs_5_.2, bf16[64,8,512]{2,1,0:T(8,128)(2,1)} %refs_6_.2), custom_call_target="tpu_custom_call" | custom-call | flops 100000000 | bytes 4000000 | tf_op jit(solution)/shard_map/pallas_call | solution.py:160
  3.3 5.6 %all-to-all-start = ((bf16[16,10,8,512]{3,2,1,0:T(8,128)(2,1)}), bf16[16,10,8,512]{3,2,1,0:T(8,128)(2,1)S(1)}, u32[]{:S(2)}, u32[]{:S(2)}) async-start(bf16[16,10,8,512]{3,2,1,0:T(8,128)(2,1)} %shard_map.91), calls=%async_computation | async-start | bytes 2621440 | tf_op jit(solution)/shard_map/all_to_all | solution.py:464
  8.9 3.4 %shard_map.92 = (bf16[8,10,8,512]{3,2,1,0:T(8,128)(2,1)}, bf16[8,10,8,512]{3,2,1,0:T(8,128)(2,1)}) custom-call(s32[2,64]{1,0:T(2,128)} %bitcast.6, s32[2,64]{1,0:T(2,128)} %bitcast.7, s32[2,64]{1,0:T(2,128)} %bitcast.9, s32[64,2,512]{2,1,0:T(2,128)} %refs_3_.2, bf16[64,2,512]{2,1,0:T(2,128)(2,1)} %refs_4_.2, s32[64,512]{1,0:T(8,128)} %refs_5_.2, ...), custom_call_target="tpu_custom_call" | custom-call | flops 100000000 | bytes 4000000 | tf_op jit(solution)/shard_map/pallas_call | solution.py:160
  12.3 0.4 collective-permute-start
  12.7 2.1 %collective-permute-done.taken = bf16[8,10,8,512]{3,2,1,0:T(8,128)(2,1)} collective-permute-done((bf16[8,10,8,512]{3,2,1,0:T(8,128)(2,1)}, bf16[8,10,8,512]{3,2,1,0:T(8,128)(2,1)}, u32[]{:S(2)}, u32[]{:S(2)}) %collective-permute-start) | collective-permute-done | bytes 655392 | tf_op jit(solution)/shard_map/ppermute | solution.py:466
  14.8 2.3 %shard_map.93 = (bf16[4,10,8,512]{3,2,1,0:T(8,128)(2,1)}, bf16[4,10,8,512]{3,2,1,0:T(8,128)(2,1)}, bf16[4,10,8,512]{3,2,1,0:T(8,128)(2,1)}, bf16[4,10,8,512]{3,2,1,0:T(8,128)(2,1)}) custom-call(bf16[8,10,8,512]{3,2,1,0:T(8,128)(2,1)} %get-tuple-element.36.kept, bf16[8,10,8,512]{3,2,1,0:T(8,128)(2,1)} %collective-permute-done.taken), custom_call_target="tpu_custom_call" | custom-call | bytes 2621440 | tf_op jit(solution)/shard_map/pallas_call | solution.py:203
  17.1 1.2 %collective-permute-start.4 = (bf16[4,10,8,512]{3,2,1,0:T(8,128)(2,1)}, bf16[4,10,8,512]{3,2,1,0:T(8,128)(2,1)S(1)}, u32[]{:S(2)}, u32[]{:S(2)}) collective-permute-start(bf16[4,10,8,512]{3,2,1,0:T(8,128)(2,1)} %get-tuple-element.41), channel_id=1, source_target_pairs={{0,4},{1,7},{2,6},{3,5},{4,0},{5,3},{6,2},{7,1},{8,12},{9,15},{10,... | collective-permute-start | bytes 983048 | tf_op jit(solution)/shard_map/ppermute | solution.py:471
  18.4 1.6 %collective-permute-start.3 = (bf16[4,10,8,512]{3,2,1,0:T(8,128)(2,1)}, bf16[4,10,8,512]{3,2,1,0:T(8,128)(2,1)S(1)}, u32[]{:S(2)}, u32[]{:S(2)}) collective-permute-start(bf16[4,10,8,512]{3,2,1,0:T(8,128)(2,1)} %get-tuple-element.40), channel_id=1, source_target_pairs={{0,2},{1,1},{2,0},{3,3},{4,6},{5,5},{6,4},{7,7},{8,10},{9,9},{10,8... | collective-permute-start | bytes 983048 | tf_op jit(solution)/shard_map/ppermute | solution.py:471
  20.0 1.2 %collective-permute-start.1 = (bf16[4,10,8,512]{3,2,1,0:T(8,128)(2,1)}, bf16[4,10,8,512]{3,2,1,0:T(8,128)(2,1)S(1)}, u32[]{:S(2)}, u32[]{:S(2)}) collective-permute-start(bf16[4,10,8,512]{3,2,1,0:T(8,128)(2,1)} %get-tuple-element.38), channel_id=1, source_target_pairs={{0,8},{1,11},{2,10},{3,9},{4,12},{5,15},{6,14},{7,13},{8,0},{9,3},... | collective-permute-start | bytes 983048 | tf_op jit(solution)/shard_map/ppermute | solution.py:471
  21.2 1.2 %collective-permute-start.2 = (bf16[4,10,8,512]{3,2,1,0:T(8,128)(2,1)}, bf16[4,10,8,512]{3,2,1,0:T(8,128)(2,1)S(1)}, u32[]{:S(2)}, u32[]{:S(2)}) collective-permute-start(bf16[4,10,8,512]{3,2,1,0:T(8,128)(2,1)} %get-tuple-element.39), channel_id=1, source_target_pairs={{0,14},{1,13},{2,12},{3,15},{4,10},{5,9},{6,8},{7,11},{8,6},{9,5},... | collective-permute-start | bytes 983048 | tf_op jit(solution)/shard_map/ppermute | solution.py:471
  22.3 4.9 %all-to-all-done.refs_0_ = bf16[16,10,8,512]{3,2,1,0:T(8,128)(2,1)S(1)} async-done(((bf16[16,10,8,512]{3,2,1,0:T(8,128)(2,1)}), bf16[16,10,8,512]{3,2,1,0:T(8,128)(2,1)S(1)}, u32[]{:S(2)}, u32[]{:S(2)}) %all-to-all-start) | async-done | bytes 1310752 | tf_op jit(solution)/shard_map/all_to_all | solution.py:464
  27.3 5.6 %shard_map.94 = f32[72,8,128]{2,1,0:T(8,128)S(1)} custom-call(bf16[16,10,8,512]{3,2,1,0:T(8,128)(2,1)S(1)} %all-to-all-done.refs_0_), custom_call_target="tpu_custom_call" | custom-call | flops 1207959552 | bytes 1310720 | tf_op jit(solution)/shard_map/pallas_call | solution.py:318
  32.9 1.2 %collective-permute-start.6 = (f32[72,8,128]{2,1,0:T(8,128)S(1)}, f32[72,8,128]{2,1,0:T(8,128)S(1)}, u32[]{:S(2)}, u32[]{:S(2)}) collective-permute-start(f32[72,8,128]{2,1,0:T(8,128)S(1)} %shard_map.94), channel_id=1, source_target_pairs={{0,24},{4,28},{8,16},{12,20},{16,8},{20,12},{24,0},{28,4},{1,25},{... | collective-permute-start | bytes 884744 | tf_op jit(solution)/shard_map/ppermute | solution.py:479
  34.1 7.9 %collective-permute-done.4.refs_0_ = bf16[4,10,8,512]{3,2,1,0:T(8,128)(2,1)S(1)} collective-permute-done((bf16[4,10,8,512]{3,2,1,0:T(8,128)(2,1)}, bf16[4,10,8,512]{3,2,1,0:T(8,128)(2,1)S(1)}, u32[]{:S(2)}, u32[]{:S(2)}) %collective-permute-start.4) | collective-permute-done | bytes 327712 | tf_op jit(solution)/shard_map/ppermute | solution.py:471
  42.0 1.5 %shard_map.95 = (f32[72,8,128]{2,1,0:T(8,128)S(1)}, f32[72,8,128]{2,1,0:T(8,128)S(1)}) custom-call(bf16[4,10,8,512]{3,2,1,0:T(8,128)(2,1)S(1)} %collective-permute-done.4.refs_0_), custom_call_target="tpu_custom_call" | custom-call | flops 301989888 | bytes 327680 | tf_op jit(solution)/shard_map/pallas_call | solution.py:318
  43.6 1.5 %shard_map.96 = (f32[72,8,128]{2,1,0:T(8,128)S(1)}, f32[72,8,128]{2,1,0:T(8,128)S(1)}) custom-call(bf16[4,10,8,512]{3,2,1,0:T(8,128)(2,1)S(1)} %collective-permute-done.3.refs_0_, f32[72,8,128]{2,1,0:T(8,128)S(1)} %get-tuple-element.44.refs_1_, f32[72,8,128]{2,1,0:T(8,128)S(1)} %get-tuple-element.46.refs_2_), custom_call_target="tpu_custom_call" | custom-call | flops 301989888 | bytes 327680 | tf_op jit(solution)/shard_map/pallas_call | solution.py:318
  45.0 0.0 copy-start
  45.1 0.0 copy-start.1
  45.1 0.0 copy-start.2
  45.1 1.5 %shard_map.98 = f32[72,8,128]{2,1,0:T(8,128)S(1)} custom-call(bf16[4,10,8,512]{3,2,1,0:T(8,128)(2,1)S(1)} %collective-permute-done.1.refs_0_, bf16[4,10,8,512]{3,2,1,0:T(8,128)(2,1)S(1)} %collective-permute-done.2.refs_1_, f32[72,8,128]{2,1,0:T(8,128)S(1)} %get-tuple-element.51.refs_2_), custom_call_target="tpu_custom_call" | custom-call | flops 301989888 | bytes 327680 | tf_op jit(solution)/shard_map/pallas_call | solution.py:318
  46.6 0.1 collective-permute-start.5
  46.7 1.5 %shard_map.97.total = f32[72,8,128]{2,1,0:T(8,128)S(1)} custom-call(bf16[4,10,8,512]{3,2,1,0:T(8,128)(2,1)S(1)} %collective-permute-done.1.refs_0_, bf16[4,10,8,512]{3,2,1,0:T(8,128)(2,1)S(1)} %collective-permute-done.2.refs_1_, f32[72,8,128]{2,1,0:T(8,128)S(1)} %get-tuple-element.50.refs_2_), custom_call_target="tpu_custom_call" | custom-call | flops 301989888 | bytes 327680 | tf_op jit(solution)/shard_map/pallas_call | solution.py:318
  48.2 0.1 collective-permute-done.5.other
  48.3 0.2 shard_map.99
  48.5 5.6 %collective-permute-start.8 = (f32[64,128]{1,0:T(8,128)S(1)}, f32[64,128]{1,0:T(8,128)S(1)}, u32[]{:S(2)}, u32[]{:S(2)}) collective-permute-start(f32[64,128]{1,0:T(8,128)S(1)} %get-tuple-element.53), channel_id=1, source_target_pairs={{4,8},{12,16},{20,24},{8,4},{16,12},{24,20},{5,9},{13,17},{21,25},... | collective-permute-start | bytes 98312 | tf_op jit(solution)/shard_map/ppermute | solution.py:357
  54.0 0.1 collective-permute-start.7
  54.1 1.6 %collective-permute-done.8 = f32[64,128]{1,0:T(8,128)S(1)} collective-permute-done((f32[64,128]{1,0:T(8,128)S(1)}, f32[64,128]{1,0:T(8,128)S(1)}, u32[]{:S(2)}, u32[]{:S(2)}) %collective-permute-start.8) | collective-permute-done | bytes 32800 | tf_op jit(solution)/shard_map/ppermute | solution.py:357
  55.8 1.1 %collective-permute-done.7 = f32[64,128]{1,0:T(8,128)S(1)} collective-permute-done((f32[64,128]{1,0:T(8,128)S(1)}, f32[64,128]{1,0:T(8,128)S(1)}, u32[]{:S(2)}, u32[]{:S(2)}) %collective-permute-start.7) | collective-permute-done | bytes 32800 | tf_op jit(solution)/shard_map/ppermute | solution.py:356
  56.9 3.4 %collective-permute-start.10 = (f32[10,8,128]{2,1,0:T(8,128)S(1)}, f32[10,8,128]{2,1,0:T(8,128)S(1)}, u32[]{:S(2)}, u32[]{:S(2)}) collective-permute-start(f32[10,8,128]{2,1,0:T(8,128)S(1)} %pad_maximum_fusion), channel_id=1, source_target_pairs={{1,2},{2,1},{5,6},{6,5},{9,10},{10,9},{13,14},{14,13},{17,18},{18,... | collective-permute-start | bytes 122888 | tf_op jit(solution)/shard_map/ppermute | solution.py:357
  60.4 0.1 collective-permute-start.9
  60.5 1.8 %collective-permute-done.10 = f32[10,8,128]{2,1,0:T(8,128)S(1)} collective-permute-done((f32[10,8,128]{2,1,0:T(8,128)S(1)}, f32[10,8,128]{2,1,0:T(8,128)S(1)}, u32[]{:S(2)}, u32[]{:S(2)}) %collective-permute-start.10) | collective-permute-done | bytes 40992 | tf_op jit(solution)/shard_map/ppermute | solution.py:357
  62.3 2.0 %shard_map.100 = f32[8,64,128]{2,1,0:T(8,128)} custom-call(f32[8,64,128]{2,1,0:T(8,128)S(1)} %get-tuple-element.52.merged, f32[64,128]{1,0:T(8,128)S(1)} %get-tuple-element.57.before, f32[64,128]{1,0:T(8,128)S(1)} %get-tuple-element.56.after, f32[10,8,128]{2,1,0:T(8,128)S(1)} %get-tuple-element.59.above, f32[10,8,128]{2,1,0:T(8,128)S(1)} %get-tuple-element.58.below, ...), custom_call_target="tpu_custom_call" | custom-call | tf_op jit(solution)/shard_map/pallas_call | solution.py:500
  (15 shorter events, 0.1 us)
Async XLA Ops:
  3.3 23.9 %all-to-all-start = ((bf16[16,10,8,512]{3,2,1,0:T(8,128)(2,1)}), bf16[16,10,8,512]{3,2,1,0:T(8,128)(2,1)S(1)}, u32[]{:S(2)}, u32[]{:S(2)}) async-start(bf16[16,10,8,512]{3,2,1,0:T(8,128)(2,1)} %shard_map.91), calls=%async_computation | async-start | bytes 2621440 | tf_op jit(solution)/shard_map/all_to_all | solution.py:464
  12.3 2.5 %collective-permute-start = (bf16[8,10,8,512]{3,2,1,0:T(8,128)(2,1)}, bf16[8,10,8,512]{3,2,1,0:T(8,128)(2,1)}, u32[]{:S(2)}, u32[]{:S(2)}) collective-permute-start(bf16[8,10,8,512]{3,2,1,0:T(8,128)(2,1)} %get-tuple-element.37), channel_id=1, source_target_pairs={{0,1},{1,0},{2,3},{3,2},{4,5},{5,4},{6,7},{7,6},{8,9},{9,8},{10,11... | collective-permute-start | bytes 1966088 | tf_op jit(solution)/shard_map/ppermute | solution.py:466
  17.1 24.9 %collective-permute-start.4 = (bf16[4,10,8,512]{3,2,1,0:T(8,128)(2,1)}, bf16[4,10,8,512]{3,2,1,0:T(8,128)(2,1)S(1)}, u32[]{:S(2)}, u32[]{:S(2)}) collective-permute-start(bf16[4,10,8,512]{3,2,1,0:T(8,128)(2,1)} %get-tuple-element.41), channel_id=1, source_target_pairs={{0,4},{1,7},{2,6},{3,5},{4,0},{5,3},{6,2},{7,1},{8,12},{9,15},{10,... | collective-permute-start | bytes 983048 | tf_op jit(solution)/shard_map/ppermute | solution.py:471
  18.4 25.2 %collective-permute-start.3 = (bf16[4,10,8,512]{3,2,1,0:T(8,128)(2,1)}, bf16[4,10,8,512]{3,2,1,0:T(8,128)(2,1)S(1)}, u32[]{:S(2)}, u32[]{:S(2)}) collective-permute-start(bf16[4,10,8,512]{3,2,1,0:T(8,128)(2,1)} %get-tuple-element.40), channel_id=1, source_target_pairs={{0,2},{1,1},{2,0},{3,3},{4,6},{5,5},{6,4},{7,7},{8,10},{9,9},{10,8... | collective-permute-start | bytes 983048 | tf_op jit(solution)/shard_map/ppermute | solution.py:471
  20.0 25.1 %collective-permute-start.1 = (bf16[4,10,8,512]{3,2,1,0:T(8,128)(2,1)}, bf16[4,10,8,512]{3,2,1,0:T(8,128)(2,1)S(1)}, u32[]{:S(2)}, u32[]{:S(2)}) collective-permute-start(bf16[4,10,8,512]{3,2,1,0:T(8,128)(2,1)} %get-tuple-element.38), channel_id=1, source_target_pairs={{0,8},{1,11},{2,10},{3,9},{4,12},{5,15},{6,14},{7,13},{8,0},{9,3},... | collective-permute-start | bytes 983048 | tf_op jit(solution)/shard_map/ppermute | solution.py:471
  21.2 23.9 %collective-permute-start.2 = (bf16[4,10,8,512]{3,2,1,0:T(8,128)(2,1)}, bf16[4,10,8,512]{3,2,1,0:T(8,128)(2,1)S(1)}, u32[]{:S(2)}, u32[]{:S(2)}) collective-permute-start(bf16[4,10,8,512]{3,2,1,0:T(8,128)(2,1)} %get-tuple-element.39), channel_id=1, source_target_pairs={{0,14},{1,13},{2,12},{3,15},{4,10},{5,9},{6,8},{7,11},{8,6},{9,5},... | collective-permute-start | bytes 983048 | tf_op jit(solution)/shard_map/ppermute | solution.py:471
  32.9 15.3 %collective-permute-start.6 = (f32[72,8,128]{2,1,0:T(8,128)S(1)}, f32[72,8,128]{2,1,0:T(8,128)S(1)}, u32[]{:S(2)}, u32[]{:S(2)}) collective-permute-start(f32[72,8,128]{2,1,0:T(8,128)S(1)} %shard_map.94), channel_id=1, source_target_pairs={{0,24},{4,28},{8,16},{12,20},{16,8},{20,12},{24,0},{28,4},{1,25},{... | collective-permute-start | bytes 884744 | tf_op jit(solution)/shard_map/ppermute | solution.py:479
  45.0 3.2 %copy-start = (f32[8,64,128]{2,1,0:T(8,128)S(1)}, f32[8,64,128]{2,1,0:T(8,128)}, u32[]{:S(2)}) copy-start(f32[8,64,128]{2,1,0:T(8,128)} %land_flux.1) | copy-start | bytes 786436
  45.1 3.2 %copy-start.1 = (f32[64,128]{1,0:T(8,128)S(1)}, f32[64,128]{1,0:T(8,128)}, u32[]{:S(2)}) copy-start(f32[64,128]{1,0:T(8,128)} %kappa.3) | copy-start | bytes 98308
  45.1 3.2 %copy-start.2 = (f32[64,128]{1,0:T(8,128)S(1)}, f32[64,128]{1,0:T(8,128)}, u32[]{:S(2)}) copy-start(f32[64,128]{1,0:T(8,128)} %land_area.1) | copy-start | bytes 98308
  46.6 1.6 %collective-permute-start.5 = (f32[72,8,128]{2,1,0:T(8,128)S(1)}, f32[72,8,128]{2,1,0:T(8,128)S(1)}, u32[]{:S(2)}, u32[]{:S(2)}) collective-permute-start(f32[72,8,128]{2,1,0:T(8,128)S(1)} %shard_map.98), channel_id=1, source_target_pairs={{0,1},{1,0},{2,3},{3,2},{4,5},{5,4},{6,7},{7,6},{8,9},{9,8},{10,11... | collective-permute-start | bytes 884744 | tf_op jit(solution)/shard_map/ppermute | solution.py:493
  48.5 7.3 %collective-permute-start.8 = (f32[64,128]{1,0:T(8,128)S(1)}, f32[64,128]{1,0:T(8,128)S(1)}, u32[]{:S(2)}, u32[]{:S(2)}) collective-permute-start(f32[64,128]{1,0:T(8,128)S(1)} %get-tuple-element.53), channel_id=1, source_target_pairs={{4,8},{12,16},{20,24},{8,4},{16,12},{24,20},{5,9},{13,17},{21,25},... | collective-permute-start | bytes 98312 | tf_op jit(solution)/shard_map/ppermute | solution.py:357
  54.0 2.8 %collective-permute-start.7 = (f32[64,128]{1,0:T(8,128)S(1)}, f32[64,128]{1,0:T(8,128)S(1)}, u32[]{:S(2)}, u32[]{:S(2)}) collective-permute-start(f32[64,128]{1,0:T(8,128)S(1)} %get-tuple-element.53), channel_id=1, source_target_pairs={{0,4},{4,0},{8,12},{12,8},{16,20},{20,16},{24,28},{28,24},{1,5},{5... | collective-permute-start | bytes 98312 | tf_op jit(solution)/shard_map/ppermute | solution.py:356
  56.9 5.3 %collective-permute-start.10 = (f32[10,8,128]{2,1,0:T(8,128)S(1)}, f32[10,8,128]{2,1,0:T(8,128)S(1)}, u32[]{:S(2)}, u32[]{:S(2)}) collective-permute-start(f32[10,8,128]{2,1,0:T(8,128)S(1)} %pad_maximum_fusion), channel_id=1, source_target_pairs={{1,2},{2,1},{5,6},{6,5},{9,10},{10,9},{13,14},{14,13},{17,18},{18,... | collective-permute-start | bytes 122888 | tf_op jit(solution)/shard_map/ppermute | solution.py:357
  60.4 1.9 %collective-permute-start.9 = (f32[10,8,128]{2,1,0:T(8,128)S(1)}, f32[10,8,128]{2,1,0:T(8,128)S(1)}, u32[]{:S(2)}, u32[]{:S(2)}) collective-permute-start(f32[10,8,128]{2,1,0:T(8,128)S(1)} %pad_maximum_fusion), channel_id=1, source_target_pairs={{0,1},{1,0},{2,3},{3,2},{4,5},{5,4},{6,7},{7,6},{8,9},{9,8},{10,11... | collective-permute-start | bytes 122888 | tf_op jit(solution)/shard_map/ppermute | solution.py:356

commit v5 on v4

--- a/solution.py
+++ b/solution.py
@@ -13,6 +13,8 @@
 SWEEPS = 3
 LAYERS = 4
 EDGE = 4
+MEAN_SCALE = 2.0**8
+WEIGHT_SCALE = 2.0**-2
 TOGETHER = 8
 LANE_BLOCK = 14
 
@@ -38,8 +40,13 @@
     return number & 1
 
 
+def swapped(position, core):
+    return position ^ ((((position >> 1) - 1) >> 31) & 1 & (1 ^ core))
+
+
 def carried(position, core):
-    return 2 * position + (parity(position) ^ 1 ^ core)
+    index = swapped(position, core)
+    return 2 * index + (parity(index) ^ 1 ^ core)
 
 
 def pack_kernel(cap, near, mirror, *refs):
@@ -48,8 +55,8 @@
     copies = [
         pltpu.make_async_copy(given[i], held[i], in_sems.at[i]) for i in range(len(given))
     ]
-    for copy in copies:
-        copy.start()
+    for i in (0, 6, 1, 2, 3, 4, 5):
+        copies[i].start()
     dest_s, dest_v, tile_v, target, weight, mask, fields = held
     crossings, tiles = dest_v.shape
     half, cells = out_held.shape[0], fields.shape[2]
@@ -65,7 +72,8 @@
         index = owner - first
         distance = (index ^ here) >> 1
         carrier = 1 - parity(distance)
-        block = (carrier ^ core) * (half // 2) + (distance >> 1) * 2 + ((index & 1) ^ carrier)
+        position = swapped(distance >> 1, carrier)
+        block = (carrier ^ core) * (half // 2) + position * 2 + ((index & 1) ^ carrier)
         return jnp.where((index >= 0) & (index < half), block, -1)
 
     def owner_of(block):
@@ -94,6 +102,33 @@
             return carry
 
         lax.fori_loop(0, tiles, enter, 0, unroll=16)
+
+    copies[6].wait()
+    parts = out_sems.shape[0] // 2
+    step = half // parts
+    sent = []
+
+    def send(part, rows):
+        into = outs[part * step // outs[0].shape[0]]
+        there = part * step % outs[0].shape[0]
+        copy = pltpu.make_async_copy(
+            out_held.at[pl.ds(part * step, step), rows],
+            into.at[pl.ds(there, step), rows],
+            out_sems.at[len(sent)],
+        )
+        copy.start()
+        sent.append(copy)
+
+    for part in range(parts):
+
+        def fill(g, carry):
+            owner = owner_of(g)
+            for n in range(cap):
+                out_held[g, n] = fields[source[owner * cap + n]]
+            return carry
+
+        lax.fori_loop(part * step, (part + 1) * step, fill, 0, unroll=2)
+        send(part, pl.ds(0, cap))
 
     for copy in copies[1:6]:
         copy.wait()
@@ -131,23 +166,8 @@
             rows = packed[g * cap : (g + 1) * cap]
             out_held[g, row] = rows if cap == 8 else jnp.concatenate([rows, spare], axis=0)
 
-    copies[6].wait()
-    step = half // out_sems.shape[0]
-    sent = []
-    for part in range(out_sems.shape[0]):
-
-        def fill(g, carry):
-            owner = owner_of(g)
-            for n in range(cap):
-                out_held[g, n] = fields[source[owner * cap + n]]
-            return carry
-
-        lax.fori_loop(part * step, (part + 1) * step, fill, 0, unroll=2)
-        block = pl.ds(part * step, step)
-        out = outs[part * step // outs[0].shape[0]]
-        into = out.at[pl.ds(part * step % out.shape[0], step)]
-        sent.append(pltpu.make_async_copy(out_held.at[block], into, out_sems.at[part]))
-        sent[-1].start()
+    for part in range(parts):
+        send(part, pl.ds(cap, 2))
     for copy in sent:
         copy.wait()
 
@@ -169,7 +189,7 @@
             pltpu.SMEM((owners,), I32),
             pltpu.SMEM((owners * cap,), I32),
             pltpu.SemaphoreType.DMA((len(given),)),
-            pltpu.SemaphoreType.DMA((4,)),
+            pltpu.SemaphoreType.DMA((8,)),
         ],
         compiler_params=params(62),
         cost_estimate=pl.CostEstimate(
@@ -231,7 +251,7 @@
     return tile, row, lax.shift_right_logical(cell, row) - ATM_COLS
 
 
-def bin_slots(cap, picked, arrays, *refs):
+def bin_slots(cap, picked, arrays, averaged, *refs):
     given, before, totals = refs[:arrays], refs[arrays : -len(picked)], refs[-len(picked) :]
     for n, (pick, total) in enumerate(zip(picked, totals, strict=True)):
         total[...] = before[n][...] if before else jnp.zeros_like(total)
@@ -244,6 +264,18 @@
                 return carry
 
             lax.fori_loop(0, number // together, some, 0, unroll=number == together)
+        if averaged:
+            average(total)
+
+
+def average(total):
+    rows_here = total.shape[0] * TILE_ROWS // (TILE_ROWS + 1)
+    for tile in range(rows_here // TILE_ROWS):
+        weight = total[rows_here + tile]
+        factor = jnp.where(weight > 0.0, MEAN_SCALE / weight, 0.0)
+        for row in range(TILE_ROWS):
+            total[tile * TILE_ROWS + row] = total[tile * TILE_ROWS + row] * factor[row : row + 1]
+        total[rows_here + tile] = weight * WEIGHT_SCALE
 
 
 def bin_block(cap, slots, i, total):
@@ -291,11 +323,13 @@
 def merge_kernel(total, other, passed, land_flux, land_area, kappa, merged, strips, edges):
     field_count, rows_here, cols_here = land_flux.shape
     area = land_area[...]
-    denom = total[rows_here:] + other[rows_here:] + passed[rows_here:]
+    weight = passed[rows_here:] * (1.0 / WEIGHT_SCALE)
+    denom = total[rows_here:] + other[rows_here:] + weight
     denom = denom.reshape(rows_here, cols_here) + area
     lane = iota((rows_here, cols_here), 1)
     border = (lane < SWEEPS) | (lane >= cols_here - SWEEPS)
-    numer = total[:rows_here] + other[:rows_here] + passed[:rows_here]
+    weight = weight.reshape(rows_here, 1, cols_here) * (1.0 / MEAN_SCALE)
+    numer = total[:rows_here] + other[:rows_here] + passed[:rows_here] * weight
     numer = jnp.swapaxes(numer, 0, 1)
     packed = jnp.zeros((rows_here, cols_here), F32)
     for f in range(field_count + 1):
@@ -310,20 +344,20 @@
     strips[...] = packed
 
 
-def bin_all(arrays, picked, earlier, cap, rows_here):
+def bin_all(arrays, picked, earlier, cap, rows_here, averaged=False):
     _, rows, field_count, cells = arrays[0].shape
     shape = (rows_here // TILE_ROWS * (TILE_ROWS + 1), field_count, ATM_COLS)
     number = sum(part[2] for pick in picked for part in pick)
     each = 2 * (field_count + 1) * TILE_ROWS * cells * ATM_COLS
     return pl.pallas_call(
-        functools.partial(bin_slots, cap, picked, len(arrays)),
+        functools.partial(bin_slots, cap, picked, len(arrays), averaged),
         out_shape=[jax.ShapeDtypeStruct(shape, F32)] * len(picked),
         in_specs=[VMEM] * (len(arrays) + len(earlier)),
         out_specs=[VMEM] * len(picked),
         compiler_params=params(),
         cost_estimate=pl.CostEstimate(
-            flops=number * 8 * each,
-            bytes_accessed=number * rows * field_count * cells * 2,
+            flops=number * 8 * each if averaged else 0,
+            bytes_accessed=number * rows * field_count * cells * 2 if averaged else 0,
             transcendentals=0,
         ),
     )(*arrays, *earlier)
@@ -471,12 +505,12 @@
         return lax.ppermute(messages[j], ("gx", "gy"), pairing)
 
     half_way = len(messages) // 2
-    soon = [deliver(j) for j in reversed(range(half_way))]
+    soon = [deliver(j) for j in range(half_way)]
     late = [deliver(j) for j in range(half_way, len(messages))]
 
-    far_total = bin_all([far_got], [[(0, 0, half)]], [], cap, rows_here)[0]
+    far_total = bin_all([far_got], [[(0, 0, half)]], [], cap, rows_here, averaged=True)[0]
     opposite = [(i, i ^ (mirror // width_y)) for i in range(width_x)]
-    passed = lax.ppermute(far_total, "gx", opposite)
+    passed = lax.ppermute(far_total.astype(jnp.float16), "gx", opposite).astype(F32)
 
     def sums(messages, *which, earlier=()):
         picked = [[(j, 2 * i, 2) for j in range(len(messages))] for i in which]
@@ -488,7 +522,7 @@
         totals = sums([message], 0, 1, earlier=totals)
         far_total = totals[0]
     own, other = totals
-    late, own = lax.optimization_barrier((late, own))
+    late, own, passed = lax.optimization_barrier((late, own, passed))
     other = sums(late, 1, earlier=[other])[0]
     other = lax.ppermute(other, ("gx", "gy"), [(i, i ^ 1) for i in everywhere])
     own = sums(late, 0, earlier=[own])[0]

time: 64.6 us -> 63.4 us (0.981)
  the two profiles are of different devices: /device:TPU:21 before, /device:TPU:9 now
where the time goes in v5:
time: 63.4 us; the launch traced here: 63.1 us
  starting transfers between devices  23.4 us (37%)
  Pallas kernels  22.8 us (36%)
  waiting for transfers between devices  15.7 us (25%)
  local copies, waits for them, and re-layouts  0.86 us (1%)
    pallas_call x5, Pallas kernels, bin_all(): pl.pallas_call(functools.partial(bin_slots, cap, picked, len(arrays), ave...  11.6 us
    ppermute x2, starting transfers between devices, neighbours(): two = lax.ppermute(values, axis, second)  9.67 us
    pallas_call x2, Pallas kernels, pack(): pl.pallas_call(functools.partial(pack_kernel, cap, near, mirror), out_sha...  6.58 us
    ppermute x4, waiting for transfers between devices, deliver(): return lax.ppermute(messages[j], ('gx', 'gy'), pairing)  6.11 us
    all_to_all x1, starting transfers between devices, shards(): far_got = exchange(far_slots)  5.53 us
    ppermute x4, starting transfers between devices, deliver(): return lax.ppermute(messages[j], ('gx', 'gy'), pairing)  5.18 us
    all_to_all x1, waiting for transfers between devices, shards(): far_got = exchange(far_slots)  3.3 us
    ppermute x2, waiting for transfers between devices, neighbours(): two = lax.ppermute(values, axis, second)  3.17 us
  transfers between devices with their start and end apart: 12, of which 7 were waited for; matrix products, arithmetic and copies ran while one was open for 0% of the time, Pallas kernels for 25%

profile of v5, /device:TPU:9, one launch (start us, length us, event | category | flops | bytes accessed | tf_op | source)
XLA Modules:
  0.0 63.1 jit_solution(17653635948463824963)
XLA Ops:
  0.0 3.1 %shard_map.91 = bf16[16,10,8,512]{3,2,1,0:T(8,128)(2,1)} custom-call(s32[2,64]{1,0:T(2,128)} %bitcast.4, s32[2,64]{1,0:T(2,128)} %bitcast.5, s32[2,64]{1,0:T(2,128)} %bitcast.8, s32[64,2,512]{2,1,0:T(2,128)} %refs_3_.2, bf16[64,2,512]{2,1,0:T(2,128)(2,1)} %refs_4_.2, s32[64,512]{1,0:T(8,128)} %refs_5_.2, bf16[64,8,512]{2,1,0:T(8,128)(2,1)} %refs_6_.2), custom_call_target="tpu_custom_call" | custom-call | flops 100000000 | bytes 4000000 | tf_op jit(solution)/shard_map/pallas_call | solution.py:180
  3.2 5.5 %all-to-all-start = ((bf16[16,10,8,512]{3,2,1,0:T(8,128)(2,1)}), bf16[16,10,8,512]{3,2,1,0:T(8,128)(2,1)S(1)}, u32[]{:S(2)}, u32[]{:S(2)}) async-start(bf16[16,10,8,512]{3,2,1,0:T(8,128)(2,1)} %shard_map.91), calls=%async_computation | async-start | bytes 2621440 | tf_op jit(solution)/shard_map/all_to_all | solution.py:498
  8.7 3.4 %shard_map.92 = (bf16[8,10,8,512]{3,2,1,0:T(8,128)(2,1)}, bf16[8,10,8,512]{3,2,1,0:T(8,128)(2,1)}) custom-call(s32[2,64]{1,0:T(2,128)} %bitcast.6, s32[2,64]{1,0:T(2,128)} %bitcast.7, s32[2,64]{1,0:T(2,128)} %bitcast.9, s32[64,2,512]{2,1,0:T(2,128)} %refs_3_.2, bf16[64,2,512]{2,1,0:T(2,128)(2,1)} %refs_4_.2, s32[64,512]{1,0:T(8,128)} %refs_5_.2, ...), custom_call_target="tpu_custom_call" | custom-call | flops 100000000 | bytes 4000000 | tf_op jit(solution)/shard_map/pallas_call | solution.py:180
  12.1 0.4 collective-permute-start
  12.6 1.9 %collective-permute-done.taken = bf16[8,10,8,512]{3,2,1,0:T(8,128)(2,1)S(1)} collective-permute-done((bf16[8,10,8,512]{3,2,1,0:T(8,128)(2,1)}, bf16[8,10,8,512]{3,2,1,0:T(8,128)(2,1)S(1)}, u32[]{:S(2)}, u32[]{:S(2)}) %collective-permute-start) | collective-permute-done | bytes 655392 | tf_op jit(solution)/shard_map/ppermute | solution.py:500
  14.5 0.8 %copy-done.3 = bf16[8,10,8,512]{3,2,1,0:T(8,128)(2,1)} copy-done((bf16[8,10,8,512]{3,2,1,0:T(8,128)(2,1)}, bf16[8,10,8,512]{3,2,1,0:T(8,128)(2,1)S(1)}, u32[]{:S(2)}) %copy-start.3) | copy-done | bytes 655384
  15.3 2.3 %shard_map.93 = (bf16[4,10,8,512]{3,2,1,0:T(8,128)(2,1)}, bf16[4,10,8,512]{3,2,1,0:T(8,128)(2,1)}, bf16[4,10,8,512]{3,2,1,0:T(8,128)(2,1)}, bf16[4,10,8,512]{3,2,1,0:T(8,128)(2,1)}) custom-call(bf16[8,10,8,512]{3,2,1,0:T(8,128)(2,1)} %get-tuple-element.37.kept, bf16[8,10,8,512]{3,2,1,0:T(8,128)(2,1)} %copy-done.3), custom_call_target="tpu_custom_call" | custom-call | bytes 2621440 | tf_op jit(solution)/shard_map/pallas_call | solution.py:223
  17.7 1.6 %collective-permute-start.4 = (bf16[4,10,8,512]{3,2,1,0:T(8,128)(2,1)}, bf16[4,10,8,512]{3,2,1,0:T(8,128)(2,1)S(1)}, u32[]{:S(2)}, u32[]{:S(2)}) collective-permute-start(bf16[4,10,8,512]{3,2,1,0:T(8,128)(2,1)} %get-tuple-element.42), channel_id=1, source_target_pairs={{0,4},{1,1},{2,6},{3,3},{4,0},{5,5},{6,2},{7,7},{8,12},{9,9},{10,1... | collective-permute-start | bytes 983048 | tf_op jit(solution)/shard_map/ppermute | solution.py:505
  19.3 2.1 %collective-permute-start.3 = (bf16[4,10,8,512]{3,2,1,0:T(8,128)(2,1)}, bf16[4,10,8,512]{3,2,1,0:T(8,128)(2,1)S(1)}, u32[]{:S(2)}, u32[]{:S(2)}) collective-permute-start(bf16[4,10,8,512]{3,2,1,0:T(8,128)(2,1)} %get-tuple-element.41), channel_id=1, source_target_pairs={{0,2},{1,7},{2,0},{3,5},{4,6},{5,3},{6,4},{7,1},{8,10},{9,15},{10,... | collective-permute-start | bytes 983048 | tf_op jit(solution)/shard_map/ppermute | solution.py:505
  21.4 0.3 collective-permute-start.1
  21.7 1.2 %collective-permute-start.2 = (bf16[4,10,8,512]{3,2,1,0:T(8,128)(2,1)}, bf16[4,10,8,512]{3,2,1,0:T(8,128)(2,1)S(1)}, u32[]{:S(2)}, u32[]{:S(2)}) collective-permute-start(bf16[4,10,8,512]{3,2,1,0:T(8,128)(2,1)} %get-tuple-element.40), channel_id=1, source_target_pairs={{0,14},{1,13},{2,12},{3,15},{4,10},{5,9},{6,8},{7,11},{8,6},{9,5},... | collective-permute-start | bytes 983048 | tf_op jit(solution)/shard_map/ppermute | solution.py:505
  22.8 3.3 %all-to-all-done.refs_0_ = bf16[16,10,8,512]{3,2,1,0:T(8,128)(2,1)S(1)} async-done(((bf16[16,10,8,512]{3,2,1,0:T(8,128)(2,1)}), bf16[16,10,8,512]{3,2,1,0:T(8,128)(2,1)S(1)}, u32[]{:S(2)}, u32[]{:S(2)}) %all-to-all-start) | async-done | bytes 1310752 | tf_op jit(solution)/shard_map/all_to_all | solution.py:498
  26.1 5.6 %shard_map.94 = f32[72,8,128]{2,1,0:T(8,128)S(1)} custom-call(bf16[16,10,8,512]{3,2,1,0:T(8,128)(2,1)S(1)} %all-to-all-done.refs_0_), custom_call_target="tpu_custom_call" | custom-call | flops 1207959552 | bytes 1310720 | tf_op jit(solution)/shard_map/pallas_call | solution.py:352
  31.8 2.4 %collective-permute-start.5 = (f16[72,8,128]{2,1,0:T(8,128)(2,1)S(1)}, f16[72,8,128]{2,1,0:T(8,128)(2,1)S(1)}, u32[]{:S(2)}, u32[]{:S(2)}) collective-permute-start(f16[72,8,128]{2,1,0:T(8,128)(2,1)S(1)} %convert_element_type.6), channel_id=1, source_target_pairs={{0,24},{4,28},{8,16},{12,20},{16,8},{20,12},{24,0},{28,4},{1,25},{... | collective-permute-start | bytes 442376 | tf_op jit(solution)/shard_map/ppermute | solution.py:513
  34.2 1.5 %shard_map.95 = (f32[72,8,128]{2,1,0:T(8,128)S(1)}, f32[72,8,128]{2,1,0:T(8,128)S(1)}) custom-call(bf16[4,10,8,512]{3,2,1,0:T(8,128)(2,1)S(1)} %collective-permute-done.4.refs_0_), custom_call_target="tpu_custom_call" | custom-call | tf_op jit(solution)/shard_map/pallas_call | solution.py:352
  35.7 6.1 %collective-permute-done.3.refs_0_ = bf16[4,10,8,512]{3,2,1,0:T(8,128)(2,1)S(1)} collective-permute-done((bf16[4,10,8,512]{3,2,1,0:T(8,128)(2,1)}, bf16[4,10,8,512]{3,2,1,0:T(8,128)(2,1)S(1)}, u32[]{:S(2)}, u32[]{:S(2)}) %collective-permute-start.3) | collective-permute-done | bytes 327712 | tf_op jit(solution)/shard_map/ppermute | solution.py:505
  41.8 1.5 %shard_map.96 = (f32[72,8,128]{2,1,0:T(8,128)S(1)}, f32[72,8,128]{2,1,0:T(8,128)S(1)}) custom-call(bf16[4,10,8,512]{3,2,1,0:T(8,128)(2,1)S(1)} %collective-permute-done.3.refs_0_, f32[72,8,128]{2,1,0:T(8,128)S(1)} %get-tuple-element.45.refs_1_, f32[72,8,128]{2,1,0:T(8,128)S(1)} %get-tuple-element.47.refs_2_), custom_call_target="tpu_custom_call" | custom-call | tf_op jit(solution)/shard_map/pallas_call | solution.py:352
  43.4 0.0 copy-start
  43.4 0.0 copy-start.2
  43.4 1.5 %shard_map.98 = f32[72,8,128]{2,1,0:T(8,128)S(1)} custom-call(bf16[4,10,8,512]{3,2,1,0:T(8,128)(2,1)S(1)} %collective-permute-done.1.refs_0_, bf16[4,10,8,512]{3,2,1,0:T(8,128)(2,1)S(1)} %collective-permute-done.2.refs_1_, f32[72,8,128]{2,1,0:T(8,128)S(1)} %get-tuple-element.52.refs_2_), custom_call_target="tpu_custom_call" | custom-call | tf_op jit(solution)/shard_map/pallas_call | solution.py:352
  44.9 0.1 collective-permute-start.6
  45.0 1.5 %shard_map.97.total = f32[72,8,128]{2,1,0:T(8,128)S(1)} custom-call(bf16[4,10,8,512]{3,2,1,0:T(8,128)(2,1)S(1)} %collective-permute-done.1.refs_0_, bf16[4,10,8,512]{3,2,1,0:T(8,128)(2,1)S(1)} %collective-permute-done.2.refs_1_, f32[72,8,128]{2,1,0:T(8,128)S(1)} %get-tuple-element.51.refs_2_), custom_call_target="tpu_custom_call" | custom-call | tf_op jit(solution)/shard_map/pallas_call | solution.py:352
  46.5 0.1 collective-permute-done.6.other
  46.6 0.2 shard_map.99
  46.8 5.5 %collective-permute-start.8 = (f32[64,128]{1,0:T(8,128)S(1)}, f32[64,128]{1,0:T(8,128)S(1)}, u32[]{:S(2)}, u32[]{:S(2)}) collective-permute-start(f32[64,128]{1,0:T(8,128)S(1)} %get-tuple-element.55), channel_id=1, source_target_pairs={{4,8},{12,16},{20,24},{8,4},{16,12},{24,20},{5,9},{13,17},{21,25},... | collective-permute-start | bytes 98312 | tf_op jit(solution)/shard_map/ppermute | solution.py:391
  52.3 0.1 collective-permute-start.7
  52.4 1.6 %collective-permute-done.8 = f32[64,128]{1,0:T(8,128)S(1)} collective-permute-done((f32[64,128]{1,0:T(8,128)S(1)}, f32[64,128]{1,0:T(8,128)S(1)}, u32[]{:S(2)}, u32[]{:S(2)}) %collective-permute-start.8) | collective-permute-done | bytes 32800 | tf_op jit(solution)/shard_map/ppermute | solution.py:391
  54.0 1.1 %collective-permute-done.7 = f32[64,128]{1,0:T(8,128)S(1)} collective-permute-done((f32[64,128]{1,0:T(8,128)S(1)}, f32[64,128]{1,0:T(8,128)S(1)}, u32[]{:S(2)}, u32[]{:S(2)}) %collective-permute-start.7) | collective-permute-done | bytes 32800 | tf_op jit(solution)/shard_map/ppermute | solution.py:390
  55.2 4.2 %collective-permute-start.10 = (f32[10,8,128]{2,1,0:T(8,128)S(1)}, f32[10,8,128]{2,1,0:T(8,128)S(1)}, u32[]{:S(2)}, u32[]{:S(2)}) collective-permute-start(f32[10,8,128]{2,1,0:T(8,128)S(1)} %pad_maximum_fusion), channel_id=1, source_target_pairs={{1,2},{2,1},{5,6},{6,5},{9,10},{10,9},{13,14},{14,13},{17,18},{18,... | collective-permute-start | bytes 122888 | tf_op jit(solution)/shard_map/ppermute | solution.py:391
  59.4 0.1 collective-permute-start.9
  59.5 1.6 %collective-permute-done.10 = f32[10,8,128]{2,1,0:T(8,128)S(1)} collective-permute-done((f32[10,8,128]{2,1,0:T(8,128)S(1)}, f32[10,8,128]{2,1,0:T(8,128)S(1)}, u32[]{:S(2)}, u32[]{:S(2)}) %collective-permute-start.10) | collective-permute-done | bytes 40992 | tf_op jit(solution)/shard_map/ppermute | solution.py:391
  61.1 2.0 %shard_map.100 = f32[8,64,128]{2,1,0:T(8,128)} custom-call(f32[8,64,128]{2,1,0:T(8,128)S(1)} %get-tuple-element.54.merged, f32[64,128]{1,0:T(8,128)S(1)} %get-tuple-element.59.before, f32[64,128]{1,0:T(8,128)S(1)} %get-tuple-element.58.after, f32[10,8,128]{2,1,0:T(8,128)S(1)} %get-tuple-element.61.above, f32[10,8,128]{2,1,0:T(8,128)S(1)} %get-tuple-element.60.below, ...), custom_call_target="tpu_custom_call" | custom-call | tf_op jit(solution)/shard_map/pallas_call | solution.py:534
  (19 shorter events, 0.1 us)
Async XLA Ops:
  3.2 23.0 %all-to-all-start = ((bf16[16,10,8,512]{3,2,1,0:T(8,128)(2,1)}), bf16[16,10,8,512]{3,2,1,0:T(8,128)(2,1)S(1)}, u32[]{:S(2)}, u32[]{:S(2)}) async-start(bf16[16,10,8,512]{3,2,1,0:T(8,128)(2,1)} %shard_map.91), calls=%async_computation | async-start | bytes 2621440 | tf_op jit(solution)/shard_map/all_to_all | solution.py:498
  12.1 2.4 %collective-permute-start = (bf16[8,10,8,512]{3,2,1,0:T(8,128)(2,1)}, bf16[8,10,8,512]{3,2,1,0:T(8,128)(2,1)S(1)}, u32[]{:S(2)}, u32[]{:S(2)}) collective-permute-start(bf16[8,10,8,512]{3,2,1,0:T(8,128)(2,1)} %get-tuple-element.38), channel_id=1, source_target_pairs={{0,1},{1,0},{2,3},{3,2},{4,5},{5,4},{6,7},{7,6},{8,9},{9,8},{10,11... | collective-permute-start | bytes 1966088 | tf_op jit(solution)/shard_map/ppermute | solution.py:500
  14.5 0.8 %copy-start.3 = (bf16[8,10,8,512]{3,2,1,0:T(8,128)(2,1)}, bf16[8,10,8,512]{3,2,1,0:T(8,128)(2,1)S(1)}, u32[]{:S(2)}) copy-start(bf16[8,10,8,512]{3,2,1,0:T(8,128)(2,1)S(1)} %collective-permute-done.taken) | copy-start | bytes 1966084
  17.7 16.5 %collective-permute-start.4 = (bf16[4,10,8,512]{3,2,1,0:T(8,128)(2,1)}, bf16[4,10,8,512]{3,2,1,0:T(8,128)(2,1)S(1)}, u32[]{:S(2)}, u32[]{:S(2)}) collective-permute-start(bf16[4,10,8,512]{3,2,1,0:T(8,128)(2,1)} %get-tuple-element.42), channel_id=1, source_target_pairs={{0,4},{1,1},{2,6},{3,3},{4,0},{5,5},{6,2},{7,7},{8,12},{9,9},{10,1... | collective-permute-start | bytes 983048 | tf_op jit(solution)/shard_map/ppermute | solution.py:505
  19.3 22.5 %collective-permute-start.3 = (bf16[4,10,8,512]{3,2,1,0:T(8,128)(2,1)}, bf16[4,10,8,512]{3,2,1,0:T(8,128)(2,1)S(1)}, u32[]{:S(2)}, u32[]{:S(2)}) collective-permute-start(bf16[4,10,8,512]{3,2,1,0:T(8,128)(2,1)} %get-tuple-element.41), channel_id=1, source_target_pairs={{0,2},{1,7},{2,0},{3,5},{4,6},{5,3},{6,4},{7,1},{8,10},{9,15},{10,... | collective-permute-start | bytes 983048 | tf_op jit(solution)/shard_map/ppermute | solution.py:505
  21.4 22.0 %collective-permute-start.1 = (bf16[4,10,8,512]{3,2,1,0:T(8,128)(2,1)}, bf16[4,10,8,512]{3,2,1,0:T(8,128)(2,1)S(1)}, u32[]{:S(2)}, u32[]{:S(2)}) collective-permute-start(bf16[4,10,8,512]{3,2,1,0:T(8,128)(2,1)} %get-tuple-element.39), channel_id=1, source_target_pairs={{0,8},{1,11},{2,10},{3,9},{4,12},{5,15},{6,14},{7,13},{8,0},{9,3},... | collective-permute-start | bytes 983048 | tf_op jit(solution)/shard_map/ppermute | solution.py:505
  21.7 21.7 %collective-permute-start.2 = (bf16[4,10,8,512]{3,2,1,0:T(8,128)(2,1)}, bf16[4,10,8,512]{3,2,1,0:T(8,128)(2,1)S(1)}, u32[]{:S(2)}, u32[]{:S(2)}) collective-permute-start(bf16[4,10,8,512]{3,2,1,0:T(8,128)(2,1)} %get-tuple-element.40), channel_id=1, source_target_pairs={{0,14},{1,13},{2,12},{3,15},{4,10},{5,9},{6,8},{7,11},{8,6},{9,5},... | collective-permute-start | bytes 983048 | tf_op jit(solution)/shard_map/ppermute | solution.py:505
  31.8 11.5 %collective-permute-start.5 = (f16[72,8,128]{2,1,0:T(8,128)(2,1)S(1)}, f16[72,8,128]{2,1,0:T(8,128)(2,1)S(1)}, u32[]{:S(2)}, u32[]{:S(2)}) collective-permute-start(f16[72,8,128]{2,1,0:T(8,128)(2,1)S(1)} %convert_element_type.6), channel_id=1, source_target_pairs={{0,24},{4,28},{8,16},{12,20},{16,8},{20,12},{24,0},{28,4},{1,25},{... | collective-permute-start | bytes 442376 | tf_op jit(solution)/shard_map/ppermute | solution.py:513
  43.4 3.2 %copy-start = (f32[8,64,128]{2,1,0:T(8,128)S(1)}, f32[8,64,128]{2,1,0:T(8,128)}, u32[]{:S(2)}) copy-start(f32[8,64,128]{2,1,0:T(8,128)} %land_flux.1) | copy-start | bytes 786436
  43.4 3.2 %copy-start.1 = (f32[64,128]{1,0:T(8,128)S(1)}, f32[64,128]{1,0:T(8,128)}, u32[]{:S(2)}) copy-start(f32[64,128]{1,0:T(8,128)} %kappa.3) | copy-start | bytes 98308
  43.4 3.2 %copy-start.2 = (f32[64,128]{1,0:T(8,128)S(1)}, f32[64,128]{1,0:T(8,128)}, u32[]{:S(2)}) copy-start(f32[64,128]{1,0:T(8,128)} %land_area.1) | copy-start | bytes 98308
  44.9 1.6 %collective-permute-start.6 = (f32[72,8,128]{2,1,0:T(8,128)S(1)}, f32[72,8,128]{2,1,0:T(8,128)S(1)}, u32[]{:S(2)}, u32[]{:S(2)}) collective-permute-start(f32[72,8,128]{2,1,0:T(8,128)S(1)} %shard_map.98), channel_id=1, source_target_pairs={{0,1},{1,0},{2,3},{3,2},{4,5},{5,4},{6,7},{7,6},{8,9},{9,8},{10,11... | collective-permute-start | bytes 884744 | tf_op jit(solution)/shard_map/ppermute | solution.py:527
  46.8 7.2 %collective-permute-start.8 = (f32[64,128]{1,0:T(8,128)S(1)}, f32[64,128]{1,0:T(8,128)S(1)}, u32[]{:S(2)}, u32[]{:S(2)}) collective-permute-start(f32[64,128]{1,0:T(8,128)S(1)} %get-tuple-element.55), channel_id=1, source_target_pairs={{4,8},{12,16},{20,24},{8,4},{16,12},{24,20},{5,9},{13,17},{21,25},... | collective-permute-start | bytes 98312 | tf_op jit(solution)/shard_map/ppermute | solution.py:391
  52.3 2.8 %collective-permute-start.7 = (f32[64,128]{1,0:T(8,128)S(1)}, f32[64,128]{1,0:T(8,128)S(1)}, u32[]{:S(2)}, u32[]{:S(2)}) collective-permute-start(f32[64,128]{1,0:T(8,128)S(1)} %get-tuple-element.55), channel_id=1, source_target_pairs={{0,4},{4,0},{8,12},{12,8},{16,20},{20,16},{24,28},{28,24},{1,5},{5... | collective-permute-start | bytes 98312 | tf_op jit(solution)/shard_map/ppermute | solution.py:390
  55.2 5.9 %collective-permute-start.10 = (f32[10,8,128]{2,1,0:T(8,128)S(1)}, f32[10,8,128]{2,1,0:T(8,128)S(1)}, u32[]{:S(2)}, u32[]{:S(2)}) collective-permute-start(f32[10,8,128]{2,1,0:T(8,128)S(1)} %pad_maximum_fusion), channel_id=1, source_target_pairs={{1,2},{2,1},{5,6},{6,5},{9,10},{10,9},{13,14},{14,13},{17,18},{18,... | collective-permute-start | bytes 122888 | tf_op jit(solution)/shard_map/ppermute | solution.py:391
  59.4 1.7 %collective-permute-start.9 = (f32[10,8,128]{2,1,0:T(8,128)S(1)}, f32[10,8,128]{2,1,0:T(8,128)S(1)}, u32[]{:S(2)}, u32[]{:S(2)}) collective-permute-start(f32[10,8,128]{2,1,0:T(8,128)S(1)} %pad_maximum_fusion), channel_id=1, source_target_pairs={{0,1},{1,0},{2,3},{3,2},{4,5},{5,4},{6,7},{7,6},{8,9},{9,8},{10,11... | collective-permute-start | bytes 122888 | tf_op jit(solution)/shard_map/ppermute | solution.py:390

commit v6 on v5

--- a/solution.py
+++ b/solution.py
@@ -13,8 +13,9 @@
 SWEEPS = 3
 LAYERS = 4
 EDGE = 4
-MEAN_SCALE = 2.0**8
+MEAN_SCALE = 2.0**13
 WEIGHT_SCALE = 2.0**-2
+PART = 4
 TOGETHER = 8
 LANE_BLOCK = 14
 
@@ -50,8 +51,14 @@
 
 
 def pack_kernel(cap, near, mirror, *refs):
-    given, outs, held, out_held = refs[:7], refs[7:-12], refs[-12:-5], refs[-5]
-    count, source, in_sems, out_sems = refs[-4:]
+    if near:
+        given, outs, held = refs[:7], refs[7:-10], refs[-10:-3]
+        count, source, in_sems = refs[-3:]
+        blocks = outs
+    else:
+        given, out, held = refs[:7], refs[7], refs[8:15]
+        out_held, count, source, in_sems, out_sems = refs[15:]
+        blocks = [out_held.at[pl.ds(i * PART, PART)] for i in range(out.shape[0] // PART)]
     copies = [
         pltpu.make_async_copy(given[i], held[i], in_sems.at[i]) for i in range(len(given))
     ]
@@ -59,7 +66,8 @@
         copies[i].start()
     dest_s, dest_v, tile_v, target, weight, mask, fields = held
     crossings, tiles = dest_v.shape
-    half, cells = out_held.shape[0], fields.shape[2]
+    step = blocks[0].shape[0]
+    half, cells = len(blocks) * step, fields.shape[2]
     owners, slots = 2 * half, half * cap
     me = lax.axis_index("gx") * lax.axis_size("gy") + lax.axis_index("gy")
     first = me // half * half
@@ -104,30 +112,25 @@
         lax.fori_loop(0, tiles, enter, 0, unroll=16)
 
     copies[6].wait()
-    parts = out_sems.shape[0] // 2
-    step = half // parts
     sent = []
 
     def send(part, rows):
-        into = outs[part * step // outs[0].shape[0]]
-        there = part * step % outs[0].shape[0]
-        copy = pltpu.make_async_copy(
-            out_held.at[pl.ds(part * step, step), rows],
-            into.at[pl.ds(there, step), rows],
-            out_sems.at[len(sent)],
-        )
+        if near:
+            return
+        into = out.at[pl.ds(part * step, step), rows]
+        copy = pltpu.make_async_copy(blocks[part].at[:, rows], into, out_sems.at[len(sent)])
         copy.start()
         sent.append(copy)
 
-    for part in range(parts):
+    for part, block in enumerate(blocks):
 
         def fill(g, carry):
-            owner = owner_of(g)
+            owner = owner_of(part * step + g)
             for n in range(cap):
-                out_held[g, n] = fields[source[owner * cap + n]]
+                block[g, n] = fields[source[owner * cap + n]]
             return carry
 
-        lax.fori_loop(part * step, (part + 1) * step, fill, 0, unroll=2)
+        lax.fori_loop(0, step, fill, 0, unroll=2)
         send(part, pl.ds(0, cap))
 
     for copy in copies[1:6]:
@@ -164,9 +167,10 @@
     for g in range(half):
         for row, packed in ((cap, packed_w), (cap + 1, packed_c)):
             rows = packed[g * cap : (g + 1) * cap]
-            out_held[g, row] = rows if cap == 8 else jnp.concatenate([rows, spare], axis=0)
-
-    for part in range(parts):
+            rows = rows if cap == 8 else jnp.concatenate([rows, spare], axis=0)
+            blocks[g // step][g % step, row] = rows
+
+    for part in range(len(blocks)):
         send(part, pl.ds(cap, 2))
     for copy in sent:
         copy.wait()
@@ -177,45 +181,34 @@
     shape = (half, cap + 2) + fields.shape[1:]
     parts = 2 if near else 1
     given = (dest, dest, tile, target, weight, mask, fields)
+    scratch = [pltpu.SMEM(dest.shape, I32)] + [pltpu.VMEM(a.shape, a.dtype) for a in given[1:]]
+    if not near:
+        scratch.append(pltpu.VMEM(shape, BF16))
+    scratch += [
+        pltpu.SMEM((owners,), I32),
+        pltpu.SMEM((owners * cap,), I32),
+        pltpu.SemaphoreType.DMA((len(given),)),
+    ]
+    if not near:
+        scratch.append(pltpu.SemaphoreType.DMA((2 * (half // PART),)))
     return pl.pallas_call(
         functools.partial(pack_kernel, cap, near, mirror),
         out_shape=[jax.ShapeDtypeStruct((half // parts,) + shape[1:], BF16)] * parts,
         in_specs=[HBM] * len(given),
-        out_specs=[HBM] * parts,
-        scratch_shapes=[pltpu.SMEM(dest.shape, I32)]
-        + [pltpu.VMEM(a.shape, a.dtype) for a in given[1:]]
-        + [
-            pltpu.VMEM(shape, BF16),
-            pltpu.SMEM((owners,), I32),
-            pltpu.SMEM((owners * cap,), I32),
-            pltpu.SemaphoreType.DMA((len(given),)),
-            pltpu.SemaphoreType.DMA((8,)),
-        ],
-        compiler_params=params(62),
+        out_specs=[VMEM if near else HBM] * parts,
+        scratch_shapes=scratch,
+        compiler_params=params(50 if near else 62),
         cost_estimate=pl.CostEstimate(
             flops=10**8, bytes_accessed=4 * 10**6, transcendentals=0
         ),
     )(*given)
 
 
-def join_kernel(kept, taken, *refs):
-    outs, (held, in_sems, out_sems) = refs[:-3], refs[-3:]
-    arriving = []
-    for j in range(len(outs)):
+def join_kernel(kept, taken, *outs):
+    for j, out in enumerate(outs):
         for rel in range(2):
-            for src, blocks in enumerate((kept, taken)):
-                at = 4 * j + 2 * rel + src
-                copy = pltpu.make_async_copy(blocks.at[2 * j + rel], held.at[at], in_sems.at[at])
-                copy.start()
-                arriving.append(copy)
-    leaving = []
-    for j, out in enumerate(outs):
-        for copy in arriving[4 * j : 4 * j + 4]:
-            copy.wait()
-        leaving.append(pltpu.make_async_copy(held.at[pl.ds(4 * j, 4)], out, out_sems.at[j]))
-        leaving[-1].start()
-    for copy in leaving:
-        copy.wait()
+            out[2 * rel] = kept[2 * j + rel]
+            out[2 * rel + 1] = taken[2 * j + rel]
 
 
 def join(kept, taken):
@@ -223,14 +216,9 @@
     return pl.pallas_call(
         join_kernel,
         out_shape=[jax.ShapeDtypeStruct((4,) + taken.shape[1:], BF16)] * number,
-        in_specs=[HBM] * 2,
-        out_specs=[HBM] * number,
-        scratch_shapes=[
-            pltpu.VMEM((4 * number,) + taken.shape[1:], BF16),
-            pltpu.SemaphoreType.DMA((4 * number,)),
-            pltpu.SemaphoreType.DMA((number,)),
-        ],
-        compiler_params=params(62),
+        in_specs=[VMEM] * 2,
+        out_specs=[VMEM] * number,
+        compiler_params=params(),
         cost_estimate=pl.CostEstimate(
             flops=0, bytes_accessed=4 * taken.size * 2, transcendentals=0
         ),
@@ -504,9 +492,8 @@
         pairing = [(i, i ^ 2 * carried(j, i & 1)) for i in everywhere]
         return lax.ppermute(messages[j], ("gx", "gy"), pairing)
 
-    half_way = len(messages) // 2
-    soon = [deliver(j) for j in range(half_way)]
-    late = [deliver(j) for j in range(half_way, len(messages))]
+    soon = [deliver(j) for j in range(0, len(messages), 2)]
+    late = [deliver(j) for j in range(1, len(messages), 2)]
 
     far_total = bin_all([far_got], [[(0, 0, half)]], [], cap, rows_here, averaged=True)[0]
     opposite = [(i, i ^ (mirror // width_y)) for i in range(width_x)]
@@ -522,8 +509,9 @@
         totals = sums([message], 0, 1, earlier=totals)
         far_total = totals[0]
     own, other = totals
-    late, own, passed = lax.optimization_barrier((late, own, passed))
+    late, own = lax.optimization_barrier((late, own))
     other = sums(late, 1, earlier=[other])[0]
+    other, passed = lax.optimization_barrier((other, passed))
     other = lax.ppermute(other, ("gx", "gy"), [(i, i ^ 1) for i in everywhere])
     own = sums(late, 0, earlier=[own])[0]
 

time: 63.4 us -> 61.9 us (0.976)
  the two profiles are of different devices: /device:TPU:9 before, /device:TPU:21 now
where the time goes in v6:
time: 61.9 us; the launch traced here: 61.2 us
  starting transfers between devices  21.9 us (35%)
  Pallas kernels  20.6 us (33%)
  waiting for transfers between devices  18.3 us (30%)
    pallas_call x5, Pallas kernels, bin_all(): pl.pallas_call(functools.partial(bin_slots, cap, picked, len(arrays), ave...  11.6 us
    ppermute x2, starting transfers between devices, neighbours(): two = lax.ppermute(values, axis, second)  8.72 us
    all_to_all x1, waiting for transfers between devices, shards(): far_got = exchange(far_slots)  7.43 us
    pallas_call x2, Pallas kernels, pack(): pl.pallas_call(functools.partial(pack_kernel, cap, near, mirror), out_sha...  5.76 us
    all_to_all x1, starting transfers between devices, shards(): far_got = exchange(far_slots)  5.71 us
    ppermute x4, starting transfers between devices, deliver(): return lax.ppermute(messages[j], ('gx', 'gy'), pairing)  5.17 us
    ppermute x4, waiting for transfers between devices, deliver(): return lax.ppermute(messages[j], ('gx', 'gy'), pairing)  4.83 us
    ppermute x2, waiting for transfers between devices, neighbours(): two = lax.ppermute(values, axis, second)  3.33 us
  transfers between devices with their start and end apart: 12, of which 6 were waited for; matrix products, arithmetic and copies ran while one was open for 0% of the time, Pallas kernels for 25%

profile of v6, /device:TPU:21, one launch (start us, length us, event | category | flops | bytes accessed | tf_op | source)
XLA Modules:
  0.0 61.2 jit_solution(13847108675356469204)
XLA Ops:
  0.0 3.2 %shard_map.91 = bf16[16,10,8,512]{3,2,1,0:T(8,128)(2,1)} custom-call(s32[2,64]{1,0:T(2,128)} %bitcast.4, s32[2,64]{1,0:T(2,128)} %bitcast.5, s32[2,64]{1,0:T(2,128)} %bitcast.8, s32[64,2,512]{2,1,0:T(2,128)} %refs_3_.2, bf16[64,2,512]{2,1,0:T(2,128)(2,1)} %refs_4_.2, s32[64,512]{1,0:T(8,128)} %refs_5_.2, bf16[64,8,512]{2,1,0:T(8,128)(2,1)} %refs_6_.2), custom_call_target="tpu_custom_call" | custom-call | flops 100000000 | bytes 4000000 | tf_op jit(solution)/shard_map/pallas_call | solution.py:194
  3.2 0.0 copy-start
  3.2 0.0 copy-start.1
  3.2 0.0 copy-start.3
  3.2 0.0 copy-start.7
  3.2 5.7 %all-to-all-start = ((bf16[16,10,8,512]{3,2,1,0:T(8,128)(2,1)}), bf16[16,10,8,512]{3,2,1,0:T(8,128)(2,1)S(1)}, u32[]{:S(2)}, u32[]{:S(2)}) async-start(bf16[16,10,8,512]{3,2,1,0:T(8,128)(2,1)} %shard_map.91), calls=%async_computation | async-start | bytes 2621440 | tf_op jit(solution)/shard_map/all_to_all | solution.py:486
  9.0 2.6 %shard_map.92 = (bf16[8,10,8,512]{3,2,1,0:T(8,128)(2,1)S(1)}, bf16[8,10,8,512]{3,2,1,0:T(8,128)(2,1)S(1)}) custom-call(s32[2,64]{1,0:T(2,128)S(1)} %bitcast.6, s32[2,64]{1,0:T(2,128)S(1)} %bitcast.7, s32[2,64]{1,0:T(2,128)S(1)} %bitcast.9, s32[64,2,512]{2,1,0:T(2,128)S(1)} %copy-done.1, bf16[64,2,512]{2,1,0:T(2,128)(2,1)S(1)} %copy-done.2, ...), custom_call_target="tpu_custom_call" | custom-call | flops 100000000 | bytes 4000000 | tf_op jit(solution)/shard_map/pallas_call | solution.py:194
  11.6 0.4 collective-permute-start
  12.0 1.7 %collective-permute-done.taken = bf16[8,10,8,512]{3,2,1,0:T(8,128)(2,1)S(1)} collective-permute-done((bf16[8,10,8,512]{3,2,1,0:T(8,128)(2,1)S(1)}, bf16[8,10,8,512]{3,2,1,0:T(8,128)(2,1)S(1)}, u32[]{:S(2)}, u32[]{:S(2)}) %collective-permute-start) | collective-permute-done | bytes 655392 | tf_op jit(solution)/shard_map/ppermute | solution.py:488
  13.8 0.9 %shard_map.93 = (bf16[4,10,8,512]{3,2,1,0:T(8,128)(2,1)}, bf16[4,10,8,512]{3,2,1,0:T(8,128)(2,1)S(1)}, bf16[4,10,8,512]{3,2,1,0:T(8,128)(2,1)}, bf16[4,10,8,512]{3,2,1,0:T(8,128)(2,1)S(1)}) custom-call(bf16[8,10,8,512]{3,2,1,0:T(8,128)(2,1)S(1)} %get-tuple-element.38.kept, bf16[8,10,8,512]{3,2,1,0:T(8,128)(2,1)S(1)} %collective-permute-done.taken), custom_call_target="tpu_custom_call" | custom-call | bytes 2621440 | tf_op jit(solution)/shard_map/pallas_call | solution.py:216
  14.7 1.6 %collective-permute-start.4 = (bf16[4,10,8,512]{3,2,1,0:T(8,128)(2,1)}, bf16[4,10,8,512]{3,2,1,0:T(8,128)(2,1)S(1)}, u32[]{:S(2)}, u32[]{:S(2)}) collective-permute-start(bf16[4,10,8,512]{3,2,1,0:T(8,128)(2,1)} %get-tuple-element.43), channel_id=1, source_target_pairs={{0,4},{1,1},{2,6},{3,3},{4,0},{5,5},{6,2},{7,7},{8,12},{9,9},{10,1... | collective-permute-start | bytes 983048 | tf_op jit(solution)/shard_map/ppermute | solution.py:493
  16.3 2.1 %collective-permute-start.3 = (bf16[4,10,8,512]{3,2,1,0:T(8,128)(2,1)}, bf16[4,10,8,512]{3,2,1,0:T(8,128)(2,1)S(1)}, u32[]{:S(2)}, u32[]{:S(2)}) collective-permute-start(bf16[4,10,8,512]{3,2,1,0:T(8,128)(2,1)} %get-tuple-element.42), channel_id=1, source_target_pairs={{0,8},{1,11},{2,10},{3,9},{4,12},{5,15},{6,14},{7,13},{8,0},{9,3},... | collective-permute-start | bytes 983048 | tf_op jit(solution)/shard_map/ppermute | solution.py:493
  18.4 0.3 collective-permute-start.1
  18.7 1.2 %collective-permute-start.2 = (bf16[4,10,8,512]{3,2,1,0:T(8,128)(2,1)S(1)}, bf16[4,10,8,512]{3,2,1,0:T(8,128)(2,1)S(1)}, u32[]{:S(2)}, u32[]{:S(2)}) collective-permute-start(bf16[4,10,8,512]{3,2,1,0:T(8,128)(2,1)S(1)} %get-tuple-element.41), channel_id=1, source_target_pairs={{0,14},{1,13},{2,12},{3,15},{4,10},{5,9},{6,8},{7,11},{8,6},{9,5},... | collective-permute-start | bytes 983048 | tf_op jit(solution)/shard_map/ppermute | solution.py:493
  19.9 7.4 %all-to-all-done.refs_0_ = bf16[16,10,8,512]{3,2,1,0:T(8,128)(2,1)S(1)} async-done(((bf16[16,10,8,512]{3,2,1,0:T(8,128)(2,1)}), bf16[16,10,8,512]{3,2,1,0:T(8,128)(2,1)S(1)}, u32[]{:S(2)}, u32[]{:S(2)}) %all-to-all-start) | async-done | bytes 1310752 | tf_op jit(solution)/shard_map/all_to_all | solution.py:486
  27.3 5.6 %shard_map.94 = f32[72,8,128]{2,1,0:T(8,128)S(1)} custom-call(bf16[16,10,8,512]{3,2,1,0:T(8,128)(2,1)S(1)} %all-to-all-done.refs_0_), custom_call_target="tpu_custom_call" | custom-call | flops 1207959552 | bytes 1310720 | tf_op jit(solution)/shard_map/pallas_call | solution.py:340
  33.0 1.2 %collective-permute-start.5 = (f16[72,8,128]{2,1,0:T(8,128)(2,1)S(1)}, f16[72,8,128]{2,1,0:T(8,128)(2,1)S(1)}, u32[]{:S(2)}, u32[]{:S(2)}) collective-permute-start(f16[72,8,128]{2,1,0:T(8,128)(2,1)S(1)} %convert_element_type.6), channel_id=1, source_target_pairs={{0,24},{4,28},{8,16},{12,20},{16,8},{20,12},{24,0},{28,4},{1,25},{... | collective-permute-start | bytes 442376 | tf_op jit(solution)/shard_map/ppermute | solution.py:500
  34.2 1.5 %shard_map.95 = (f32[72,8,128]{2,1,0:T(8,128)S(1)}, f32[72,8,128]{2,1,0:T(8,128)S(1)}) custom-call(bf16[4,10,8,512]{3,2,1,0:T(8,128)(2,1)S(1)} %collective-permute-done.4.refs_0_), custom_call_target="tpu_custom_call" | custom-call | tf_op jit(solution)/shard_map/pallas_call | solution.py:340
  35.8 1.5 %shard_map.96 = (f32[72,8,128]{2,1,0:T(8,128)S(1)}, f32[72,8,128]{2,1,0:T(8,128)S(1)}) custom-call(bf16[4,10,8,512]{3,2,1,0:T(8,128)(2,1)S(1)} %collective-permute-done.3.refs_0_, f32[72,8,128]{2,1,0:T(8,128)S(1)} %get-tuple-element.46.refs_1_, f32[72,8,128]{2,1,0:T(8,128)S(1)} %get-tuple-element.48.refs_2_), custom_call_target="tpu_custom_call" | custom-call | tf_op jit(solution)/shard_map/pallas_call | solution.py:340
  37.2 4.8 %collective-permute-done.1.refs_0_ = bf16[4,10,8,512]{3,2,1,0:T(8,128)(2,1)S(1)} collective-permute-done((bf16[4,10,8,512]{3,2,1,0:T(8,128)(2,1)S(1)}, bf16[4,10,8,512]{3,2,1,0:T(8,128)(2,1)S(1)}, u32[]{:S(2)}, u32[]{:S(2)}) %collective-permute-start.1) | collective-permute-done | bytes 327712 | tf_op jit(solution)/shard_map/ppermute | solution.py:493
  42.1 1.5 %shard_map.98 = f32[72,8,128]{2,1,0:T(8,128)S(1)} custom-call(bf16[4,10,8,512]{3,2,1,0:T(8,128)(2,1)S(1)} %collective-permute-done.1.refs_0_, bf16[4,10,8,512]{3,2,1,0:T(8,128)(2,1)S(1)} %collective-permute-done.2.refs_1_, f32[72,8,128]{2,1,0:T(8,128)S(1)} %get-tuple-element.53.refs_2_), custom_call_target="tpu_custom_call" | custom-call | tf_op jit(solution)/shard_map/pallas_call | solution.py:340
  43.6 0.4 collective-permute-start.6
  44.1 1.5 %shard_map.97.total = f32[72,8,128]{2,1,0:T(8,128)S(1)} custom-call(bf16[4,10,8,512]{3,2,1,0:T(8,128)(2,1)S(1)} %collective-permute-done.1.refs_0_, bf16[4,10,8,512]{3,2,1,0:T(8,128)(2,1)S(1)} %collective-permute-done.2.refs_1_, f32[72,8,128]{2,1,0:T(8,128)S(1)} %get-tuple-element.52.refs_2_), custom_call_target="tpu_custom_call" | custom-call | tf_op jit(solution)/shard_map/pallas_call | solution.py:340
  45.6 0.2 shard_map.99
  45.8 3.7 %collective-permute-start.8 = (f32[64,128]{1,0:T(8,128)S(1)}, f32[64,128]{1,0:T(8,128)S(1)}, u32[]{:S(2)}, u32[]{:S(2)}) collective-permute-start(f32[64,128]{1,0:T(8,128)S(1)} %get-tuple-element.57), channel_id=1, source_target_pairs={{4,8},{12,16},{20,24},{8,4},{16,12},{24,20},{5,9},{13,17},{21,25},... | collective-permute-start | bytes 98312 | tf_op jit(solution)/shard_map/ppermute | solution.py:379
  49.5 0.1 collective-permute-start.7
  49.6 1.8 %collective-permute-done.8 = f32[64,128]{1,0:T(8,128)S(1)} collective-permute-done((f32[64,128]{1,0:T(8,128)S(1)}, f32[64,128]{1,0:T(8,128)S(1)}, u32[]{:S(2)}, u32[]{:S(2)}) %collective-permute-start.8) | collective-permute-done | bytes 32800 | tf_op jit(solution)/shard_map/ppermute | solution.py:379
  51.4 1.0 %collective-permute-done.7 = f32[64,128]{1,0:T(8,128)S(1)} collective-permute-done((f32[64,128]{1,0:T(8,128)S(1)}, f32[64,128]{1,0:T(8,128)S(1)}, u32[]{:S(2)}, u32[]{:S(2)}) %collective-permute-start.7) | collective-permute-done | bytes 32800 | tf_op jit(solution)/shard_map/ppermute | solution.py:378
  52.4 5.0 %collective-permute-start.10 = (f32[10,8,128]{2,1,0:T(8,128)S(1)}, f32[10,8,128]{2,1,0:T(8,128)S(1)}, u32[]{:S(2)}, u32[]{:S(2)}) collective-permute-start(f32[10,8,128]{2,1,0:T(8,128)S(1)} %pad_maximum_fusion), channel_id=1, source_target_pairs={{1,2},{2,1},{5,6},{6,5},{9,10},{10,9},{13,14},{14,13},{17,18},{18,... | collective-permute-start | bytes 122888 | tf_op jit(solution)/shard_map/ppermute | solution.py:379
  57.5 0.1 collective-permute-start.9
  57.5 1.6 %collective-permute-done.10 = f32[10,8,128]{2,1,0:T(8,128)S(1)} collective-permute-done((f32[10,8,128]{2,1,0:T(8,128)S(1)}, f32[10,8,128]{2,1,0:T(8,128)S(1)}, u32[]{:S(2)}, u32[]{:S(2)}) %collective-permute-start.10) | collective-permute-done | bytes 40992 | tf_op jit(solution)/shard_map/ppermute | solution.py:379
  59.1 2.0 %shard_map.100 = f32[8,64,128]{2,1,0:T(8,128)} custom-call(f32[8,64,128]{2,1,0:T(8,128)S(1)} %get-tuple-element.56.merged, f32[64,128]{1,0:T(8,128)S(1)} %get-tuple-element.61.before, f32[64,128]{1,0:T(8,128)S(1)} %get-tuple-element.60.after, f32[10,8,128]{2,1,0:T(8,128)S(1)} %get-tuple-element.63.above, f32[10,8,128]{2,1,0:T(8,128)S(1)} %get-tuple-element.62.below, ...), custom_call_target="tpu_custom_call" | custom-call | tf_op jit(solution)/shard_map/pallas_call | solution.py:522
  (29 shorter events, 0.2 us)
Async XLA Ops:
  3.2 5.8 %copy-start = (bf16[64,8,512]{2,1,0:T(8,128)(2,1)S(1)}, bf16[64,8,512]{2,1,0:T(8,128)(2,1)}, u32[]{:S(2)}) copy-start(bf16[64,8,512]{2,1,0:T(8,128)(2,1)} %refs_6_.2) | copy-start | bytes 1572868
  3.2 5.8 %copy-start.1 = (s32[64,2,512]{2,1,0:T(2,128)S(1)}, s32[64,2,512]{2,1,0:T(2,128)}, u32[]{:S(2)}) copy-start(s32[64,2,512]{2,1,0:T(2,128)} %refs_3_.2) | copy-start | bytes 786436
  3.2 5.8 %copy-start.2 = (bf16[64,2,512]{2,1,0:T(2,128)(2,1)S(1)}, bf16[64,2,512]{2,1,0:T(2,128)(2,1)}, u32[]{:S(2)}) copy-start(bf16[64,2,512]{2,1,0:T(2,128)(2,1)} %refs_4_.2) | copy-start | bytes 393220
  3.2 5.8 %copy-start.3 = (s32[64,512]{1,0:T(8,128)S(1)}, s32[64,512]{1,0:T(8,128)}, u32[]{:S(2)}) copy-start(s32[64,512]{1,0:T(8,128)} %refs_5_.2) | copy-start | bytes 393220
  3.2 5.8 %copy-start.7 = (s32[64,2]{0,1:T(2,128)S(1)}, s32[64,2]{0,1:T(2,128)}, u32[]{:S(2)}) copy-start(s32[64,2]{0,1:T(2,128)} %param.10) | copy-start | bytes 1540
  3.2 5.8 %copy-start.8 = (s32[64,2]{0,1:T(2,128)S(1)}, s32[64,2]{0,1:T(2,128)}, u32[]{:S(2)}) copy-start(s32[64,2]{0,1:T(2,128)} %param.11) | copy-start | bytes 1540
  3.2 24.1 %all-to-all-start = ((bf16[16,10,8,512]{3,2,1,0:T(8,128)(2,1)}), bf16[16,10,8,512]{3,2,1,0:T(8,128)(2,1)S(1)}, u32[]{:S(2)}, u32[]{:S(2)}) async-start(bf16[16,10,8,512]{3,2,1,0:T(8,128)(2,1)} %shard_map.91), calls=%async_computation | async-start | bytes 2621440 | tf_op jit(solution)/shard_map/all_to_all | solution.py:486
  11.6 2.2 %collective-permute-start = (bf16[8,10,8,512]{3,2,1,0:T(8,128)(2,1)S(1)}, bf16[8,10,8,512]{3,2,1,0:T(8,128)(2,1)S(1)}, u32[]{:S(2)}, u32[]{:S(2)}) collective-permute-start(bf16[8,10,8,512]{3,2,1,0:T(8,128)(2,1)S(1)} %get-tuple-element.39), channel_id=1, source_target_pairs={{0,1},{1,0},{2,3},{3,2},{4,5},{5,4},{6,7},{7,6},{8,9},{9,8},{10,11... | collective-permute-start | bytes 1966088 | tf_op jit(solution)/shard_map/ppermute | solution.py:488
  14.7 19.5 %collective-permute-start.4 = (bf16[4,10,8,512]{3,2,1,0:T(8,128)(2,1)}, bf16[4,10,8,512]{3,2,1,0:T(8,128)(2,1)S(1)}, u32[]{:S(2)}, u32[]{:S(2)}) collective-permute-start(bf16[4,10,8,512]{3,2,1,0:T(8,128)(2,1)} %get-tuple-element.43), channel_id=1, source_target_pairs={{0,4},{1,1},{2,6},{3,3},{4,0},{5,5},{6,2},{7,7},{8,12},{9,9},{10,1... | collective-permute-start | bytes 983048 | tf_op jit(solution)/shard_map/ppermute | solution.py:493
  16.3 19.4 %collective-permute-start.3 = (bf16[4,10,8,512]{3,2,1,0:T(8,128)(2,1)}, bf16[4,10,8,512]{3,2,1,0:T(8,128)(2,1)S(1)}, u32[]{:S(2)}, u32[]{:S(2)}) collective-permute-start(bf16[4,10,8,512]{3,2,1,0:T(8,128)(2,1)} %get-tuple-element.42), channel_id=1, source_target_pairs={{0,8},{1,11},{2,10},{3,9},{4,12},{5,15},{6,14},{7,13},{8,0},{9,3},... | collective-permute-start | bytes 983048 | tf_op jit(solution)/shard_map/ppermute | solution.py:493
  18.4 23.6 %collective-permute-start.1 = (bf16[4,10,8,512]{3,2,1,0:T(8,128)(2,1)S(1)}, bf16[4,10,8,512]{3,2,1,0:T(8,128)(2,1)S(1)}, u32[]{:S(2)}, u32[]{:S(2)}) collective-permute-start(bf16[4,10,8,512]{3,2,1,0:T(8,128)(2,1)S(1)} %get-tuple-element.40), channel_id=1, source_target_pairs={{0,2},{1,7},{2,0},{3,5},{4,6},{5,3},{6,4},{7,1},{8,10},{9,15},{10,... | collective-permute-start | bytes 983048 | tf_op jit(solution)/shard_map/ppermute | solution.py:493
  18.7 23.4 %collective-permute-start.2 = (bf16[4,10,8,512]{3,2,1,0:T(8,128)(2,1)S(1)}, bf16[4,10,8,512]{3,2,1,0:T(8,128)(2,1)S(1)}, u32[]{:S(2)}, u32[]{:S(2)}) collective-permute-start(bf16[4,10,8,512]{3,2,1,0:T(8,128)(2,1)S(1)} %get-tuple-element.41), channel_id=1, source_target_pairs={{0,14},{1,13},{2,12},{3,15},{4,10},{5,9},{6,8},{7,11},{8,6},{9,5},... | collective-permute-start | bytes 983048 | tf_op jit(solution)/shard_map/ppermute | solution.py:493
  33.0 10.6 %collective-permute-start.5 = (f16[72,8,128]{2,1,0:T(8,128)(2,1)S(1)}, f16[72,8,128]{2,1,0:T(8,128)(2,1)S(1)}, u32[]{:S(2)}, u32[]{:S(2)}) collective-permute-start(f16[72,8,128]{2,1,0:T(8,128)(2,1)S(1)} %convert_element_type.6), channel_id=1, source_target_pairs={{0,24},{4,28},{8,16},{12,20},{16,8},{20,12},{24,0},{28,4},{1,25},{... | collective-permute-start | bytes 442376 | tf_op jit(solution)/shard_map/ppermute | solution.py:500
  42.1 3.5 %copy-start.4 = (f32[8,64,128]{2,1,0:T(8,128)S(1)}, f32[8,64,128]{2,1,0:T(8,128)}, u32[]{:S(2)}) copy-start(f32[8,64,128]{2,1,0:T(8,128)} %land_flux.1) | copy-start | bytes 786436
  42.1 3.5 %copy-start.5 = (f32[64,128]{1,0:T(8,128)S(1)}, f32[64,128]{1,0:T(8,128)}, u32[]{:S(2)}) copy-start(f32[64,128]{1,0:T(8,128)} %kappa.3) | copy-start | bytes 98308
  42.1 3.5 %copy-start.6 = (f32[64,128]{1,0:T(8,128)S(1)}, f32[64,128]{1,0:T(8,128)}, u32[]{:S(2)}) copy-start(f32[64,128]{1,0:T(8,128)} %land_area.1) | copy-start | bytes 98308
  43.6 1.9 %collective-permute-start.6 = (f32[72,8,128]{2,1,0:T(8,128)S(1)}, f32[72,8,128]{2,1,0:T(8,128)S(1)}, u32[]{:S(2)}, u32[]{:S(2)}) collective-permute-start(f32[72,8,128]{2,1,0:T(8,128)S(1)} %shard_map.98), channel_id=1, source_target_pairs={{0,1},{1,0},{2,3},{3,2},{4,5},{5,4},{6,7},{7,6},{8,9},{9,8},{10,11... | collective-permute-start | bytes 884744 | tf_op jit(solution)/shard_map/ppermute | solution.py:515
  45.8 5.6 %collective-permute-start.8 = (f32[64,128]{1,0:T(8,128)S(1)}, f32[64,128]{1,0:T(8,128)S(1)}, u32[]{:S(2)}, u32[]{:S(2)}) collective-permute-start(f32[64,128]{1,0:T(8,128)S(1)} %get-tuple-element.57), channel_id=1, source_target_pairs={{4,8},{12,16},{20,24},{8,4},{16,12},{24,20},{5,9},{13,17},{21,25},... | collective-permute-start | bytes 98312 | tf_op jit(solution)/shard_map/ppermute | solution.py:379
  49.5 2.8 %collective-permute-start.7 = (f32[64,128]{1,0:T(8,128)S(1)}, f32[64,128]{1,0:T(8,128)S(1)}, u32[]{:S(2)}, u32[]{:S(2)}) collective-permute-start(f32[64,128]{1,0:T(8,128)S(1)} %get-tuple-element.57), channel_id=1, source_target_pairs={{0,4},{4,0},{8,12},{12,8},{16,20},{20,16},{24,28},{28,24},{1,5},{5... | collective-permute-start | bytes 98312 | tf_op jit(solution)/shard_map/ppermute | solution.py:378
  52.4 6.7 %collective-permute-start.10 = (f32[10,8,128]{2,1,0:T(8,128)S(1)}, f32[10,8,128]{2,1,0:T(8,128)S(1)}, u32[]{:S(2)}, u32[]{:S(2)}) collective-permute-start(f32[10,8,128]{2,1,0:T(8,128)S(1)} %pad_maximum_fusion), channel_id=1, source_target_pairs={{1,2},{2,1},{5,6},{6,5},{9,10},{10,9},{13,14},{14,13},{17,18},{18,... | collective-permute-start | bytes 122888 | tf_op jit(solution)/shard_map/ppermute | solution.py:379
  57.5 1.7 %collective-permute-start.9 = (f32[10,8,128]{2,1,0:T(8,128)S(1)}, f32[10,8,128]{2,1,0:T(8,128)S(1)}, u32[]{:S(2)}, u32[]{:S(2)}) collective-permute-start(f32[10,8,128]{2,1,0:T(8,128)S(1)} %pad_maximum_fusion), channel_id=1, source_target_pairs={{0,1},{1,0},{2,3},{3,2},{4,5},{5,4},{6,7},{7,6},{8,9},{9,8},{10,11... | collective-permute-start | bytes 122888 | tf_op jit(solution)/shard_map/ppermute | solution.py:378

commit v7 on v6

--- a/solution.py
+++ b/solution.py
@@ -466,7 +466,7 @@
     layer = width_x // LAYERS * width_y
     rows_here, cols_here = land_area.shape
 
-    mirror = (LAYERS - 1) * layer
+    mirror = LAYERS // 2 * layer
     pairs = (dest_device.T, dest_tile.T, cell_target, cell_weight, sea_mask, ocean_fields)
     halves = [
         [h * (device_count // 2) + i for i in range(device_count // 2)] for h in range(2)
@@ -492,7 +492,7 @@
         pairing = [(i, i ^ 2 * carried(j, i & 1)) for i in everywhere]
         return lax.ppermute(messages[j], ("gx", "gy"), pairing)
 
-    soon = [deliver(j) for j in range(0, len(messages), 2)]
+    soon = [deliver(j) for j in reversed(range(0, len(messages), 2))]
     late = [deliver(j) for j in range(1, len(messages), 2)]
 
     far_total = bin_all([far_got], [[(0, 0, half)]], [], cap, rows_here, averaged=True)[0]

time: 61.9 us -> 61.7 us (level)
  starting transfers between devices: 21.9 us -> 20.7 us
    ppermute x1, starting transfers between devices: 1.24 us -> 0.12 us  [shards(): lax.ppermute(far_total.astype(jnp.float16), 'gx', opposite).astype(F32)]
    ppermute x4, waiting for transfers between devices: 4.83 us -> 5.96 us  [deliver(): return lax.ppermute(messages[j], ('gx', 'gy'), pairing)]
    ppermute x2, starting transfers between devices: 8.72 us -> 7.71 us  [neighbours(): two = lax.ppermute(values, axis, second)]
    ppermute x2, starting transfers between devices: 0.14 us -> 1.11 us  [neighbours(): one = lax.ppermute(values, axis, first)]
  transfers between devices with their start and end apart: 12 -> 12, of which waited for: 6 -> 7; matrix products, arithmetic and copies ran while one was open for 0% -> 0% of each run, Pallas kernels for 25% -> 25%
where the time goes in v7:
time: 61.7 us; the launch traced here: 60.5 us
  starting transfers between devices  20.7 us (34%)
  Pallas kernels  20.6 us (33%)
  waiting for transfers between devices  18.8 us (30%)
    pallas_call x5, Pallas kernels, bin_all(): pl.pallas_call(functools.partial(bin_slots, cap, picked, len(arrays), ave...  11.6 us
    ppermute x2, starting transfers between devices, neighbours(): two = lax.ppermute(values, axis, second)  7.71 us
    all_to_all x1, waiting for transfers between devices, shards(): far_got = exchange(far_slots)  7.42 us
    ppermute x4, waiting for transfers between devices, deliver(): return lax.ppermute(messages[j], ('gx', 'gy'), pairing)  5.96 us
    pallas_call x2, Pallas kernels, pack(): pl.pallas_call(functools.partial(pack_kernel, cap, near, mirror), out_sha...  5.76 us
    all_to_all x1, starting transfers between devices, shards(): far_got = exchange(far_slots)  5.71 us
    ppermute x4, starting transfers between devices, deliver(): return lax.ppermute(messages[j], ('gx', 'gy'), pairing)  5.17 us
    ppermute x2, waiting for transfers between devices, neighbours(): two = lax.ppermute(values, axis, second)  2.73 us
  transfers between devices with their start and end apart: 12, of which 7 were waited for; matrix products, arithmetic and copies ran while one was open for 0% of the time, Pallas kernels for 25%

profile of v7, /device:TPU:21, one launch (start us, length us, event | category | flops | bytes accessed | tf_op | source)
XLA Modules:
  0.0 60.5 jit_solution(3040223387051028903)
XLA Ops:
  0.0 3.2 %shard_map.91 = bf16[16,10,8,512]{3,2,1,0:T(8,128)(2,1)} custom-call(s32[2,64]{1,0:T(2,128)} %bitcast.4, s32[2,64]{1,0:T(2,128)} %bitcast.5, s32[2,64]{1,0:T(2,128)} %bitcast.8, s32[64,2,512]{2,1,0:T(2,128)} %refs_3_.2, bf16[64,2,512]{2,1,0:T(2,128)(2,1)} %refs_4_.2, s32[64,512]{1,0:T(8,128)} %refs_5_.2, bf16[64,8,512]{2,1,0:T(8,128)(2,1)} %refs_6_.2), custom_call_target="tpu_custom_call" | custom-call | flops 100000000 | bytes 4000000 | tf_op jit(solution)/shard_map/pallas_call | solution.py:194
  3.2 0.0 copy-start
  3.2 0.0 copy-start.3
  3.2 0.0 copy-start.7
  3.2 5.7 %all-to-all-start = ((bf16[16,10,8,512]{3,2,1,0:T(8,128)(2,1)}), bf16[16,10,8,512]{3,2,1,0:T(8,128)(2,1)S(1)}, u32[]{:S(2)}, u32[]{:S(2)}) async-start(bf16[16,10,8,512]{3,2,1,0:T(8,128)(2,1)} %shard_map.91), calls=%async_computation | async-start | bytes 2621440 | tf_op jit(solution)/shard_map/all_to_all | solution.py:486
  9.0 2.6 %shard_map.92 = (bf16[8,10,8,512]{3,2,1,0:T(8,128)(2,1)S(1)}, bf16[8,10,8,512]{3,2,1,0:T(8,128)(2,1)S(1)}) custom-call(s32[2,64]{1,0:T(2,128)S(1)} %bitcast.6, s32[2,64]{1,0:T(2,128)S(1)} %bitcast.7, s32[2,64]{1,0:T(2,128)S(1)} %bitcast.9, s32[64,2,512]{2,1,0:T(2,128)S(1)} %copy-done.1, bf16[64,2,512]{2,1,0:T(2,128)(2,1)S(1)} %copy-done.2, ...), custom_call_target="tpu_custom_call" | custom-call | flops 100000000 | bytes 4000000 | tf_op jit(solution)/shard_map/pallas_call | solution.py:194
  11.6 0.4 collective-permute-start
  12.0 1.7 %collective-permute-done.taken = bf16[8,10,8,512]{3,2,1,0:T(8,128)(2,1)S(1)} collective-permute-done((bf16[8,10,8,512]{3,2,1,0:T(8,128)(2,1)S(1)}, bf16[8,10,8,512]{3,2,1,0:T(8,128)(2,1)S(1)}, u32[]{:S(2)}, u32[]{:S(2)}) %collective-permute-start) | collective-permute-done | bytes 655392 | tf_op jit(solution)/shard_map/ppermute | solution.py:488
  13.8 0.9 %shard_map.93 = (bf16[4,10,8,512]{3,2,1,0:T(8,128)(2,1)}, bf16[4,10,8,512]{3,2,1,0:T(8,128)(2,1)S(1)}, bf16[4,10,8,512]{3,2,1,0:T(8,128)(2,1)}, bf16[4,10,8,512]{3,2,1,0:T(8,128)(2,1)S(1)}) custom-call(bf16[8,10,8,512]{3,2,1,0:T(8,128)(2,1)S(1)} %get-tuple-element.38.kept, bf16[8,10,8,512]{3,2,1,0:T(8,128)(2,1)S(1)} %collective-permute-done.taken), custom_call_target="tpu_custom_call" | custom-call | bytes 2621440 | tf_op jit(solution)/shard_map/pallas_call | solution.py:216
  14.7 2.1 %collective-permute-start.4 = (bf16[4,10,8,512]{3,2,1,0:T(8,128)(2,1)}, bf16[4,10,8,512]{3,2,1,0:T(8,128)(2,1)S(1)}, u32[]{:S(2)}, u32[]{:S(2)}) collective-permute-start(bf16[4,10,8,512]{3,2,1,0:T(8,128)(2,1)} %get-tuple-element.43), channel_id=1, source_target_pairs={{0,8},{1,11},{2,10},{3,9},{4,12},{5,15},{6,14},{7,13},{8,0},{9,3},... | collective-permute-start | bytes 983048 | tf_op jit(solution)/shard_map/ppermute | solution.py:493
  16.8 1.6 %collective-permute-start.3 = (bf16[4,10,8,512]{3,2,1,0:T(8,128)(2,1)}, bf16[4,10,8,512]{3,2,1,0:T(8,128)(2,1)S(1)}, u32[]{:S(2)}, u32[]{:S(2)}) collective-permute-start(bf16[4,10,8,512]{3,2,1,0:T(8,128)(2,1)} %get-tuple-element.42), channel_id=1, source_target_pairs={{0,4},{1,1},{2,6},{3,3},{4,0},{5,5},{6,2},{7,7},{8,12},{9,9},{10,1... | collective-permute-start | bytes 983048 | tf_op jit(solution)/shard_map/ppermute | solution.py:493
  18.4 0.3 collective-permute-start.1
  18.7 1.2 %collective-permute-start.2 = (bf16[4,10,8,512]{3,2,1,0:T(8,128)(2,1)S(1)}, bf16[4,10,8,512]{3,2,1,0:T(8,128)(2,1)S(1)}, u32[]{:S(2)}, u32[]{:S(2)}) collective-permute-start(bf16[4,10,8,512]{3,2,1,0:T(8,128)(2,1)S(1)} %get-tuple-element.41), channel_id=1, source_target_pairs={{0,14},{1,13},{2,12},{3,15},{4,10},{5,9},{6,8},{7,11},{8,6},{9,5},... | collective-permute-start | bytes 983048 | tf_op jit(solution)/shard_map/ppermute | solution.py:493
  19.9 7.4 %all-to-all-done.refs_0_ = bf16[16,10,8,512]{3,2,1,0:T(8,128)(2,1)S(1)} async-done(((bf16[16,10,8,512]{3,2,1,0:T(8,128)(2,1)}), bf16[16,10,8,512]{3,2,1,0:T(8,128)(2,1)S(1)}, u32[]{:S(2)}, u32[]{:S(2)}) %all-to-all-start) | async-done | bytes 1310752 | tf_op jit(solution)/shard_map/all_to_all | solution.py:486
  27.3 5.6 %shard_map.94 = f32[72,8,128]{2,1,0:T(8,128)S(1)} custom-call(bf16[16,10,8,512]{3,2,1,0:T(8,128)(2,1)S(1)} %all-to-all-done.refs_0_), custom_call_target="tpu_custom_call" | custom-call | flops 1207959552 | bytes 1310720 | tf_op jit(solution)/shard_map/pallas_call | solution.py:340
  33.0 0.1 collective-permute-start.5
  33.1 0.1 collective-permute-done.4.refs_0_
  33.2 1.5 %shard_map.95 = (f32[72,8,128]{2,1,0:T(8,128)S(1)}, f32[72,8,128]{2,1,0:T(8,128)S(1)}) custom-call(bf16[4,10,8,512]{3,2,1,0:T(8,128)(2,1)S(1)} %collective-permute-done.4.refs_0_), custom_call_target="tpu_custom_call" | custom-call | tf_op jit(solution)/shard_map/pallas_call | solution.py:340
  34.7 1.5 %shard_map.96 = (f32[72,8,128]{2,1,0:T(8,128)S(1)}, f32[72,8,128]{2,1,0:T(8,128)S(1)}) custom-call(bf16[4,10,8,512]{3,2,1,0:T(8,128)(2,1)S(1)} %collective-permute-done.3.refs_0_, f32[72,8,128]{2,1,0:T(8,128)S(1)} %get-tuple-element.46.refs_1_, f32[72,8,128]{2,1,0:T(8,128)S(1)} %get-tuple-element.48.refs_2_), custom_call_target="tpu_custom_call" | custom-call | tf_op jit(solution)/shard_map/pallas_call | solution.py:340
  36.2 5.8 %collective-permute-done.1.refs_0_ = bf16[4,10,8,512]{3,2,1,0:T(8,128)(2,1)S(1)} collective-permute-done((bf16[4,10,8,512]{3,2,1,0:T(8,128)(2,1)S(1)}, bf16[4,10,8,512]{3,2,1,0:T(8,128)(2,1)S(1)}, u32[]{:S(2)}, u32[]{:S(2)}) %collective-permute-start.1) | collective-permute-done | bytes 327712 | tf_op jit(solution)/shard_map/ppermute | solution.py:493
  42.1 1.5 %shard_map.98 = f32[72,8,128]{2,1,0:T(8,128)S(1)} custom-call(bf16[4,10,8,512]{3,2,1,0:T(8,128)(2,1)S(1)} %collective-permute-done.1.refs_0_, bf16[4,10,8,512]{3,2,1,0:T(8,128)(2,1)S(1)} %collective-permute-done.2.refs_1_, f32[72,8,128]{2,1,0:T(8,128)S(1)} %get-tuple-element.53.refs_2_), custom_call_target="tpu_custom_call" | custom-call | tf_op jit(solution)/shard_map/pallas_call | solution.py:340
  43.6 0.4 collective-permute-start.6
  44.1 1.5 %shard_map.97.total = f32[72,8,128]{2,1,0:T(8,128)S(1)} custom-call(bf16[4,10,8,512]{3,2,1,0:T(8,128)(2,1)S(1)} %collective-permute-done.1.refs_0_, bf16[4,10,8,512]{3,2,1,0:T(8,128)(2,1)S(1)} %collective-permute-done.2.refs_1_, f32[72,8,128]{2,1,0:T(8,128)S(1)} %get-tuple-element.52.refs_2_), custom_call_target="tpu_custom_call" | custom-call | tf_op jit(solution)/shard_map/pallas_call | solution.py:340
  45.6 0.2 shard_map.99
  45.8 3.4 %collective-permute-start.8 = (f32[64,128]{1,0:T(8,128)S(1)}, f32[64,128]{1,0:T(8,128)S(1)}, u32[]{:S(2)}, u32[]{:S(2)}) collective-permute-start(f32[64,128]{1,0:T(8,128)S(1)} %get-tuple-element.57), channel_id=1, source_target_pairs={{4,8},{12,16},{20,24},{8,4},{16,12},{24,20},{5,9},{13,17},{21,25},... | collective-permute-start | bytes 98312 | tf_op jit(solution)/shard_map/ppermute | solution.py:379
  49.2 1.0 %collective-permute-start.7 = (f32[64,128]{1,0:T(8,128)S(1)}, f32[64,128]{1,0:T(8,128)S(1)}, u32[]{:S(2)}, u32[]{:S(2)}) collective-permute-start(f32[64,128]{1,0:T(8,128)S(1)} %get-tuple-element.57), channel_id=1, source_target_pairs={{0,4},{4,0},{8,12},{12,8},{16,20},{20,16},{24,28},{28,24},{1,5},{5... | collective-permute-start | bytes 98312 | tf_op jit(solution)/shard_map/ppermute | solution.py:378
  50.2 1.1 %collective-permute-done.8 = f32[64,128]{1,0:T(8,128)S(1)} collective-permute-done((f32[64,128]{1,0:T(8,128)S(1)}, f32[64,128]{1,0:T(8,128)S(1)}, u32[]{:S(2)}, u32[]{:S(2)}) %collective-permute-start.8) | collective-permute-done | bytes 32800 | tf_op jit(solution)/shard_map/ppermute | solution.py:379
  51.4 1.0 %collective-permute-done.7 = f32[64,128]{1,0:T(8,128)S(1)} collective-permute-done((f32[64,128]{1,0:T(8,128)S(1)}, f32[64,128]{1,0:T(8,128)S(1)}, u32[]{:S(2)}, u32[]{:S(2)}) %collective-permute-start.7) | collective-permute-done | bytes 32800 | tf_op jit(solution)/shard_map/ppermute | solution.py:378
  52.4 4.3 %collective-permute-start.10 = (f32[10,8,128]{2,1,0:T(8,128)S(1)}, f32[10,8,128]{2,1,0:T(8,128)S(1)}, u32[]{:S(2)}, u32[]{:S(2)}) collective-permute-start(f32[10,8,128]{2,1,0:T(8,128)S(1)} %pad_maximum_fusion), channel_id=1, source_target_pairs={{1,2},{2,1},{5,6},{6,5},{9,10},{10,9},{13,14},{14,13},{17,18},{18,... | collective-permute-start | bytes 122888 | tf_op jit(solution)/shard_map/ppermute | solution.py:379
  56.8 0.1 collective-permute-start.9
  56.9 1.6 %collective-permute-done.10 = f32[10,8,128]{2,1,0:T(8,128)S(1)} collective-permute-done((f32[10,8,128]{2,1,0:T(8,128)S(1)}, f32[10,8,128]{2,1,0:T(8,128)S(1)}, u32[]{:S(2)}, u32[]{:S(2)}) %collective-permute-start.10) | collective-permute-done | bytes 40992 | tf_op jit(solution)/shard_map/ppermute | solution.py:379
  58.4 2.0 %shard_map.100 = f32[8,64,128]{2,1,0:T(8,128)} custom-call(f32[8,64,128]{2,1,0:T(8,128)S(1)} %get-tuple-element.56.merged, f32[64,128]{1,0:T(8,128)S(1)} %get-tuple-element.61.before, f32[64,128]{1,0:T(8,128)S(1)} %get-tuple-element.60.after, f32[10,8,128]{2,1,0:T(8,128)S(1)} %get-tuple-element.63.above, f32[10,8,128]{2,1,0:T(8,128)S(1)} %get-tuple-element.62.below, ...), custom_call_target="tpu_custom_call" | custom-call | tf_op jit(solution)/shard_map/pallas_call | solution.py:522
  (29 shorter events, 0.2 us)
Async XLA Ops:
  3.2 5.8 %copy-start = (bf16[64,8,512]{2,1,0:T(8,128)(2,1)S(1)}, bf16[64,8,512]{2,1,0:T(8,128)(2,1)}, u32[]{:S(2)}) copy-start(bf16[64,8,512]{2,1,0:T(8,128)(2,1)} %refs_6_.2) | copy-start | bytes 1572868
  3.2 5.8 %copy-start.1 = (s32[64,2,512]{2,1,0:T(2,128)S(1)}, s32[64,2,512]{2,1,0:T(2,128)}, u32[]{:S(2)}) copy-start(s32[64,2,512]{2,1,0:T(2,128)} %refs_3_.2) | copy-start | bytes 786436
  3.2 5.8 %copy-start.2 = (bf16[64,2,512]{2,1,0:T(2,128)(2,1)S(1)}, bf16[64,2,512]{2,1,0:T(2,128)(2,1)}, u32[]{:S(2)}) copy-start(bf16[64,2,512]{2,1,0:T(2,128)(2,1)} %refs_4_.2) | copy-start | bytes 393220
  3.2 5.8 %copy-start.3 = (s32[64,512]{1,0:T(8,128)S(1)}, s32[64,512]{1,0:T(8,128)}, u32[]{:S(2)}) copy-start(s32[64,512]{1,0:T(8,128)} %refs_5_.2) | copy-start | bytes 393220
  3.2 5.8 %copy-start.7 = (s32[64,2]{0,1:T(2,128)S(1)}, s32[64,2]{0,1:T(2,128)}, u32[]{:S(2)}) copy-start(s32[64,2]{0,1:T(2,128)} %param.10) | copy-start | bytes 1540
  3.2 5.8 %copy-start.8 = (s32[64,2]{0,1:T(2,128)S(1)}, s32[64,2]{0,1:T(2,128)}, u32[]{:S(2)}) copy-start(s32[64,2]{0,1:T(2,128)} %param.11) | copy-start | bytes 1540
  3.2 24.1 %all-to-all-start = ((bf16[16,10,8,512]{3,2,1,0:T(8,128)(2,1)}), bf16[16,10,8,512]{3,2,1,0:T(8,128)(2,1)S(1)}, u32[]{:S(2)}, u32[]{:S(2)}) async-start(bf16[16,10,8,512]{3,2,1,0:T(8,128)(2,1)} %shard_map.91), calls=%async_computation | async-start | bytes 2621440 | tf_op jit(solution)/shard_map/all_to_all | solution.py:486
  11.6 2.2 %collective-permute-start = (bf16[8,10,8,512]{3,2,1,0:T(8,128)(2,1)S(1)}, bf16[8,10,8,512]{3,2,1,0:T(8,128)(2,1)S(1)}, u32[]{:S(2)}, u32[]{:S(2)}) collective-permute-start(bf16[8,10,8,512]{3,2,1,0:T(8,128)(2,1)S(1)} %get-tuple-element.39), channel_id=1, source_target_pairs={{0,1},{1,0},{2,3},{3,2},{4,5},{5,4},{6,7},{7,6},{8,9},{9,8},{10,11... | collective-permute-start | bytes 1966088 | tf_op jit(solution)/shard_map/ppermute | solution.py:488
  14.7 18.5 %collective-permute-start.4 = (bf16[4,10,8,512]{3,2,1,0:T(8,128)(2,1)}, bf16[4,10,8,512]{3,2,1,0:T(8,128)(2,1)S(1)}, u32[]{:S(2)}, u32[]{:S(2)}) collective-permute-start(bf16[4,10,8,512]{3,2,1,0:T(8,128)(2,1)} %get-tuple-element.43), channel_id=1, source_target_pairs={{0,8},{1,11},{2,10},{3,9},{4,12},{5,15},{6,14},{7,13},{8,0},{9,3},... | collective-permute-start | bytes 983048 | tf_op jit(solution)/shard_map/ppermute | solution.py:493
  16.8 17.9 %collective-permute-start.3 = (bf16[4,10,8,512]{3,2,1,0:T(8,128)(2,1)}, bf16[4,10,8,512]{3,2,1,0:T(8,128)(2,1)S(1)}, u32[]{:S(2)}, u32[]{:S(2)}) collective-permute-start(bf16[4,10,8,512]{3,2,1,0:T(8,128)(2,1)} %get-tuple-element.42), channel_id=1, source_target_pairs={{0,4},{1,1},{2,6},{3,3},{4,0},{5,5},{6,2},{7,7},{8,12},{9,9},{10,1... | collective-permute-start | bytes 983048 | tf_op jit(solution)/shard_map/ppermute | solution.py:493
  18.4 23.6 %collective-permute-start.1 = (bf16[4,10,8,512]{3,2,1,0:T(8,128)(2,1)S(1)}, bf16[4,10,8,512]{3,2,1,0:T(8,128)(2,1)S(1)}, u32[]{:S(2)}, u32[]{:S(2)}) collective-permute-start(bf16[4,10,8,512]{3,2,1,0:T(8,128)(2,1)S(1)} %get-tuple-element.40), channel_id=1, source_target_pairs={{0,2},{1,7},{2,0},{3,5},{4,6},{5,3},{6,4},{7,1},{8,10},{9,15},{10,... | collective-permute-start | bytes 983048 | tf_op jit(solution)/shard_map/ppermute | solution.py:493
  18.7 23.4 %collective-permute-start.2 = (bf16[4,10,8,512]{3,2,1,0:T(8,128)(2,1)S(1)}, bf16[4,10,8,512]{3,2,1,0:T(8,128)(2,1)S(1)}, u32[]{:S(2)}, u32[]{:S(2)}) collective-permute-start(bf16[4,10,8,512]{3,2,1,0:T(8,128)(2,1)S(1)} %get-tuple-element.41), channel_id=1, source_target_pairs={{0,14},{1,13},{2,12},{3,15},{4,10},{5,9},{6,8},{7,11},{8,6},{9,5},... | collective-permute-start | bytes 983048 | tf_op jit(solution)/shard_map/ppermute | solution.py:493
  33.0 10.6 %collective-permute-start.5 = (f16[72,8,128]{2,1,0:T(8,128)(2,1)S(1)}, f16[72,8,128]{2,1,0:T(8,128)(2,1)S(1)}, u32[]{:S(2)}, u32[]{:S(2)}) collective-permute-start(f16[72,8,128]{2,1,0:T(8,128)(2,1)S(1)} %convert_element_type.6), channel_id=1, source_target_pairs={{0,16},{4,20},{8,24},{12,28},{16,0},{20,4},{24,8},{28,12},{1,17},{... | collective-permute-start | bytes 442376 | tf_op jit(solution)/shard_map/ppermute | solution.py:500
  42.1 3.5 %copy-start.4 = (f32[8,64,128]{2,1,0:T(8,128)S(1)}, f32[8,64,128]{2,1,0:T(8,128)}, u32[]{:S(2)}) copy-start(f32[8,64,128]{2,1,0:T(8,128)} %land_flux.1) | copy-start | bytes 786436
  42.1 3.5 %copy-start.5 = (f32[64,128]{1,0:T(8,128)S(1)}, f32[64,128]{1,0:T(8,128)}, u32[]{:S(2)}) copy-start(f32[64,128]{1,0:T(8,128)} %kappa.3) | copy-start | bytes 98308
  42.1 3.5 %copy-start.6 = (f32[64,128]{1,0:T(8,128)S(1)}, f32[64,128]{1,0:T(8,128)}, u32[]{:S(2)}) copy-start(f32[64,128]{1,0:T(8,128)} %land_area.1) | copy-start | bytes 98308
  43.6 1.9 %collective-permute-start.6 = (f32[72,8,128]{2,1,0:T(8,128)S(1)}, f32[72,8,128]{2,1,0:T(8,128)S(1)}, u32[]{:S(2)}, u32[]{:S(2)}) collective-permute-start(f32[72,8,128]{2,1,0:T(8,128)S(1)} %shard_map.98), channel_id=1, source_target_pairs={{0,1},{1,0},{2,3},{3,2},{4,5},{5,4},{6,7},{7,6},{8,9},{9,8},{10,11... | collective-permute-start | bytes 884744 | tf_op jit(solution)/shard_map/ppermute | solution.py:515
  45.8 5.6 %collective-permute-start.8 = (f32[64,128]{1,0:T(8,128)S(1)}, f32[64,128]{1,0:T(8,128)S(1)}, u32[]{:S(2)}, u32[]{:S(2)}) collective-permute-start(f32[64,128]{1,0:T(8,128)S(1)} %get-tuple-element.57), channel_id=1, source_target_pairs={{4,8},{12,16},{20,24},{8,4},{16,12},{24,20},{5,9},{13,17},{21,25},... | collective-permute-start | bytes 98312 | tf_op jit(solution)/shard_map/ppermute | solution.py:379
  49.2 3.1 %collective-permute-start.7 = (f32[64,128]{1,0:T(8,128)S(1)}, f32[64,128]{1,0:T(8,128)S(1)}, u32[]{:S(2)}, u32[]{:S(2)}) collective-permute-start(f32[64,128]{1,0:T(8,128)S(1)} %get-tuple-element.57), channel_id=1, source_target_pairs={{0,4},{4,0},{8,12},{12,8},{16,20},{20,16},{24,28},{28,24},{1,5},{5... | collective-permute-start | bytes 98312 | tf_op jit(solution)/shard_map/ppermute | solution.py:378
  52.4 6.0 %collective-permute-start.10 = (f32[10,8,128]{2,1,0:T(8,128)S(1)}, f32[10,8,128]{2,1,0:T(8,128)S(1)}, u32[]{:S(2)}, u32[]{:S(2)}) collective-permute-start(f32[10,8,128]{2,1,0:T(8,128)S(1)} %pad_maximum_fusion), channel_id=1, source_target_pairs={{1,2},{2,1},{5,6},{6,5},{9,10},{10,9},{13,14},{14,13},{17,18},{18,... | collective-permute-start | bytes 122888 | tf_op jit(solution)/shard_map/ppermute | solution.py:379
  56.8 1.7 %collective-permute-start.9 = (f32[10,8,128]{2,1,0:T(8,128)S(1)}, f32[10,8,128]{2,1,0:T(8,128)S(1)}, u32[]{:S(2)}, u32[]{:S(2)}) collective-permute-start(f32[10,8,128]{2,1,0:T(8,128)S(1)} %pad_maximum_fusion), channel_id=1, source_target_pairs={{0,1},{1,0},{2,3},{3,2},{4,5},{5,4},{6,7},{7,6},{8,9},{9,8},{10,11... | collective-permute-start | bytes 122888 | tf_op jit(solution)/shard_map/ppermute | solution.py:378

commit v8 on v7

--- a/solution.py
+++ b/solution.py
@@ -490,7 +490,10 @@
 
     def deliver(j):
         pairing = [(i, i ^ 2 * carried(j, i & 1)) for i in everywhere]
-        return lax.ppermute(messages[j], ("gx", "gy"), pairing)
+        if all(a != b for a, b in pairing):
+            return lax.ppermute(messages[j], ("gx", "gy"), pairing)
+        arrived = lax.ppermute(messages[j], ("gx", "gy"), [(a, b) for a, b in pairing if a != b])
+        return jnp.where(lax.axis_index("gy") % 2 == 1, messages[j], arrived)
 
     soon = [deliver(j) for j in reversed(range(0, len(messages), 2))]
     late = [deliver(j) for j in range(1, len(messages), 2)]
@@ -509,8 +512,9 @@
         totals = sums([message], 0, 1, earlier=totals)
         far_total = totals[0]
     own, other = totals
-    late, own = lax.optimization_barrier((late, own))
-    other = sums(late, 1, earlier=[other])[0]
+    for i, message in enumerate(late):
+        late[i], other = lax.optimization_barrier((message, other))
+        other = sums([late[i]], 1, earlier=[other])[0]
     other, passed = lax.optimization_barrier((other, passed))
     other = lax.ppermute(other, ("gx", "gy"), [(i, i ^ 1) for i in everywhere])
     own = sums(late, 0, earlier=[own])[0]

time: 61.7 us -> 61.9 us (level)
    ppermute x4 -> x3, starting transfers between devices: 5.17 us -> 3.55 us  [deliver(): return lax.ppermute(messages[j], ('gx', 'gy'), pairing)]
    ppermute x0 -> x1, starting transfers between devices: none -> 1.4 us  [deliver(): lax.ppermute(messages[j], ('gx', 'gy'), [(a, b) for a, b in pairing if a...]
    ppermute x2, starting transfers between devices: 7.71 us -> 6.86 us  [neighbours(): two = lax.ppermute(values, axis, second)]
    ppermute x2, starting transfers between devices: 1.11 us -> 1.78 us  [neighbours(): one = lax.ppermute(values, axis, first)]
    pallas_call x5 -> x6, Pallas kernels: 11.6 us -> 11.8 us  [bin_all(): pl.pallas_call(functools.partial(bin_slots, cap, picked, len(arrays), ave...]
    ppermute x4 -> x3, waiting for transfers between devices: 5.96 us -> 5.91 us  [deliver(): return lax.ppermute(messages[j], ('gx', 'gy'), pairing)]
  transfers between devices with their start and end apart: 12 -> 12, of which waited for: 7 -> 6; matrix products, arithmetic and copies ran while one was open for 0% -> 0% of each run, Pallas kernels for 25% -> 25%
where the time goes in v8:
time: 61.9 us; the launch traced here: 60.8 us
  Pallas kernels  20.6 us (33%)
  starting transfers between devices  20.3 us (33%)
  waiting for transfers between devices  19.4 us (31%)
    pallas_call x6, Pallas kernels, bin_all(): pl.pallas_call(functools.partial(bin_slots, cap, picked, len(arrays), ave...  11.8 us
    all_to_all x1, waiting for transfers between devices, shards(): far_got = exchange(far_slots)  7.78 us
    ppermute x2, starting transfers between devices, neighbours(): two = lax.ppermute(values, axis, second)  6.86 us
    ppermute x3, waiting for transfers between devices, deliver(): return lax.ppermute(messages[j], ('gx', 'gy'), pairing)  5.91 us
    pallas_call x2, Pallas kernels, pack(): pl.pallas_call(functools.partial(pack_kernel, cap, near, mirror), out_sha...  5.76 us
    all_to_all x1, starting transfers between devices, shards(): far_got = exchange(far_slots)  5.71 us
    ppermute x3, starting transfers between devices, deliver(): return lax.ppermute(messages[j], ('gx', 'gy'), pairing)  3.55 us
    ppermute x2, waiting for transfers between devices, neighbours(): two = lax.ppermute(values, axis, second)  3.06 us
  transfers between devices with their start and end apart: 12, of which 6 were waited for; matrix products, arithmetic and copies ran while one was open for 0% of the time, Pallas kernels for 25%

profile of v8, /device:TPU:21, one launch (start us, length us, event | category | flops | bytes accessed | tf_op | source)
XLA Modules:
  0.0 60.8 jit_solution(2689618210840293092)
XLA Ops:
  0.0 3.2 %shard_map.91 = bf16[16,10,8,512]{3,2,1,0:T(8,128)(2,1)} custom-call(s32[2,64]{1,0:T(2,128)} %bitcast.4, s32[2,64]{1,0:T(2,128)} %bitcast.5, s32[2,64]{1,0:T(2,128)} %bitcast.8, s32[64,2,512]{2,1,0:T(2,128)} %refs_3_.2, bf16[64,2,512]{2,1,0:T(2,128)(2,1)} %refs_4_.2, s32[64,512]{1,0:T(8,128)} %refs_5_.2, bf16[64,8,512]{2,1,0:T(8,128)(2,1)} %refs_6_.2), custom_call_target="tpu_custom_call" | custom-call | flops 100000000 | bytes 4000000 | tf_op jit(solution)/shard_map/pallas_call | solution.py:194
  3.2 0.0 copy-start
  3.2 0.0 copy-start.3
  3.2 5.7 %all-to-all-start = ((bf16[16,10,8,512]{3,2,1,0:T(8,128)(2,1)}), bf16[16,10,8,512]{3,2,1,0:T(8,128)(2,1)S(1)}, u32[]{:S(2)}, u32[]{:S(2)}) async-start(bf16[16,10,8,512]{3,2,1,0:T(8,128)(2,1)} %shard_map.91), calls=%async_computation | async-start | bytes 2621440 | tf_op jit(solution)/shard_map/all_to_all | solution.py:486
  9.0 2.6 %shard_map.92 = (bf16[8,10,8,512]{3,2,1,0:T(8,128)(2,1)S(1)}, bf16[8,10,8,512]{3,2,1,0:T(8,128)(2,1)S(1)}) custom-call(s32[2,64]{1,0:T(2,128)S(1)} %bitcast.6, s32[2,64]{1,0:T(2,128)S(1)} %bitcast.7, s32[2,64]{1,0:T(2,128)S(1)} %bitcast.9, s32[64,2,512]{2,1,0:T(2,128)S(1)} %copy-done.1, bf16[64,2,512]{2,1,0:T(2,128)(2,1)S(1)} %copy-done.2, ...), custom_call_target="tpu_custom_call" | custom-call | flops 100000000 | bytes 4000000 | tf_op jit(solution)/shard_map/pallas_call | solution.py:194
  11.6 0.4 collective-permute-start
  12.0 1.7 %collective-permute-done.taken = bf16[8,10,8,512]{3,2,1,0:T(8,128)(2,1)S(1)} collective-permute-done((bf16[8,10,8,512]{3,2,1,0:T(8,128)(2,1)S(1)}, bf16[8,10,8,512]{3,2,1,0:T(8,128)(2,1)S(1)}, u32[]{:S(2)}, u32[]{:S(2)}) %collective-permute-start) | collective-permute-done | bytes 655392 | tf_op jit(solution)/shard_map/ppermute | solution.py:488
  13.8 0.8 %shard_map.93 = (bf16[4,10,8,512]{3,2,1,0:T(8,128)(2,1)S(1)}, bf16[4,10,8,512]{3,2,1,0:T(8,128)(2,1)S(1)}, bf16[4,10,8,512]{3,2,1,0:T(8,128)(2,1)}, bf16[4,10,8,512]{3,2,1,0:T(8,128)(2,1)S(1)}) custom-call(bf16[8,10,8,512]{3,2,1,0:T(8,128)(2,1)S(1)} %get-tuple-element.39.kept, bf16[8,10,8,512]{3,2,1,0:T(8,128)(2,1)S(1)} %collective-permute-done.taken), custom_call_target="tpu_custom_call" | custom-call | bytes 2621440 | tf_op jit(solution)/shard_map/pallas_call | solution.py:216
  14.6 1.4 %collective-permute-start.2 = (bf16[4,10,8,512]{3,2,1,0:T(8,128)(2,1)S(1)}, bf16[4,10,8,512]{3,2,1,0:T(8,128)(2,1)}, u32[]{:S(2)}, u32[]{:S(2)}) collective-permute-start(bf16[4,10,8,512]{3,2,1,0:T(8,128)(2,1)S(1)} %get-tuple-element.42), channel_id=1, source_target_pairs={{0,4},{2,6},{4,0},{6,2},{8,12},{10,14},{12,8},{14,10},{16,20},{18,... | collective-permute-start | bytes 983048 | tf_op jit(solution)/shard_map/ppermute | solution.py:495
  16.0 1.2 %collective-permute-start.1 = (bf16[4,10,8,512]{3,2,1,0:T(8,128)(2,1)S(1)}, bf16[4,10,8,512]{3,2,1,0:T(8,128)(2,1)S(1)}, u32[]{:S(2)}, u32[]{:S(2)}) collective-permute-start(bf16[4,10,8,512]{3,2,1,0:T(8,128)(2,1)S(1)} %get-tuple-element.41), channel_id=1, source_target_pairs={{0,2},{1,7},{2,0},{3,5},{4,6},{5,3},{6,4},{7,1},{8,10},{9,15},{10,... | collective-permute-start | bytes 983048 | tf_op jit(solution)/shard_map/ppermute | solution.py:494
  17.2 1.2 %collective-permute-start.3 = (bf16[4,10,8,512]{3,2,1,0:T(8,128)(2,1)}, bf16[4,10,8,512]{3,2,1,0:T(8,128)(2,1)S(1)}, u32[]{:S(2)}, u32[]{:S(2)}) collective-permute-start(bf16[4,10,8,512]{3,2,1,0:T(8,128)(2,1)} %get-tuple-element.43), channel_id=1, source_target_pairs={{0,8},{1,11},{2,10},{3,9},{4,12},{5,15},{6,14},{7,13},{8,0},{9,3},... | collective-permute-start | bytes 983048 | tf_op jit(solution)/shard_map/ppermute | solution.py:494
  18.4 1.2 %collective-permute-start.4 = (bf16[4,10,8,512]{3,2,1,0:T(8,128)(2,1)S(1)}, bf16[4,10,8,512]{3,2,1,0:T(8,128)(2,1)S(1)}, u32[]{:S(2)}, u32[]{:S(2)}) collective-permute-start(bf16[4,10,8,512]{3,2,1,0:T(8,128)(2,1)S(1)} %get-tuple-element.51), channel_id=1, source_target_pairs={{0,14},{1,13},{2,12},{3,15},{4,10},{5,9},{6,8},{7,11},{8,6},{9,5},... | collective-permute-start | bytes 983048 | tf_op jit(solution)/shard_map/ppermute | solution.py:494
  19.5 7.8 %all-to-all-done.refs_0_ = bf16[16,10,8,512]{3,2,1,0:T(8,128)(2,1)S(1)} async-done(((bf16[16,10,8,512]{3,2,1,0:T(8,128)(2,1)}), bf16[16,10,8,512]{3,2,1,0:T(8,128)(2,1)S(1)}, u32[]{:S(2)}, u32[]{:S(2)}) %all-to-all-start) | async-done | bytes 1310752 | tf_op jit(solution)/shard_map/all_to_all | solution.py:486
  27.3 5.6 %shard_map.94 = f32[72,8,128]{2,1,0:T(8,128)S(1)} custom-call(bf16[16,10,8,512]{3,2,1,0:T(8,128)(2,1)S(1)} %all-to-all-done.refs_0_), custom_call_target="tpu_custom_call" | custom-call | flops 1207959552 | bytes 1310720 | tf_op jit(solution)/shard_map/pallas_call | solution.py:340
  33.0 0.1 collective-permute-start.5
  33.2 0.0 collective-permute-done.3.refs_0_
  33.2 1.5 %shard_map.95 = (f32[72,8,128]{2,1,0:T(8,128)S(1)}, f32[72,8,128]{2,1,0:T(8,128)S(1)}) custom-call(bf16[4,10,8,512]{3,2,1,0:T(8,128)(2,1)S(1)} %collective-permute-done.3.refs_0_), custom_call_target="tpu_custom_call" | custom-call | tf_op jit(solution)/shard_map/pallas_call | solution.py:340
  34.7 1.5 %shard_map.96 = (f32[72,8,128]{2,1,0:T(8,128)S(1)}, f32[72,8,128]{2,1,0:T(8,128)S(1)}) custom-call(bf16[4,10,8,512]{3,2,1,0:T(8,128)(2,1)S(1)} %broadcast_select_fusion.refs_0_, f32[72,8,128]{2,1,0:T(8,128)S(1)} %get-tuple-element.46.refs_1_, f32[72,8,128]{2,1,0:T(8,128)S(1)} %get-tuple-element.48.refs_2_), custom_call_target="tpu_custom_call" | custom-call | tf_op jit(solution)/shard_map/pallas_call | solution.py:340
  36.2 5.9 %collective-permute-done.1.refs_0_ = bf16[4,10,8,512]{3,2,1,0:T(8,128)(2,1)S(1)} collective-permute-done((bf16[4,10,8,512]{3,2,1,0:T(8,128)(2,1)S(1)}, bf16[4,10,8,512]{3,2,1,0:T(8,128)(2,1)S(1)}, u32[]{:S(2)}, u32[]{:S(2)}) %collective-permute-start.1) | collective-permute-done | bytes 327712 | tf_op jit(solution)/shard_map/ppermute | solution.py:494
  42.1 0.8 %shard_map.97.refs_1_ = f32[72,8,128]{2,1,0:T(8,128)S(1)} custom-call(bf16[4,10,8,512]{3,2,1,0:T(8,128)(2,1)S(1)} %collective-permute-done.1.refs_0_, f32[72,8,128]{2,1,0:T(8,128)S(1)} %get-tuple-element.52.refs_1_), custom_call_target="tpu_custom_call" | custom-call | tf_op jit(solution)/shard_map/pallas_call | solution.py:340
  43.0 0.8 %shard_map.99 = f32[72,8,128]{2,1,0:T(8,128)S(1)} custom-call(bf16[4,10,8,512]{3,2,1,0:T(8,128)(2,1)S(1)} %collective-permute-done.4.refs_1_.refs_0_, f32[72,8,128]{2,1,0:T(8,128)S(1)} %shard_map.97.refs_1_), custom_call_target="tpu_custom_call" | custom-call | tf_op jit(solution)/shard_map/pallas_call | solution.py:340
  43.8 0.4 collective-permute-start.6
  44.3 1.5 %shard_map.98.total = f32[72,8,128]{2,1,0:T(8,128)S(1)} custom-call(bf16[4,10,8,512]{3,2,1,0:T(8,128)(2,1)S(1)} %collective-permute-done.1.refs_0_, bf16[4,10,8,512]{3,2,1,0:T(8,128)(2,1)S(1)} %collective-permute-done.4.refs_1_.refs_0_, f32[72,8,128]{2,1,0:T(8,128)S(1)} %get-tuple-element.54.refs_2_), custom_call_target="tpu_custom_call" | custom-call | tf_op jit(solution)/shard_map/pallas_call | solution.py:340
  45.8 0.2 shard_map.100
  46.0 2.5 %collective-permute-start.8 = (f32[64,128]{1,0:T(8,128)S(1)}, f32[64,128]{1,0:T(8,128)S(1)}, u32[]{:S(2)}, u32[]{:S(2)}) collective-permute-start(f32[64,128]{1,0:T(8,128)S(1)} %get-tuple-element.59), channel_id=1, source_target_pairs={{4,8},{12,16},{20,24},{8,4},{16,12},{24,20},{5,9},{13,17},{21,25},... | collective-permute-start | bytes 98312 | tf_op jit(solution)/shard_map/ppermute | solution.py:379
  48.5 1.7 %collective-permute-start.7 = (f32[64,128]{1,0:T(8,128)S(1)}, f32[64,128]{1,0:T(8,128)S(1)}, u32[]{:S(2)}, u32[]{:S(2)}) collective-permute-start(f32[64,128]{1,0:T(8,128)S(1)} %get-tuple-element.59), channel_id=1, source_target_pairs={{0,4},{4,0},{8,12},{12,8},{16,20},{20,16},{24,28},{28,24},{1,5},{5... | collective-permute-start | bytes 98312 | tf_op jit(solution)/shard_map/ppermute | solution.py:378
  50.2 1.5 %collective-permute-done.8 = f32[64,128]{1,0:T(8,128)S(1)} collective-permute-done((f32[64,128]{1,0:T(8,128)S(1)}, f32[64,128]{1,0:T(8,128)S(1)}, u32[]{:S(2)}, u32[]{:S(2)}) %collective-permute-start.8) | collective-permute-done | bytes 32800 | tf_op jit(solution)/shard_map/ppermute | solution.py:379
  51.7 0.9 %collective-permute-done.7 = f32[64,128]{1,0:T(8,128)S(1)} collective-permute-done((f32[64,128]{1,0:T(8,128)S(1)}, f32[64,128]{1,0:T(8,128)S(1)}, u32[]{:S(2)}, u32[]{:S(2)}) %collective-permute-start.7) | collective-permute-done | bytes 32800 | tf_op jit(solution)/shard_map/ppermute | solution.py:378
  52.7 4.4 %collective-permute-start.10 = (f32[10,8,128]{2,1,0:T(8,128)S(1)}, f32[10,8,128]{2,1,0:T(8,128)S(1)}, u32[]{:S(2)}, u32[]{:S(2)}) collective-permute-start(f32[10,8,128]{2,1,0:T(8,128)S(1)} %pad_maximum_fusion), channel_id=1, source_target_pairs={{1,2},{2,1},{5,6},{6,5},{9,10},{10,9},{13,14},{14,13},{17,18},{18,... | collective-permute-start | bytes 122888 | tf_op jit(solution)/shard_map/ppermute | solution.py:379
  57.1 0.1 collective-permute-start.9
  57.2 1.6 %collective-permute-done.10 = f32[10,8,128]{2,1,0:T(8,128)S(1)} collective-permute-done((f32[10,8,128]{2,1,0:T(8,128)S(1)}, f32[10,8,128]{2,1,0:T(8,128)S(1)}, u32[]{:S(2)}, u32[]{:S(2)}) %collective-permute-start.10) | collective-permute-done | bytes 40992 | tf_op jit(solution)/shard_map/ppermute | solution.py:379
  58.8 2.0 %shard_map.101 = f32[8,64,128]{2,1,0:T(8,128)} custom-call(f32[8,64,128]{2,1,0:T(8,128)S(1)} %get-tuple-element.58.merged, f32[64,128]{1,0:T(8,128)S(1)} %get-tuple-element.63.before, f32[64,128]{1,0:T(8,128)S(1)} %get-tuple-element.62.after, f32[10,8,128]{2,1,0:T(8,128)S(1)} %get-tuple-element.65.above, f32[10,8,128]{2,1,0:T(8,128)S(1)} %get-tuple-element.64.below, ...), custom_call_target="tpu_custom_call" | custom-call | tf_op jit(solution)/shard_map/pallas_call | solution.py:526
  (31 shorter events, 0.2 us)
Async XLA Ops:
  3.2 5.8 %copy-start = (bf16[64,8,512]{2,1,0:T(8,128)(2,1)S(1)}, bf16[64,8,512]{2,1,0:T(8,128)(2,1)}, u32[]{:S(2)}) copy-start(bf16[64,8,512]{2,1,0:T(8,128)(2,1)} %refs_6_.2) | copy-start | bytes 1572868
  3.2 5.8 %copy-start.1 = (s32[64,2,512]{2,1,0:T(2,128)S(1)}, s32[64,2,512]{2,1,0:T(2,128)}, u32[]{:S(2)}) copy-start(s32[64,2,512]{2,1,0:T(2,128)} %refs_3_.2) | copy-start | bytes 786436
  3.2 5.8 %copy-start.2 = (bf16[64,2,512]{2,1,0:T(2,128)(2,1)S(1)}, bf16[64,2,512]{2,1,0:T(2,128)(2,1)}, u32[]{:S(2)}) copy-start(bf16[64,2,512]{2,1,0:T(2,128)(2,1)} %refs_4_.2) | copy-start | bytes 393220
  3.2 5.8 %copy-start.3 = (s32[64,512]{1,0:T(8,128)S(1)}, s32[64,512]{1,0:T(8,128)}, u32[]{:S(2)}) copy-start(s32[64,512]{1,0:T(8,128)} %refs_5_.2) | copy-start | bytes 393220
  3.2 5.8 %copy-start.7 = (s32[64,2]{0,1:T(2,128)S(1)}, s32[64,2]{0,1:T(2,128)}, u32[]{:S(2)}) copy-start(s32[64,2]{0,1:T(2,128)} %param.10) | copy-start | bytes 1540
  3.2 5.8 %copy-start.8 = (s32[64,2]{0,1:T(2,128)S(1)}, s32[64,2]{0,1:T(2,128)}, u32[]{:S(2)}) copy-start(s32[64,2]{0,1:T(2,128)} %param.11) | copy-start | bytes 1540
  3.2 24.1 %all-to-all-start = ((bf16[16,10,8,512]{3,2,1,0:T(8,128)(2,1)}), bf16[16,10,8,512]{3,2,1,0:T(8,128)(2,1)S(1)}, u32[]{:S(2)}, u32[]{:S(2)}) async-start(bf16[16,10,8,512]{3,2,1,0:T(8,128)(2,1)} %shard_map.91), calls=%async_computation | async-start | bytes 2621440 | tf_op jit(solution)/shard_map/all_to_all | solution.py:486
  11.6 2.2 %collective-permute-start = (bf16[8,10,8,512]{3,2,1,0:T(8,128)(2,1)S(1)}, bf16[8,10,8,512]{3,2,1,0:T(8,128)(2,1)S(1)}, u32[]{:S(2)}, u32[]{:S(2)}) collective-permute-start(bf16[8,10,8,512]{3,2,1,0:T(8,128)(2,1)S(1)} %get-tuple-element.40), channel_id=1, source_target_pairs={{0,1},{1,0},{2,3},{3,2},{4,5},{5,4},{6,7},{7,6},{8,9},{9,8},{10,11... | collective-permute-start | bytes 1966088 | tf_op jit(solution)/shard_map/ppermute | solution.py:488
  14.6 18.5 %collective-permute-start.2 = (bf16[4,10,8,512]{3,2,1,0:T(8,128)(2,1)S(1)}, bf16[4,10,8,512]{3,2,1,0:T(8,128)(2,1)}, u32[]{:S(2)}, u32[]{:S(2)}) collective-permute-start(bf16[4,10,8,512]{3,2,1,0:T(8,128)(2,1)S(1)} %get-tuple-element.42), channel_id=1, source_target_pairs={{0,4},{2,6},{4,0},{6,2},{8,12},{10,14},{12,8},{14,10},{16,20},{18,... | collective-permute-start | bytes 983048 | tf_op jit(solution)/shard_map/ppermute | solution.py:495
  16.0 26.1 %collective-permute-start.1 = (bf16[4,10,8,512]{3,2,1,0:T(8,128)(2,1)S(1)}, bf16[4,10,8,512]{3,2,1,0:T(8,128)(2,1)S(1)}, u32[]{:S(2)}, u32[]{:S(2)}) collective-permute-start(bf16[4,10,8,512]{3,2,1,0:T(8,128)(2,1)S(1)} %get-tuple-element.41), channel_id=1, source_target_pairs={{0,2},{1,7},{2,0},{3,5},{4,6},{5,3},{6,4},{7,1},{8,10},{9,15},{10,... | collective-permute-start | bytes 983048 | tf_op jit(solution)/shard_map/ppermute | solution.py:494
  17.2 16.0 %collective-permute-start.3 = (bf16[4,10,8,512]{3,2,1,0:T(8,128)(2,1)}, bf16[4,10,8,512]{3,2,1,0:T(8,128)(2,1)S(1)}, u32[]{:S(2)}, u32[]{:S(2)}) collective-permute-start(bf16[4,10,8,512]{3,2,1,0:T(8,128)(2,1)} %get-tuple-element.43), channel_id=1, source_target_pairs={{0,8},{1,11},{2,10},{3,9},{4,12},{5,15},{6,14},{7,13},{8,0},{9,3},... | collective-permute-start | bytes 983048 | tf_op jit(solution)/shard_map/ppermute | solution.py:494
  18.4 24.6 %collective-permute-start.4 = (bf16[4,10,8,512]{3,2,1,0:T(8,128)(2,1)S(1)}, bf16[4,10,8,512]{3,2,1,0:T(8,128)(2,1)S(1)}, u32[]{:S(2)}, u32[]{:S(2)}) collective-permute-start(bf16[4,10,8,512]{3,2,1,0:T(8,128)(2,1)S(1)} %get-tuple-element.51), channel_id=1, source_target_pairs={{0,14},{1,13},{2,12},{3,15},{4,10},{5,9},{6,8},{7,11},{8,6},{9,5},... | collective-permute-start | bytes 983048 | tf_op jit(solution)/shard_map/ppermute | solution.py:494
  33.0 10.8 %collective-permute-start.5 = (f16[72,8,128]{2,1,0:T(8,128)(2,1)S(1)}, f16[72,8,128]{2,1,0:T(8,128)(2,1)S(1)}, u32[]{:S(2)}, u32[]{:S(2)}) collective-permute-start(f16[72,8,128]{2,1,0:T(8,128)(2,1)S(1)} %convert_element_type.6), channel_id=1, source_target_pairs={{0,16},{4,20},{8,24},{12,28},{16,0},{20,4},{24,8},{28,12},{1,17},{... | collective-permute-start | bytes 442376 | tf_op jit(solution)/shard_map/ppermute | solution.py:503
  42.9 2.9 %copy-start.4 = (f32[8,64,128]{2,1,0:T(8,128)S(1)}, f32[8,64,128]{2,1,0:T(8,128)}, u32[]{:S(2)}) copy-start(f32[8,64,128]{2,1,0:T(8,128)} %land_flux.1) | copy-start | bytes 786436
  42.9 2.9 %copy-start.5 = (f32[64,128]{1,0:T(8,128)S(1)}, f32[64,128]{1,0:T(8,128)}, u32[]{:S(2)}) copy-start(f32[64,128]{1,0:T(8,128)} %kappa.3) | copy-start | bytes 98308
  42.9 2.9 %copy-start.6 = (f32[64,128]{1,0:T(8,128)S(1)}, f32[64,128]{1,0:T(8,128)}, u32[]{:S(2)}) copy-start(f32[64,128]{1,0:T(8,128)} %land_area.1) | copy-start | bytes 98308
  43.8 1.9 %collective-permute-start.6 = (f32[72,8,128]{2,1,0:T(8,128)S(1)}, f32[72,8,128]{2,1,0:T(8,128)S(1)}, u32[]{:S(2)}, u32[]{:S(2)}) collective-permute-start(f32[72,8,128]{2,1,0:T(8,128)S(1)} %shard_map.99), channel_id=1, source_target_pairs={{0,1},{1,0},{2,3},{3,2},{4,5},{5,4},{6,7},{7,6},{8,9},{9,8},{10,11... | collective-permute-start | bytes 884744 | tf_op jit(solution)/shard_map/ppermute | solution.py:519
  46.0 5.7 %collective-permute-start.8 = (f32[64,128]{1,0:T(8,128)S(1)}, f32[64,128]{1,0:T(8,128)S(1)}, u32[]{:S(2)}, u32[]{:S(2)}) collective-permute-start(f32[64,128]{1,0:T(8,128)S(1)} %get-tuple-element.59), channel_id=1, source_target_pairs={{4,8},{12,16},{20,24},{8,4},{16,12},{24,20},{5,9},{13,17},{21,25},... | collective-permute-start | bytes 98312 | tf_op jit(solution)/shard_map/ppermute | solution.py:379
  48.5 4.1 %collective-permute-start.7 = (f32[64,128]{1,0:T(8,128)S(1)}, f32[64,128]{1,0:T(8,128)S(1)}, u32[]{:S(2)}, u32[]{:S(2)}) collective-permute-start(f32[64,128]{1,0:T(8,128)S(1)} %get-tuple-element.59), channel_id=1, source_target_pairs={{0,4},{4,0},{8,12},{12,8},{16,20},{20,16},{24,28},{28,24},{1,5},{5... | collective-permute-start | bytes 98312 | tf_op jit(solution)/shard_map/ppermute | solution.py:378
  52.7 6.1 %collective-permute-start.10 = (f32[10,8,128]{2,1,0:T(8,128)S(1)}, f32[10,8,128]{2,1,0:T(8,128)S(1)}, u32[]{:S(2)}, u32[]{:S(2)}) collective-permute-start(f32[10,8,128]{2,1,0:T(8,128)S(1)} %pad_maximum_fusion), channel_id=1, source_target_pairs={{1,2},{2,1},{5,6},{6,5},{9,10},{10,9},{13,14},{14,13},{17,18},{18,... | collective-permute-start | bytes 122888 | tf_op jit(solution)/shard_map/ppermute | solution.py:379
  57.1 1.7 %collective-permute-start.9 = (f32[10,8,128]{2,1,0:T(8,128)S(1)}, f32[10,8,128]{2,1,0:T(8,128)S(1)}, u32[]{:S(2)}, u32[]{:S(2)}) collective-permute-start(f32[10,8,128]{2,1,0:T(8,128)S(1)} %pad_maximum_fusion), channel_id=1, source_target_pairs={{0,1},{1,0},{2,3},{3,2},{4,5},{5,4},{6,7},{7,6},{8,9},{9,8},{10,11... | collective-permute-start | bytes 122888 | tf_op jit(solution)/shard_map/ppermute | solution.py:378
